TPU v7x, 512 devices: a whole 4x4x16 slice. The times are simulated.
512 devices in a mesh: row: 64 (over y_lo, z, core), col: 8 (over x, y_hi).
Axes of the slice: x: 4, y: 4 (y_hi: 2, y_lo: 2; y = y_hi * 2 + y_lo), z: 16, core: 2. Of those that a mesh axis runs over, the one named last changes fastest.
Arguments:
- x_tiles: bfloat16 [192, 32, 128, 128], P('row', 'col'), may hold values from -0.59765625 to 0.59765625
- tile_cols: int32 [192, 32], P('row', 'col'), may hold values from 0 to 191, as said below
- tile_counts: int32 [192, 8], P('row', 'col'), may hold values from 1 to 4
Outputs:
- product: bfloat16 [192, 32, 128, 128], P('row', 'col')
Inputs may be any that keep to these rules, and one draw needn't show every extreme that they name: `tile_cols`: in block row i the slots p * 4 to (p + 1) * 4 - 1 hold 4 distinct block columns of panel p, each of the form p * 24 + ((i + d) mod 24) with -2 <= d <= 2.
All inputs are finite; a program needn't handle non-finite values.
Results may differ from a plain program's by a relative error of at most 0.001.
Values may be sent and summed in bfloat16 or wider, within the bound.
No kernel may reach another device: no remote copies, remote signals or barrier semaphores. Data moves between devices by JAX's collectives and lax.ppermute only.
A program may use at most 128 MiB of HBM per device.

v0:
```python
import jax
import jax.numpy as jnp
from jax import lax
from jax.sharding import PartitionSpec as P

PANELS = 8
PS = 4


def from_behind(block, axis, distance):
    devices = range(lax.axis_size(axis))
    route = [((i - distance) % len(devices), i) for i in devices]
    return lax.ppermute(block, axis, route)


def slot_live(tile_cols, tile_counts):
    repeated = jnp.repeat(tile_counts, PS, axis=1)
    position = lax.broadcasted_iota(jnp.int32, tile_cols.shape, 1) % PS
    return position < repeated


def body(x_tiles, tile_cols, tile_counts):
    rows_here = tile_cols.shape[0]
    count_row = lax.axis_size("row")
    here = lax.axis_index("row")
    stride = count_row // PANELS
    zero_tile = jnp.zeros((), x_tiles.dtype)
    own_live = slot_live(tile_cols, tile_counts)
    left_tiles, left_cols, left_counts = (
        lax.all_gather(x_tiles, "col", axis=1, tiled=True),
        lax.all_gather(tile_cols, "col", axis=1, tiled=True),
        lax.all_gather(tile_counts, "col", axis=1, tiled=True),
    )
    left_keyed = jnp.where(slot_live(left_cols, left_counts), left_cols, -1).astype(jnp.int32)
    block = (x_tiles, tile_cols, tile_counts)
    local_span = jnp.arange(rows_here, dtype=jnp.int32)
    offsets = sorted(
        set(((p * stride + e) % count_row for p in range(PANELS) for e in (-1, 0, 1))) - {0}
    )
    pieces = [block]
    id_list = [here * rows_here + local_span]
    for offset in offsets:
        moved = from_behind((block[0], block[1], block[2]), "row", count_row - offset)
        pieces.append(moved)
        id_list.append((here + offset) % count_row * rows_here + local_span)
    stack_tiles = jnp.concatenate([piece[0] for piece in pieces], axis=0)
    stack_cols = jnp.concatenate([piece[1] for piece in pieces], axis=0)
    stack_counts = jnp.concatenate([piece[2] for piece in pieces], axis=0)
    stack_ids = jnp.concatenate(id_list, axis=0).astype(jnp.int32)
    stack_keyed = jnp.where(slot_live(stack_cols, stack_counts), stack_cols, -1).astype(jnp.int32)
    position = jnp.arange(stack_ids.shape[0], dtype=jnp.int32)
    earlier = (stack_ids[:, None] == stack_ids[None, :]) & (position[:, None] > position[None, :])
    unique_row = jnp.logical_not(jnp.any(earlier, axis=1))
    group = 2 * PS
    turns = left_cols.shape[1] // group

    def advance(accum, index):
        first = index * group
        part_tiles = lax.dynamic_slice_in_dim(left_tiles, first, group, 1)
        part_keyed = lax.dynamic_slice_in_dim(left_keyed, first, group, 1)
        part_tiles = jnp.where((part_keyed >= 0)[:, :, None, None], part_tiles, zero_tile)
        matches = (part_keyed[:, :, None] == stack_ids[None, None, :]) & unique_row[None, None, :]
        chosen = jnp.einsum(
            "rgf,fuxy->rguxy",
            matches.astype(jnp.bfloat16),
            stack_tiles,
            preferred_element_type=jnp.float32,
        ).astype(jnp.bfloat16)
        chosen_cols = jnp.sum(
            jnp.where(matches[:, :, :, None], stack_keyed[None, None, :, :], 0), axis=2
        )
        hits = (chosen_cols[:, :, :, None] == tile_cols[:, None, None, :]).astype(jnp.bfloat16)
        placed = jnp.einsum(
            "rgus,rguxy->rgsxy", hits, chosen, preferred_element_type=jnp.float32
        ).astype(jnp.bfloat16)
        accum = accum + jnp.einsum(
            "rgxy,rgsyz->rsxz", part_tiles, placed, preferred_element_type=jnp.float32
        )
        return (accum, None)

    initial = jnp.zeros(
        (rows_here, tile_cols.shape[1], x_tiles.shape[-1], x_tiles.shape[-1]), jnp.float32
    )
    summed, _ = lax.scan(advance, initial, jnp.arange(turns, dtype=jnp.int32))
    return jnp.where(own_live[:, :, None, None], summed, 0.0).astype(jnp.bfloat16)


def solution(mesh):
    placed = (P("row", "col", None, None), P("row", "col"), P("row", "col"))
    return jax.shard_map(
        body, mesh=mesh, in_specs=placed, out_specs=P("row", "col", None, None), check_vma=False
    )
```

profile of v0, /device:TPU:6, one launch (start us, length us, event | category | flops | bytes accessed | tf_op | source)
XLA Modules:
  0.0 1210.6 jit_solution(1086816939266158125)
XLA Ops:
  7.3 11.9 collective-permute-start
  45.0 5.7 collective-permute-start.13
  50.8 68.4 %collective-permute-done.12 = s32[3,1]{0,1:T(1,128)S(1)} collective-permute-done((s32[3,1]{0,1:T(1,128)}, s32[3,1]{0,1:T(1,128)S(1)}, u32[]{:S(2)}, u32[]{:S(2)}) %collective-permute-start.12) | collective-permute-done | bytes 44 | tf_op jit(solution)/shard_map/ppermute | solution.py:13
  122.1 5.3 collective-permute-start.15
  129.6 7.3 collective-permute-start.16
  142.1 9.2 collective-permute-start.18
  156.7 6.4 collective-permute-start.2
  164.0 4.4 collective-permute-start.20
  170.4 4.0 collective-permute-done.20
  178.3 4.2 collective-permute-start.3
  182.5 6.2 collective-permute-start.4
  188.8 9.0 collective-permute-start.5
  197.8 5.8 collective-permute-start.6
  203.6 6.0 collective-permute-start.7
  211.5 5.5 collective-permute-start.8
  221.0 4.8 collective-permute-start.23
  229.0 5.5 collective-permute-start.25
  234.6 5.8 collective-permute-start.26
  240.4 6.0 collective-permute-start.27
  246.5 8.0 collective-permute-start.28
  254.5 7.2 collective-permute-start.29
  261.7 4.8 collective-permute-start.30
  268.1 5.1 collective-permute-start.31
  277.5 4.0 collective-permute-start.33
  287.5 6.3 collective-permute-start.36
  293.9 5.3 collective-permute-start.37
  299.2 6.4 collective-permute-start.38
  305.7 5.9 collective-permute-start.39
  311.6 7.7 collective-permute-start.40
  319.4 6.7 collective-permute-start.41
  333.9 4.9 collective-permute-start.43
  348.5 4.2 collective-permute-start.49
  352.7 6.3 collective-permute-start.50
  359.0 8.9 collective-permute-start.51
  368.0 4.6 collective-permute-start.52
  372.6 6.0 collective-permute-start.53
  380.9 28.5 %collective-permute-done.49 = bf16[3,4,128,128]{3,0,2,1:T(4,128)(2,1)S(1)} collective-permute-done((bf16[3,4,128,128]{3,0,2,1:T(4,128)(2,1)S(1)}, bf16[3,4,128,128]{3,0,2,1:T(4,128)(2,1)S(1)}, u32[]{:S(2)}, u32[]{:S(2)}) %collective-permute-start.49) | collective-permute-done | bytes 393248 | tf_op jit(solution)/shard_map/ppermute | solution.py:13
  409.4 5.3 collective-permute-start.54
  414.6 55.7 %collective-permute-done.50 = bf16[3,4,128,128]{3,0,2,1:T(4,128)(2,1)S(1)} collective-permute-done((bf16[3,4,128,128]{3,0,2,1:T(4,128)(2,1)S(1)}, bf16[3,4,128,128]{3,0,2,1:T(4,128)(2,1)S(1)}, u32[]{:S(2)}, u32[]{:S(2)}) %collective-permute-start.50) | collective-permute-done | bytes 393248 | tf_op jit(solution)/shard_map/ppermute | solution.py:13
  474.2 13.3 %collective-permute-done.52 = bf16[3,4,128,128]{3,0,2,1:T(4,128)(2,1)S(1)} collective-permute-done((bf16[3,4,128,128]{3,0,2,1:T(4,128)(2,1)S(1)}, bf16[3,4,128,128]{3,0,2,1:T(4,128)(2,1)S(1)}, u32[]{:S(2)}, u32[]{:S(2)}) %collective-permute-start.52) | collective-permute-done | bytes 393248 | tf_op jit(solution)/shard_map/ppermute | solution.py:13
  487.5 4.5 collective-permute-start.57
  492.0 38.1 %collective-permute-done.53 = bf16[3,4,128,128]{3,0,2,1:T(4,128)(2,1)S(1)} collective-permute-done((bf16[3,4,128,128]{3,0,2,1:T(4,128)(2,1)S(1)}, bf16[3,4,128,128]{3,0,2,1:T(4,128)(2,1)S(1)}, u32[]{:S(2)}, u32[]{:S(2)}) %collective-permute-start.53) | collective-permute-done | bytes 393248 | tf_op jit(solution)/shard_map/ppermute | solution.py:13
  530.1 57.3 %collective-permute-start.58 = (bf16[3,4,128,128]{3,0,2,1:T(4,128)(2,1)S(1)}, bf16[3,4,128,128]{3,0,2,1:T(4,128)(2,1)}, u32[]{:S(2)}, u32[]{:S(2)}) collective-permute-start(bf16[3,4,128,128]{3,0,2,1:T(4,128)(2,1)S(1)} %copy.170), channel_id=1, source_target_pairs={{264,0},{272,8},{280,16},{288,24},{296,32},{304,40},{312,48},{320,... | collective-permute-start | bytes 1179656 | tf_op jit(solution)/shard_map/ppermute | solution.py:13
  588.0 15.8 %all-gather = s32[8,1,3]{2,1,0:T(1,128)S(1)} all-gather(s32[1,1,3]{2,1,0:T(1,128)} %bitcast.55), channel_id=1, replica_groups=mesh['row'=64,'col'=8] {'col'}, dimensions={0}, use_global_device_ids=true | all-gather | bytes 108 | tf_op jit(solution)/shard_map/all_gather | solution.py:32
  605.6 31.0 %all-gather.1 = s32[8,4,3]{2,1,0:T(4,128)S(1)} all-gather(s32[1,4,3]{2,1,0:T(4,128)S(1)} %bitcast.53), channel_id=1, replica_groups=mesh['row'=64,'col'=8] {'col'}, dimensions={0}, use_global_device_ids=true | all-gather | bytes 432 | tf_op jit(solution)/shard_map/all_gather | solution.py:31
  640.8 13.2 %collective-permute-start.61 = (bf16[3,4,128,128]{3,0,2,1:T(4,128)(2,1)S(1)}, bf16[3,4,128,128]{3,0,2,1:T(4,128)(2,1)S(1)}, u32[]{:S(2)}, u32[]{:S(2)}) collective-permute-start(bf16[3,4,128,128]{3,0,2,1:T(4,128)(2,1)S(1)} %copy.170), channel_id=1, source_target_pairs={{328,0},{336,8},{344,16},{352,24},{360,32},{368,40},{376,48},{384,... | collective-permute-start | bytes 1179656 | tf_op jit(solution)/shard_map/ppermute | solution.py:13
  654.1 23.7 %collective-permute-start.62 = (bf16[3,4,128,128]{3,0,2,1:T(4,128)(2,1)S(1)}, bf16[3,4,128,128]{3,0,2,1:T(4,128)(2,1)S(1)}, u32[]{:S(2)}, u32[]{:S(2)}) collective-permute-start(bf16[3,4,128,128]{3,0,2,1:T(4,128)(2,1)S(1)} %copy.170), channel_id=1, source_target_pairs={{376,0},{384,8},{392,16},{400,24},{408,32},{416,40},{424,48},{432,... | collective-permute-start | bytes 1179656 | tf_op jit(solution)/shard_map/ppermute | solution.py:13
  677.7 21.4 %collective-permute-start.63 = (bf16[3,4,128,128]{3,0,2,1:T(4,128)(2,1)S(1)}, bf16[3,4,128,128]{3,0,2,1:T(4,128)(2,1)S(1)}, u32[]{:S(2)}, u32[]{:S(2)}) collective-permute-start(bf16[3,4,128,128]{3,0,2,1:T(4,128)(2,1)S(1)} %copy.170), channel_id=1, source_target_pairs={{384,0},{392,8},{400,16},{408,24},{416,32},{424,40},{432,48},{440,... | collective-permute-start | bytes 1179656 | tf_op jit(solution)/shard_map/ppermute | solution.py:13
  701.1 8.9 collective-permute-done.60
  710.0 126.5 %collective-permute-start.65 = (bf16[3,4,128,128]{3,0,2,1:T(4,128)(2,1)S(1)}, bf16[3,4,128,128]{3,0,2,1:T(4,128)(2,1)}, u32[]{:S(2)}, u32[]{:S(2)}) collective-permute-start(bf16[3,4,128,128]{3,0,2,1:T(4,128)(2,1)S(1)} %copy.170), channel_id=1, source_target_pairs={{440,0},{448,8},{456,16},{464,24},{472,32},{480,40},{488,48},{496,... | collective-permute-start | bytes 1179656 | tf_op jit(solution)/shard_map/ppermute | solution.py:13
  840.4 77.2 %collective-permute-start.68 = (bf16[3,4,128,128]{3,0,2,1:T(4,128)(2,1)S(1)}, bf16[3,4,128,128]{3,0,2,1:T(4,128)(2,1)}, u32[]{:S(2)}, u32[]{:S(2)}) collective-permute-start(bf16[3,4,128,128]{3,0,2,1:T(4,128)(2,1)S(1)} %copy.170), channel_id=1, source_target_pairs={{504,0},{0,8},{8,16},{16,24},{24,32},{32,40},{40,48},{48,56},{56,6... | collective-permute-start | bytes 1179656 | tf_op jit(solution)/shard_map/ppermute | solution.py:13
  919.4 11.2 collective-permute-done.66
  930.6 20.6 %collective-permute-done.67 = bf16[3,4,128,128]{3,0,2,1:T(4,128)(2,1)} collective-permute-done((bf16[3,4,128,128]{3,0,2,1:T(4,128)(2,1)S(1)}, bf16[3,4,128,128]{3,0,2,1:T(4,128)(2,1)}, u32[]{:S(2)}, u32[]{:S(2)}) %collective-permute-start.67) | collective-permute-done | bytes 393248 | tf_op jit(solution)/shard_map/ppermute | solution.py:13
  951.3 18.9 %collective-permute-done.68 = bf16[3,4,128,128]{3,0,2,1:T(4,128)(2,1)} collective-permute-done((bf16[3,4,128,128]{3,0,2,1:T(4,128)(2,1)S(1)}, bf16[3,4,128,128]{3,0,2,1:T(4,128)(2,1)}, u32[]{:S(2)}, u32[]{:S(2)}) %collective-permute-start.68) | collective-permute-done | bytes 393248 | tf_op jit(solution)/shard_map/ppermute | solution.py:13
  970.2 153.6 %concatenate.18 = bf16[72,4,128,128]{3,0,2,1:T(8,128)(2,1)} concatenate(bf16[3,4,128,128]{3,0,2,1:T(4,128)(2,1)S(1)} %copy.170, bf16[3,4,128,128]{3,0,2,1:T(4,128)(2,1)S(1)} %collective-permute-done.46, bf16[3,4,128,128]{3,0,2,1:T(4,128)(2,1)S(1)} %collective-permute-done.47, bf16[3,4,128,128]{3,0,2,1:T(4,128)(2,1)S(1)} %collective-permute-done.48, ...), dimensions={0} | concatenate | bytes 18874368 | tf_op jit(solution)/shard_map/concatenate | solution.py:46
  1123.8 78.9 %while.11 = (s32[]{:T(128)}, f32[3,4,128,128]{2,3,1,0:T(8,128)S(1)}, s32[4]{0:T(128)S(1)}, s32[3,32]{1,0:T(4,128)S(1)}, s32[72]{0:T(128)S(1)}, /*index=5*/pred[7...) while((s32[]{:T(128)}, ...), condition=%wide.region_3.4_spmd.clone, body=%wide.region_1.3_spmd.clone.sunk | while | flops 645681728 | bytes 24386944 | solution.py:84
  1125.2 6.8 fusion.48
  1132.4 7.7 fusion.49
  1144.9 6.8 fusion.48
  1152.1 7.7 fusion.49
  1164.6 6.8 fusion.48
  1171.8 7.7 fusion.49
  1184.3 6.8 fusion.48
  1191.6 7.7 fusion.49
  (214 shorter events, 126.7 us)
Async XLA Ops:
  6.5 1117.2 %all-gather.4.cloned.1.call-start = ((), (), s32[]{:S(2)}) async-start(), calls=%async_computation | async-start | bytes 3538944 | tf_op jit(solution)/shard_map/all_gather | solution.py:30
  7.3 28.8 %collective-permute-start = (s32[3,1]{0,1:T(1,128)}, s32[3,1]{0,1:T(1,128)S(1)}, u32[]{:S(2)}, u32[]{:S(2)}) collective-permute-start(s32[3,1]{0,1:T(1,128)} %param.7), channel_id=1, source_target_pairs={{8,0},{16,8},{24,16},{32,24},{40,32},{48,40},{56,48},{64,56},{72,6... | collective-permute-start | bytes 44 | tf_op jit(solution)/shard_map/ppermute | solution.py:13
  19.1 19.2 %collective-permute-start.1 = (s32[3,1]{0,1:T(1,128)}, s32[3,1]{0,1:T(1,128)S(1)}, u32[]{:S(2)}, u32[]{:S(2)}) collective-permute-start(s32[3,1]{0,1:T(1,128)} %param.7), channel_id=1, source_target_pairs={{56,0},{64,8},{72,16},{80,24},{88,32},{96,40},{104,48},{112,56},{1... | collective-permute-start | bytes 44 | tf_op jit(solution)/shard_map/ppermute | solution.py:13
  24.4 334.6 %collective-permute-start.46 = (bf16[3,4,128,128]{3,0,2,1:T(4,128)(2,1)S(1)}, bf16[3,4,128,128]{3,0,2,1:T(4,128)(2,1)S(1)}, u32[]{:S(2)}, u32[]{:S(2)}) collective-permute-start(bf16[3,4,128,128]{3,0,2,1:T(4,128)(2,1)S(1)} %copy.170), channel_id=1, source_target_pairs={{8,0},{16,8},{24,16},{32,24},{40,32},{48,40},{56,48},{64,56},{72,6... | collective-permute-start | bytes 1179656 | tf_op jit(solution)/shard_map/ppermute | solution.py:13
  28.1 339.8 %collective-permute-start.47 = (bf16[3,4,128,128]{3,0,2,1:T(4,128)(2,1)S(1)}, bf16[3,4,128,128]{3,0,2,1:T(4,128)(2,1)S(1)}, u32[]{:S(2)}, u32[]{:S(2)}) collective-permute-start(bf16[3,4,128,128]{3,0,2,1:T(4,128)(2,1)S(1)} %copy.170), channel_id=1, source_target_pairs={{56,0},{64,8},{72,16},{80,24},{88,32},{96,40},{104,48},{112,56},{1... | collective-permute-start | bytes 1179656 | tf_op jit(solution)/shard_map/ppermute | solution.py:13
  31.9 340.7 %collective-permute-start.48 = (bf16[3,4,128,128]{3,0,2,1:T(4,128)(2,1)S(1)}, bf16[3,4,128,128]{3,0,2,1:T(4,128)(2,1)S(1)}, u32[]{:S(2)}, u32[]{:S(2)}) collective-permute-start(bf16[3,4,128,128]{3,0,2,1:T(4,128)(2,1)S(1)} %copy.170), channel_id=1, source_target_pairs={{64,0},{72,8},{80,16},{88,24},{96,32},{104,40},{112,48},{120,56},{... | collective-permute-start | bytes 1179656 | tf_op jit(solution)/shard_map/ppermute | solution.py:13
  42.3 76.9 %collective-permute-start.12 = (s32[3,1]{0,1:T(1,128)}, s32[3,1]{0,1:T(1,128)S(1)}, u32[]{:S(2)}, u32[]{:S(2)}) collective-permute-start(s32[3,1]{0,1:T(1,128)} %param.7), channel_id=1, source_target_pairs={{264,0},{272,8},{280,16},{288,24},{296,32},{304,40},{312,48},{320,... | collective-permute-start | bytes 44 | tf_op jit(solution)/shard_map/ppermute | solution.py:13
  45.0 77.1 %collective-permute-start.13 = (s32[3,1]{0,1:T(1,128)}, s32[3,1]{0,1:T(1,128)S(1)}, u32[]{:S(2)}, u32[]{:S(2)}) collective-permute-start(s32[3,1]{0,1:T(1,128)} %param.7), channel_id=1, source_target_pairs={{312,0},{320,8},{328,16},{336,24},{344,32},{352,40},{360,48},{368,... | collective-permute-start | bytes 44 | tf_op jit(solution)/shard_map/ppermute | solution.py:13
  119.2 10.4 collective-permute-start.14
  122.1 14.8 %collective-permute-start.15 = (s32[3,1]{0,1:T(1,128)}, s32[3,1]{0,1:T(1,128)S(1)}, u32[]{:S(2)}, u32[]{:S(2)}) collective-permute-start(s32[3,1]{0,1:T(1,128)} %param.7), channel_id=1, source_target_pairs={{328,0},{336,8},{344,16},{352,24},{360,32},{368,40},{376,48},{384,... | collective-permute-start | bytes 44 | tf_op jit(solution)/shard_map/ppermute | solution.py:13
  129.6 12.5 %collective-permute-start.16 = (s32[3,1]{0,1:T(1,128)}, s32[3,1]{0,1:T(1,128)S(1)}, u32[]{:S(2)}, u32[]{:S(2)}) collective-permute-start(s32[3,1]{0,1:T(1,128)} %param.7), channel_id=1, source_target_pairs={{376,0},{384,8},{392,16},{400,24},{408,32},{416,40},{424,48},{432,... | collective-permute-start | bytes 44 | tf_op jit(solution)/shard_map/ppermute | solution.py:13
  137.0 15.2 %collective-permute-start.17 = (s32[3,1]{0,1:T(1,128)}, s32[3,1]{0,1:T(1,128)S(1)}, u32[]{:S(2)}, u32[]{:S(2)}) collective-permute-start(s32[3,1]{0,1:T(1,128)} %param.7), channel_id=1, source_target_pairs={{384,0},{392,8},{400,16},{408,24},{416,32},{424,40},{432,48},{440,... | collective-permute-start | bytes 44 | tf_op jit(solution)/shard_map/ppermute | solution.py:13
  142.1 14.6 %collective-permute-start.18 = (s32[3,1]{0,1:T(1,128)}, s32[3,1]{0,1:T(1,128)S(1)}, u32[]{:S(2)}, u32[]{:S(2)}) collective-permute-start(s32[3,1]{0,1:T(1,128)} %param.7), channel_id=1, source_target_pairs={{392,0},{400,8},{408,16},{416,24},{424,32},{432,40},{440,48},{448,... | collective-permute-start | bytes 44 | tf_op jit(solution)/shard_map/ppermute | solution.py:13
  152.1 11.9 collective-permute-start.19
  156.7 11.8 collective-permute-start.2
  164.0 10.4 collective-permute-start.20
  168.5 9.8 collective-permute-start.21
  178.3 10.4 collective-permute-start.3
  182.5 15.3 %collective-permute-start.4 = (s32[3,1]{0,1:T(1,128)}, s32[3,1]{0,1:T(1,128)S(1)}, u32[]{:S(2)}, u32[]{:S(2)}) collective-permute-start(s32[3,1]{0,1:T(1,128)} %param.7), channel_id=1, source_target_pairs={{120,0},{128,8},{136,16},{144,24},{152,32},{160,40},{168,48},{176,... | collective-permute-start | bytes 44 | tf_op jit(solution)/shard_map/ppermute | solution.py:13
  188.8 14.8 %collective-permute-start.5 = (s32[3,1]{0,1:T(1,128)}, s32[3,1]{0,1:T(1,128)S(1)}, u32[]{:S(2)}, u32[]{:S(2)}) collective-permute-start(s32[3,1]{0,1:T(1,128)} %param.7), channel_id=1, source_target_pairs={{128,0},{136,8},{144,16},{152,24},{160,32},{168,40},{176,48},{184,... | collective-permute-start | bytes 44 | tf_op jit(solution)/shard_map/ppermute | solution.py:13
  197.8 13.7 %collective-permute-start.6 = (s32[3,1]{0,1:T(1,128)}, s32[3,1]{0,1:T(1,128)S(1)}, u32[]{:S(2)}, u32[]{:S(2)}) collective-permute-start(s32[3,1]{0,1:T(1,128)} %param.7), channel_id=1, source_target_pairs={{136,0},{144,8},{152,16},{160,24},{168,32},{176,40},{184,48},{192,... | collective-permute-start | bytes 44 | tf_op jit(solution)/shard_map/ppermute | solution.py:13
  203.6 13.4 %collective-permute-start.7 = (s32[3,1]{0,1:T(1,128)}, s32[3,1]{0,1:T(1,128)S(1)}, u32[]{:S(2)}, u32[]{:S(2)}) collective-permute-start(s32[3,1]{0,1:T(1,128)} %param.7), channel_id=1, source_target_pairs={{184,0},{192,8},{200,16},{208,24},{216,32},{224,40},{232,48},{240,... | collective-permute-start | bytes 44 | tf_op jit(solution)/shard_map/ppermute | solution.py:13
  211.5 9.5 collective-permute-start.8
  217.0 8.9 collective-permute-start.9
  225.9 8.6 collective-permute-start.24
  229.0 11.4 collective-permute-start.25
  234.6 11.9 collective-permute-start.26
  240.4 14.1 %collective-permute-start.27 = (s32[3,4]{0,1:T(4,128)S(1)}, s32[3,4]{0,1:T(4,128)S(1)}, u32[]{:S(2)}, u32[]{:S(2)}) collective-permute-start(s32[3,4]{0,1:T(4,128)S(1)} %copy.146), channel_id=1, source_target_pairs={{120,0},{128,8},{136,16},{144,24},{152,32},{160,40},{168,48},{176,... | collective-permute-start | bytes 152 | tf_op jit(solution)/shard_map/ppermute | solution.py:13
  246.5 15.2 %collective-permute-start.28 = (s32[3,4]{0,1:T(4,128)S(1)}, s32[3,4]{0,1:T(4,128)S(1)}, u32[]{:S(2)}, u32[]{:S(2)}) collective-permute-start(s32[3,4]{0,1:T(4,128)S(1)} %copy.146), channel_id=1, source_target_pairs={{128,0},{136,8},{144,16},{152,24},{160,32},{168,40},{176,48},{184,... | collective-permute-start | bytes 152 | tf_op jit(solution)/shard_map/ppermute | solution.py:13
  254.5 13.6 %collective-permute-start.29 = (s32[3,4]{0,1:T(4,128)S(1)}, s32[3,4]{0,1:T(4,128)S(1)}, u32[]{:S(2)}, u32[]{:S(2)}) collective-permute-start(s32[3,4]{0,1:T(4,128)S(1)} %copy.146), channel_id=1, source_target_pairs={{136,0},{144,8},{152,16},{160,24},{168,32},{176,40},{184,48},{192,... | collective-permute-start | bytes 152 | tf_op jit(solution)/shard_map/ppermute | solution.py:13
  261.7 11.5 collective-permute-start.30
  268.1 9.4 collective-permute-start.31
  273.3 8.8 collective-permute-start.32
  284.8 9.1 collective-permute-start.35
  287.5 11.7 collective-permute-start.36
  293.9 11.8 collective-permute-start.37
  299.2 12.4 %collective-permute-start.38 = (s32[3,4]{0,1:T(4,128)S(1)}, s32[3,4]{0,1:T(4,128)S(1)}, u32[]{:S(2)}, u32[]{:S(2)}) collective-permute-start(s32[3,4]{0,1:T(4,128)S(1)} %copy.146), channel_id=1, source_target_pairs={{328,0},{336,8},{344,16},{352,24},{360,32},{368,40},{376,48},{384,... | collective-permute-start | bytes 152 | tf_op jit(solution)/shard_map/ppermute | solution.py:13
  305.7 13.7 %collective-permute-start.39 = (s32[3,4]{0,1:T(4,128)S(1)}, s32[3,4]{0,1:T(4,128)S(1)}, u32[]{:S(2)}, u32[]{:S(2)}) collective-permute-start(s32[3,4]{0,1:T(4,128)S(1)} %copy.146), channel_id=1, source_target_pairs={{376,0},{384,8},{392,16},{400,24},{408,32},{416,40},{424,48},{432,... | collective-permute-start | bytes 152 | tf_op jit(solution)/shard_map/ppermute | solution.py:13
  311.6 15.1 %collective-permute-start.40 = (s32[3,4]{0,1:T(4,128)S(1)}, s32[3,4]{0,1:T(4,128)S(1)}, u32[]{:S(2)}, u32[]{:S(2)}) collective-permute-start(s32[3,4]{0,1:T(4,128)S(1)} %copy.146), channel_id=1, source_target_pairs={{384,0},{392,8},{400,16},{408,24},{416,32},{424,40},{432,48},{440,... | collective-permute-start | bytes 152 | tf_op jit(solution)/shard_map/ppermute | solution.py:13
  319.4 14.5 %collective-permute-start.41 = (s32[3,4]{0,1:T(4,128)S(1)}, s32[3,4]{0,1:T(4,128)S(1)}, u32[]{:S(2)}, u32[]{:S(2)}) collective-permute-start(s32[3,4]{0,1:T(4,128)S(1)} %copy.146), channel_id=1, source_target_pairs={{392,0},{400,8},{408,16},{416,24},{424,32},{432,40},{440,48},{448,... | collective-permute-start | bytes 152 | tf_op jit(solution)/shard_map/ppermute | solution.py:13
  326.7 12.1 collective-permute-start.42
  333.9 10.3 collective-permute-start.43
  338.8 9.7 collective-permute-start.44
  344.1 8.5 collective-permute-start.45
  348.5 60.9 %collective-permute-start.49 = (bf16[3,4,128,128]{3,0,2,1:T(4,128)(2,1)S(1)}, bf16[3,4,128,128]{3,0,2,1:T(4,128)(2,1)S(1)}, u32[]{:S(2)}, u32[]{:S(2)}) collective-permute-start(bf16[3,4,128,128]{3,0,2,1:T(4,128)(2,1)S(1)} %copy.170), channel_id=1, source_target_pairs={{72,0},{80,8},{88,16},{96,24},{104,32},{112,40},{120,48},{128,56},... | collective-permute-start | bytes 1179656 | tf_op jit(solution)/shard_map/ppermute | solution.py:13
  352.7 117.6 %collective-permute-start.50 = (bf16[3,4,128,128]{3,0,2,1:T(4,128)(2,1)S(1)}, bf16[3,4,128,128]{3,0,2,1:T(4,128)(2,1)S(1)}, u32[]{:S(2)}, u32[]{:S(2)}) collective-permute-start(bf16[3,4,128,128]{3,0,2,1:T(4,128)(2,1)S(1)} %copy.170), channel_id=1, source_target_pairs={{120,0},{128,8},{136,16},{144,24},{152,32},{160,40},{168,48},{176,... | collective-permute-start | bytes 1179656 | tf_op jit(solution)/shard_map/ppermute | solution.py:13
  359.0 113.2 %collective-permute-start.51 = (bf16[3,4,128,128]{3,0,2,1:T(4,128)(2,1)S(1)}, bf16[3,4,128,128]{3,0,2,1:T(4,128)(2,1)S(1)}, u32[]{:S(2)}, u32[]{:S(2)}) collective-permute-start(bf16[3,4,128,128]{3,0,2,1:T(4,128)(2,1)S(1)} %copy.170), channel_id=1, source_target_pairs={{128,0},{136,8},{144,16},{152,24},{160,32},{168,40},{176,48},{184,... | collective-permute-start | bytes 1179656 | tf_op jit(solution)/shard_map/ppermute | solution.py:13
  368.0 119.5 %collective-permute-start.52 = (bf16[3,4,128,128]{3,0,2,1:T(4,128)(2,1)S(1)}, bf16[3,4,128,128]{3,0,2,1:T(4,128)(2,1)S(1)}, u32[]{:S(2)}, u32[]{:S(2)}) collective-permute-start(bf16[3,4,128,128]{3,0,2,1:T(4,128)(2,1)S(1)} %copy.170), channel_id=1, source_target_pairs={{136,0},{144,8},{152,16},{160,24},{168,32},{176,40},{184,48},{192,... | collective-permute-start | bytes 1179656 | tf_op jit(solution)/shard_map/ppermute | solution.py:13
  372.6 157.5 %collective-permute-start.53 = (bf16[3,4,128,128]{3,0,2,1:T(4,128)(2,1)S(1)}, bf16[3,4,128,128]{3,0,2,1:T(4,128)(2,1)S(1)}, u32[]{:S(2)}, u32[]{:S(2)}) collective-permute-start(bf16[3,4,128,128]{3,0,2,1:T(4,128)(2,1)S(1)} %copy.170), channel_id=1, source_target_pairs={{184,0},{192,8},{200,16},{208,24},{216,32},{224,40},{232,48},{240,... | collective-permute-start | bytes 1179656 | tf_op jit(solution)/shard_map/ppermute | solution.py:13
  409.4 227.5 %collective-permute-start.54 = (bf16[3,4,128,128]{3,0,2,1:T(4,128)(2,1)S(1)}, bf16[3,4,128,128]{3,0,2,1:T(4,128)(2,1)}, u32[]{:S(2)}, u32[]{:S(2)}) collective-permute-start(bf16[3,4,128,128]{3,0,2,1:T(4,128)(2,1)S(1)} %copy.170), channel_id=1, source_target_pairs={{192,0},{200,8},{208,16},{216,24},{224,32},{232,40},{240,48},{248,... | collective-permute-start | bytes 1179656 | tf_op jit(solution)/shard_map/ppermute | solution.py:13
  470.3 168.5 %collective-permute-start.55 = (bf16[3,4,128,128]{3,0,2,1:T(4,128)(2,1)S(1)}, bf16[3,4,128,128]{3,0,2,1:T(4,128)(2,1)}, u32[]{:S(2)}, u32[]{:S(2)}) collective-permute-start(bf16[3,4,128,128]{3,0,2,1:T(4,128)(2,1)S(1)} %copy.170), channel_id=1, source_target_pairs={{200,0},{208,8},{216,16},{224,24},{232,32},{240,40},{248,48},{256,... | collective-permute-start | bytes 1179656 | tf_op jit(solution)/shard_map/ppermute | solution.py:13
  472.3 168.5 %collective-permute-start.56 = (bf16[3,4,128,128]{3,0,2,1:T(4,128)(2,1)S(1)}, bf16[3,4,128,128]{3,0,2,1:T(4,128)(2,1)}, u32[]{:S(2)}, u32[]{:S(2)}) collective-permute-start(bf16[3,4,128,128]{3,0,2,1:T(4,128)(2,1)S(1)} %copy.170), channel_id=1, source_target_pairs={{248,0},{256,8},{264,16},{272,24},{280,32},{288,40},{296,48},{304,... | collective-permute-start | bytes 1179656 | tf_op jit(solution)/shard_map/ppermute | solution.py:13
  487.5 166.6 %collective-permute-start.57 = (bf16[3,4,128,128]{3,0,2,1:T(4,128)(2,1)S(1)}, bf16[3,4,128,128]{3,0,2,1:T(4,128)(2,1)}, u32[]{:S(2)}, u32[]{:S(2)}) collective-permute-start(bf16[3,4,128,128]{3,0,2,1:T(4,128)(2,1)S(1)} %copy.170), channel_id=1, source_target_pairs={{256,0},{264,8},{272,16},{280,24},{288,32},{296,40},{304,48},{312,... | collective-permute-start | bytes 1179656 | tf_op jit(solution)/shard_map/ppermute | solution.py:13
  530.1 147.6 %collective-permute-start.58 = (bf16[3,4,128,128]{3,0,2,1:T(4,128)(2,1)S(1)}, bf16[3,4,128,128]{3,0,2,1:T(4,128)(2,1)}, u32[]{:S(2)}, u32[]{:S(2)}) collective-permute-start(bf16[3,4,128,128]{3,0,2,1:T(4,128)(2,1)S(1)} %copy.170), channel_id=1, source_target_pairs={{264,0},{272,8},{280,16},{288,24},{296,32},{304,40},{312,48},{320,... | collective-permute-start | bytes 1179656 | tf_op jit(solution)/shard_map/ppermute | solution.py:13
  636.9 62.3 %collective-permute-start.59 = (bf16[3,4,128,128]{3,0,2,1:T(4,128)(2,1)S(1)}, bf16[3,4,128,128]{3,0,2,1:T(4,128)(2,1)S(1)}, u32[]{:S(2)}, u32[]{:S(2)}) collective-permute-start(bf16[3,4,128,128]{3,0,2,1:T(4,128)(2,1)S(1)} %copy.170), channel_id=1, source_target_pairs={{312,0},{320,8},{328,16},{336,24},{344,32},{352,40},{360,48},{368,... | collective-permute-start | bytes 1179656 | tf_op jit(solution)/shard_map/ppermute | solution.py:13
  638.9 71.1 %collective-permute-start.60 = (bf16[3,4,128,128]{3,0,2,1:T(4,128)(2,1)S(1)}, bf16[3,4,128,128]{3,0,2,1:T(4,128)(2,1)S(1)}, u32[]{:S(2)}, u32[]{:S(2)}) collective-permute-start(bf16[3,4,128,128]{3,0,2,1:T(4,128)(2,1)S(1)} %copy.170), channel_id=1, source_target_pairs={{320,0},{328,8},{336,16},{344,24},{352,32},{360,40},{368,48},{376,... | collective-permute-start | bytes 1179656 | tf_op jit(solution)/shard_map/ppermute | solution.py:13
  640.8 195.7 %collective-permute-start.61 = (bf16[3,4,128,128]{3,0,2,1:T(4,128)(2,1)S(1)}, bf16[3,4,128,128]{3,0,2,1:T(4,128)(2,1)S(1)}, u32[]{:S(2)}, u32[]{:S(2)}) collective-permute-start(bf16[3,4,128,128]{3,0,2,1:T(4,128)(2,1)S(1)} %copy.170), channel_id=1, source_target_pairs={{328,0},{336,8},{344,16},{352,24},{360,32},{368,40},{376,48},{384,... | collective-permute-start | bytes 1179656 | tf_op jit(solution)/shard_map/ppermute | solution.py:13
  654.1 184.3 %collective-permute-start.62 = (bf16[3,4,128,128]{3,0,2,1:T(4,128)(2,1)S(1)}, bf16[3,4,128,128]{3,0,2,1:T(4,128)(2,1)S(1)}, u32[]{:S(2)}, u32[]{:S(2)}) collective-permute-start(bf16[3,4,128,128]{3,0,2,1:T(4,128)(2,1)S(1)} %copy.170), channel_id=1, source_target_pairs={{376,0},{384,8},{392,16},{400,24},{408,32},{416,40},{424,48},{432,... | collective-permute-start | bytes 1179656 | tf_op jit(solution)/shard_map/ppermute | solution.py:13
  677.7 162.6 %collective-permute-start.63 = (bf16[3,4,128,128]{3,0,2,1:T(4,128)(2,1)S(1)}, bf16[3,4,128,128]{3,0,2,1:T(4,128)(2,1)S(1)}, u32[]{:S(2)}, u32[]{:S(2)}) collective-permute-start(bf16[3,4,128,128]{3,0,2,1:T(4,128)(2,1)S(1)} %copy.170), channel_id=1, source_target_pairs={{384,0},{392,8},{400,16},{408,24},{416,32},{424,40},{432,48},{440,... | collective-permute-start | bytes 1179656 | tf_op jit(solution)/shard_map/ppermute | solution.py:13
  699.2 220.2 %collective-permute-start.64 = (bf16[3,4,128,128]{3,0,2,1:T(4,128)(2,1)S(1)}, bf16[3,4,128,128]{3,0,2,1:T(4,128)(2,1)}, u32[]{:S(2)}, u32[]{:S(2)}) collective-permute-start(bf16[3,4,128,128]{3,0,2,1:T(4,128)(2,1)S(1)} %copy.170), channel_id=1, source_target_pairs={{392,0},{400,8},{408,16},{416,24},{424,32},{432,40},{440,48},{448,... | collective-permute-start | bytes 1179656 | tf_op jit(solution)/shard_map/ppermute | solution.py:13
  710.0 209.4 %collective-permute-start.65 = (bf16[3,4,128,128]{3,0,2,1:T(4,128)(2,1)S(1)}, bf16[3,4,128,128]{3,0,2,1:T(4,128)(2,1)}, u32[]{:S(2)}, u32[]{:S(2)}) collective-permute-start(bf16[3,4,128,128]{3,0,2,1:T(4,128)(2,1)S(1)} %copy.170), channel_id=1, source_target_pairs={{440,0},{448,8},{456,16},{464,24},{472,32},{480,40},{488,48},{496,... | collective-permute-start | bytes 1179656 | tf_op jit(solution)/shard_map/ppermute | solution.py:13
  836.5 94.2 %collective-permute-start.66 = (bf16[3,4,128,128]{3,0,2,1:T(4,128)(2,1)S(1)}, bf16[3,4,128,128]{3,0,2,1:T(4,128)(2,1)}, u32[]{:S(2)}, u32[]{:S(2)}) collective-permute-start(bf16[3,4,128,128]{3,0,2,1:T(4,128)(2,1)S(1)} %copy.170), channel_id=1, source_target_pairs={{448,0},{456,8},{464,16},{472,24},{480,32},{488,40},{496,48},{504,... | collective-permute-start | bytes 1179656 | tf_op jit(solution)/shard_map/ppermute | solution.py:13
  838.4 112.8 %collective-permute-start.67 = (bf16[3,4,128,128]{3,0,2,1:T(4,128)(2,1)S(1)}, bf16[3,4,128,128]{3,0,2,1:T(4,128)(2,1)}, u32[]{:S(2)}, u32[]{:S(2)}) collective-permute-start(bf16[3,4,128,128]{3,0,2,1:T(4,128)(2,1)S(1)} %copy.170), channel_id=1, source_target_pairs={{456,0},{464,8},{472,16},{480,24},{488,32},{496,40},{504,48},{0,56... | collective-permute-start | bytes 1179656 | tf_op jit(solution)/shard_map/ppermute | solution.py:13
  840.4 129.8 %collective-permute-start.68 = (bf16[3,4,128,128]{3,0,2,1:T(4,128)(2,1)S(1)}, bf16[3,4,128,128]{3,0,2,1:T(4,128)(2,1)}, u32[]{:S(2)}, u32[]{:S(2)}) collective-permute-start(bf16[3,4,128,128]{3,0,2,1:T(4,128)(2,1)S(1)} %copy.170), channel_id=1, source_target_pairs={{504,0},{0,8},{8,16},{16,24},{24,32},{32,40},{40,48},{48,56},{56,6... | collective-permute-start | bytes 1179656 | tf_op jit(solution)/shard_map/ppermute | solution.py:13
  (39 other events, 4731.3 us)
Sparse Core Ops, SparseCore 0:
  10.6 82.2 all-gather.3
where the time goes:
time: 1230 us; the launch traced here: 1210 us
  starting transfers between devices  612 us (50%)
  waiting for transfers between devices  293 us (24%)
  local copies, waits for them, and re-layouts  162 us (13%)
  matrix products  71.5 us (6%)
  blocking collectives  46.8 us (4%)
  between operations  15 us (1%)
    ppermute x69, starting transfers between devices, from_behind(): return lax.ppermute(block, axis, route)  612 us
    ppermute x69, waiting for transfers between devices, from_behind(): return lax.ppermute(block, axis, route)  293 us
    concatenate x1, local copies, waits for them, and re-layouts, body(): stack_tiles = jnp.concatenate([piece[0] for piece in pieces], axis=0)  154 us
    all_gather x1, blocking collectives, body(): lax.all_gather(tile_cols, 'col', axis=1, tiled=True)  31 us
    dot_general x4, matrix products, advance(): jnp.einsum('rgus,rguxy->rgsxy', hits, chosen, preferred_element_type=jnp....  30.8 us
    dot_general x4, matrix products, advance(): jnp.einsum('rgf,fuxy->rguxy', matches.astype(jnp.bfloat16), stack_tiles,...  27.2 us
  transfers between devices with their start and end apart: 70, of which 28 were waited for; matrix products, arithmetic and copies ran while one was open for 14% of the time, Pallas kernels for 0%

commit v1 on v0

v1 whole, which is shorter than its diff:
```python
import functools

import jax
import jax.numpy as jnp
from jax import lax
from jax.experimental import pallas as pl
from jax.experimental.pallas import tpu as pltpu
from jax.sharding import PartitionSpec as P

BF16, F32, I32 = jnp.bfloat16, jnp.float32, jnp.int32
T = 128
LIMIT = 48 << 20
BLOCK = 12 * T + 16
HEAD, TAIL = T, T + 16
PIECE = 3 * (HEAD + TAIL)
ANY = pl.BlockSpec(memory_space=pl.ANY)
VMEM = pl.BlockSpec(memory_space=pltpu.VMEM)
SMEM = pl.BlockSpec(memory_space=pltpu.SMEM)


def routes(move):
    pairs = []
    for row in range(64):
        for col in range(8):
            a, z, k, x, h = move(row // 32, row // 2 % 16, row % 2, col // 2, col % 2)
            pairs.append((row * 8 + col, (a * 32 + z % 16 * 2 + k) * 8 + x % 4 * 2 + h))
    return pairs


def along_z(n):
    return routes(lambda a, z, k, x, h: (a, z + n, k, x, h))


def along_x(n):
    return routes(lambda a, z, k, x, h: (a, z, k, x + n, h))


def along_y(n):
    def move(a, z, k, x, h):
        y = (2 * h + a + n) % 4
        return y % 2, z, k, x, y // 2

    return routes(move)


CORE = routes(lambda a, z, k, x, h: (a, z, 1 - k, x, h))
HALO = routes(lambda a, z, k, x, h: (a, z + 2 * k - 1, 1 - k, x, h))
PLANE = routes(lambda a, z, k, x, h: (1 - a, z, k, x, h))


def send(block, pairs):
    return lax.ppermute(block, ("row", "col"), pairs)


def params():
    return pltpu.CompilerParams(vmem_limit_bytes=LIMIT)


def cost(flops, moved):
    return pl.CostEstimate(flops=flops, bytes_accessed=moved, transcendentals=0)


def lanes():
    return lax.broadcasted_iota(I32, (1, T), 1)


def turned(v):
    return pltpu.roll(v, T // 2, 1)


def pack_kernel(place, cols, counts, x, a_out, b0_out, b1_out, k_out):
    row = lax.broadcasted_iota(I32, (16, T), 0)
    left = lax.broadcasted_iota(I32, (16, T), 1) < T // 2
    plain = jnp.full((16, T), 9, I32)
    paired = jnp.full((16, T), 9, I32)
    for r in range(3):
        keys = []
        for t in range(4):
            away = (cols[r, t] - (place[0] * 3 + r) + 240) % 24
            away = jnp.where(away > 12, away - 24, away)
            keys.append(jnp.where(t < counts[r, 0], away, 9))
            plain = jnp.where(row == r * 4 + t, keys[t], plain)
        for m in range(2):
            first, second = keys[2 * m], keys[2 * m + 1]
            paired = jnp.where(row == r * 4 + 2 * m, jnp.where(left, first, second), paired)
            paired = jnp.where(row == r * 4 + 2 * m + 1, jnp.where(left, second, first), paired)
    a_out[12 * T :, :] = plain.astype(F32).astype(BF16)
    paired = paired.astype(F32)
    k_out[...] = paired.astype(BF16)
    here = lanes() < T // 2
    for r in range(3):
        tail = 3 * HEAD + r * TAIL
        keyed = jnp.concatenate([paired[4 * r : 4 * r + 4], jnp.full((12, T), 9.0, F32)], axis=0)
        keyed = keyed.astype(BF16)
        b0_out[tail + T : tail + TAIL, :] = keyed
        b1_out[tail + T : tail + TAIL, :] = keyed
        for m in range(2):
            at = r * HEAD if m == 0 else tail
            even = x[r, 2 * m]
            odd = x[r, 2 * m + 1]
            a_out[(4 * r + 2 * m) * T : (4 * r + 2 * m + 1) * T, :] = even
            a_out[(4 * r + 2 * m + 1) * T : (4 * r + 2 * m + 2) * T, :] = odd
            even, odd = even.astype(F32), odd.astype(F32)
            b0_out[at : at + T, :] = jnp.where(here, even, turned(odd)).astype(BF16)
            b1_out[at : at + T, :] = jnp.where(here, turned(even), odd).astype(BF16)


def pack(place, cols, counts, x):
    shapes = ((BLOCK, T), (PIECE, T), (PIECE, T), (16, T))
    return pl.pallas_call(
        pack_kernel,
        out_shape=[jax.ShapeDtypeStruct(s, BF16) for s in shapes],
        in_specs=[SMEM, SMEM, SMEM, VMEM],
        out_specs=[VMEM] * 4,
        compiler_params=params(),
        cost_estimate=cost(1 << 20, 6 << 20),
        name="pack",
    )(place, cols, counts, x)


def run_all(copies):
    for copy in copies:
        copy.start()
    for copy in copies:
        copy.wait()


def sort_kernel(place, own, g1, g2, g3, keys, same, other, sem):
    a, x = place[1], place[4]
    last = pltpu.make_async_copy(keys, other.at[pl.ds(2 * BLOCK, 16)], sem.at[4])
    last.start()
    copies = []
    for k, source in enumerate((own, g1, g2, g3)):
        panel = (x - k + 4) % 4
        at = pl.multiple_of(panel % 2 * BLOCK, 16)
        to_same = pltpu.make_async_copy(source, same.at[pl.ds(at, BLOCK)], sem.at[k])
        to_other = pltpu.make_async_copy(source, other.at[pl.ds(at, BLOCK)], sem.at[k])
        pl.when(panel // 2 == a)(to_same.start)
        pl.when(panel // 2 != a)(to_other.start)
        copies.append(to_same)
    for copy in copies:
        copy.wait()
    last.wait()


def sort_panels(place, own, g1, g2, g3, keys):
    return pl.pallas_call(
        sort_kernel,
        out_shape=[
            jax.ShapeDtypeStruct((2 * BLOCK, T), BF16),
            jax.ShapeDtypeStruct((2 * BLOCK + 16, T), BF16),
        ],
        in_specs=[SMEM] + [ANY] * 5,
        out_specs=[ANY] * 2,
        scratch_shapes=[pltpu.SemaphoreType.DMA((5,))],
        compiler_params=params(),
        cost_estimate=cost(0, 4 << 20),
        name="sort_panels",
    )(place, own, g1, g2, g3, keys)


def left_kernel(place, same, r1, rm, r2, out, partner, held, sem):
    a, h = place[1], place[5]
    copies = []
    near = jnp.where(a == 1, h, 1 - h)
    for q, (source, half) in enumerate(((same, h), (r2, 1 - h), (r1, near), (rm, 1 - near))):
        for e in range(2):
            copies.append(
                pltpu.make_async_copy(
                    source.at[pl.ds(e * BLOCK, BLOCK)],
                    held.at[q // 2 * 4 + 2 * e + half],
                    sem.at[2 * q + e],
                )
            )
    for copy in copies:
        copy.start()
    from_r1 = pltpu.make_async_copy(r1.at[pl.ds(2 * BLOCK, 16)], partner, sem.at[8])
    from_rm = pltpu.make_async_copy(rm.at[pl.ds(2 * BLOCK, 16)], partner, sem.at[8])
    pl.when(a == 1)(from_r1.start)
    pl.when(a == 0)(from_rm.start)
    for copy in copies:
        copy.wait()
    from_r1.wait()

    def one(q, carry):
        low = pl.multiple_of(q // 4 * T, T)
        keys = held[q, 12 * T :, :].astype(F32)
        for i in range(3):
            tiles = [held[q, (4 * i + t) * T : (4 * i + t + 1) * T, :].astype(F32) for t in range(4)]
            for d in range(5):
                parts = [
                    tiles[t] * jnp.where(keys[4 * i + t : 4 * i + t + 1] == float(d - 2), 1.0, 0.0)
                    for t in range(4)
                ]
                block = (parts[0] + parts[1]) + (parts[2] + parts[3])
                out[i, q % 4, pl.ds(low, T), d * T : (d + 1) * T] = block.astype(BF16)
        return carry

    lax.fori_loop(0, 8, one, 0)


def left_panels(place, same, r1, rm, r2):
    return pl.pallas_call(
        left_kernel,
        out_shape=[
            jax.ShapeDtypeStruct((3, 4, 2 * T, 5 * T), BF16),
            jax.ShapeDtypeStruct((16, T), BF16),
        ],
        in_specs=[SMEM] + [ANY] * 4,
        out_specs=[VMEM, VMEM],
        scratch_shapes=[pltpu.VMEM((8, BLOCK, T), BF16), pltpu.SemaphoreType.DMA((9,))],
        compiler_params=params(),
        cost_estimate=cost(20 << 20, 8 << 20),
        name="left_panels",
    )(place, same, r1, rm, r2)


def edge_kernel(place, own, up, down, far_head, far_tail, to_core, to_halo, sem):
    b, core = place[2], place[3]
    copies = []
    for n, (out, start) in enumerate(((to_core, 1 - core), (to_halo, core))):
        for k, (source, panel) in enumerate(((own, b), (up, (b + 3) % 4), (down, (b + 1) % 4), (None, (b + 2) % 4))):
            head, tail = (source, source) if source is not None else (far_head, far_tail)
            base = 3 * HEAD if source is not None else 0
            copies.append(
                pltpu.make_async_copy(
                    head.at[pl.ds(pl.multiple_of(start * HEAD, 16), 2 * HEAD)],
                    out.at[panel, pl.ds(0, 2 * HEAD)],
                    sem.at[8 * n + 2 * k],
                )
            )
            copies.append(
                pltpu.make_async_copy(
                    tail.at[pl.ds(pl.multiple_of(base + start * TAIL, 16), 2 * TAIL)],
                    out.at[panel, pl.ds(2 * HEAD, 2 * TAIL)],
                    sem.at[8 * n + 2 * k + 1],
                )
            )
    run_all(copies)


def edges(place, own, up, down, far_head, far_tail):
    shape = jax.ShapeDtypeStruct((4, 2 * (HEAD + TAIL), T), BF16)
    return pl.pallas_call(
        edge_kernel,
        out_shape=[shape, shape],
        in_specs=[SMEM] + [ANY] * 5,
        out_specs=[ANY] * 2,
        scratch_shapes=[pltpu.SemaphoreType.DMA((16,))],
        compiler_params=params(),
        cost_estimate=cost(0, 4 << 20),
        name="edges",
    )(place, own, up, down, far_head, far_tail)


def multiply_kernel(
    place, own, up, down, far_head, far_tail, from_core, from_halo, left, mine, partner,
    keep, give, heads, tails, right, sem,
):
    b, core = place[2], place[3]
    copies = []
    for k, (source, panel) in enumerate(((own, b), (up, (b + 3) % 4), (down, (b + 1) % 4), (None, (b + 2) % 4))):
        head = far_head if source is None else source.at[pl.ds(0, 3 * HEAD)]
        tail = far_tail if source is None else source.at[pl.ds(3 * HEAD, 3 * TAIL)]
        copies.append(pltpu.make_async_copy(head, heads.at[panel, pl.ds(2 * HEAD, 3 * HEAD)], sem.at[2 * k]))
        copies.append(pltpu.make_async_copy(tail, tails.at[panel, pl.ds(2 * TAIL, 3 * TAIL)], sem.at[2 * k + 1]))
    for k, (source, slot) in enumerate(((from_core, 5 * (1 - core)), (from_halo, 5 * core))):
        copies.append(
            pltpu.make_async_copy(
                source.at[:, pl.ds(0, 2 * HEAD)],
                heads.at[:, pl.ds(pl.multiple_of(slot * HEAD, 16), 2 * HEAD)],
                sem.at[8 + 2 * k],
            )
        )
        copies.append(
            pltpu.make_async_copy(
                source.at[:, pl.ds(2 * HEAD, 2 * TAIL)],
                tails.at[:, pl.ds(pl.multiple_of(slot * TAIL, 16), 2 * TAIL)],
                sem.at[9 + 2 * k],
            )
        )
    run_all(copies)
    half = (lanes() >= T // 2).astype(F32)
    zero = jnp.zeros((T, T), BF16)
    sums = [None] * 3
    for p in range(4):
        for k in range(7):
            keys = tails[p, k * TAIL + T : (k + 1) * TAIL, :].astype(F32) + float(k)
            v0 = heads[p, k * HEAD : (k + 1) * HEAD, :].astype(F32)
            v1 = tails[p, k * TAIL : k * TAIL + T, :].astype(F32)
            w0, w1 = turned(v0), turned(v1)
            for w in range(4):
                into = (p % 2, slice(k * T, (k + 1) * T), slice(w * T, (w + 1) * T))
                if 2 * w + 1 < k - 2 or 2 * w > k + 2:
                    right[into] = zero
                    continue
                target = half + float(2 * w)
                pick = [jnp.where(keys[n : n + 1] == target, 1.0, 0.0) for n in range(4)]
                block = (v0 * pick[0] + w0 * pick[1]) + (v1 * pick[2] + w1 * pick[3])
                right[into] = block.astype(BF16)
        for i in range(3):
            first = i // 2 * T
            part = jnp.dot(
                left[i, p],
                right[p % 2, i * T : (i + 5) * T, first : first + 3 * T],
                preferred_element_type=F32,
            )
            sums[i] = part if sums[i] is None else sums[i] + part
    for i in range(3):
        for side, (out, source) in enumerate(((keep, mine), (give, partner))):
            keys = source[...].astype(F32)[4 * i : 4 * i + 4] + float(i + 2)
            for m in range(2):
                total = None
                for w in range(3):
                    v = sums[i][side * T : (side + 1) * T, w * T : (w + 1) * T]
                    target = half + float(2 * (w + i // 2))
                    swap = (1.0 - half) + float(2 * (w + i // 2))
                    key = keys[2 * m : 2 * m + 1]
                    part = v * jnp.where(key == target, 1.0, 0.0)
                    part = part + turned(v) * jnp.where(key == swap, 1.0, 0.0)
                    total = part if total is None else total + part
                out[i, m] = total


def multiply(place, pieces, received, left, mine, partner):
    shape = jax.ShapeDtypeStruct((3, 2, T, T), F32)
    return pl.pallas_call(
        multiply_kernel,
        out_shape=[shape, shape],
        in_specs=[SMEM] + [ANY] * 7 + [VMEM] * 3,
        out_specs=[VMEM, VMEM],
        scratch_shapes=[
            pltpu.VMEM((4, 7 * HEAD, T), BF16),
            pltpu.VMEM((4, 7 * TAIL, T), BF16),
            pltpu.VMEM((2, 7 * T, 4 * T), BF16),
            pltpu.SemaphoreType.DMA((12,)),
        ],
        compiler_params=params(),
        cost_estimate=cost(3 << 30, 10 << 20),
        name="multiply",
    )(place, *pieces, *received, left, mine, partner)


def finish_kernel(own0, got0, own1, got1, out):
    here = lanes() < T // 2
    for i in range(3):
        for m in range(2):
            low = own0[i, m] + got0[i, m]
            high = own1[i, m] + got1[i, m]
            out[i, 2 * m] = jnp.where(here, low, turned(high)).astype(BF16)
            out[i, 2 * m + 1] = jnp.where(here, turned(low), high).astype(BF16)


def finish(own0, got0, own1, got1):
    return pl.pallas_call(
        finish_kernel,
        out_shape=jax.ShapeDtypeStruct((3, 4, T, T), BF16),
        in_specs=[VMEM] * 4,
        out_specs=VMEM,
        compiler_params=params(),
        cost_estimate=cost(1 << 20, 2 << 20),
        name="finish",
    )(own0, got0, own1, got1)


def after(value, *others):
    return lax.optimization_barrier((value,) + others)[0]


def body(x_tiles, tile_cols, tile_counts):
    row, col = lax.axis_index("row"), lax.axis_index("col")
    place = jnp.stack([row, row // 32, row // 8 % 4, row % 2, col // 2, col % 2]).astype(I32)
    block, piece0, piece1, keys = pack(place, tile_cols, tile_counts, x_tiles)
    own = (piece0, piece1)
    up = [None, None]
    down = [None, None]
    far_head = [None, None]
    far_tail = [None, None]
    for h in range(2):
        up[h], down[h] = send(own[h], along_z(4)), send(own[h], along_z(-4))
    g1, g3, g2 = send(block, along_x(1)), send(block, along_x(-1)), send(block, along_x(2))
    for h in range(2):
        far_head[h] = send(up[h][: 3 * HEAD], along_z(4))
        far_tail[h] = send(down[h][3 * HEAD :], along_z(-4))
    same, other = sort_panels(place, block, g1, g2, g3, keys)
    r1, rm, r2 = send(other, along_y(1)), send(other, along_y(-1)), send(same, along_y(2))
    left, partner = left_panels(place, same, r1, rm, r2)
    kept, got = [], []
    for h in range(2):
        pieces = (own[h], up[h], down[h], far_head[h], far_tail[h])
        to_core, to_halo = edges(place, *pieces)
        received = (send(to_core, CORE), send(to_halo, HALO))
        keep, give = multiply(place, pieces, received, left, keys, partner)
        kept.append(keep)
        got.append(send(give, PLANE))
    return finish(kept[0], got[0], kept[1], got[1])


def solution(mesh):
    placed = (P("row", "col", None, None), P("row", "col"), P("row", "col"))
    return jax.shard_map(
        body, mesh=mesh, in_specs=placed, out_specs=P("row", "col", None, None), check_vma=False
    )
```

time: 1230 us -> 170 us (0.14); the launches traced: 1210 us -> 168 us
  starting transfers between devices: 612 us -> 100 us
  waiting for transfers between devices: 293 us -> 36.9 us
  local copies, waits for them, and re-layouts: 162 us -> 2.54 us
  matrix products: 71.5 us -> 0 us
  blocking collectives: 46.8 us -> 0 us
  Pallas kernels: 0 us -> 28 us
  between operations: 15 us -> 0.34 us
    ppermute x69 -> x20, starting transfers between devices: 612 us -> 100 us  [send(): return lax.ppermute(block, ('row', 'col'), pairs)]
    ppermute x69 -> x20, waiting for transfers between devices: 293 us -> 36.9 us  [send(): return lax.ppermute(block, ('row', 'col'), pairs)]
    concatenate x4 -> x0, local copies, waits for them, and re-layouts: 155 us -> none  [the longest x1 154 us: body(): stack_tiles = jnp.concatenate([piece[0] for piece in pieces], axis=0)]
    dot_general x12 -> x0, matrix products: 71.5 us -> none  [the longest x4 30.8 us: advance(): jnp.einsum('rgus,rguxy->rgsxy', hits, chosen, preferred_element_type=jnp....]
    all_gather x2 -> x0, blocking collectives: 46.8 us -> none  [the longest x1 31 us: body(): lax.all_gather(tile_cols, 'col', axis=1, tiled=True)]
    pallas_call x0 -> x8, Pallas kernels: none -> 28 us  [the longest x2 14 us: multiply(): pl.pallas_call(multiply_kernel, out_shape=[shape, shape], in_specs=[SMEM]...]
  transfers between devices with their start and end apart: 70 -> 20, of which waited for: 28 -> 7; matrix products, arithmetic and copies ran while one was open for 14% -> 0% of each run, Pallas kernels for 0% -> 16%
where the time goes in v1:
time: 170 us; the launch traced here: 168 us
  starting transfers between devices  100 us (59%)
  waiting for transfers between devices  36.9 us (22%)
  Pallas kernels  28 us (16%)
  local copies, waits for them, and re-layouts  2.54 us (1%)
    ppermute x20, starting transfers between devices, send(): return lax.ppermute(block, ('row', 'col'), pairs)  100 us
    ppermute x20, waiting for transfers between devices, send(): return lax.ppermute(block, ('row', 'col'), pairs)  36.9 us
    pallas_call x2, Pallas kernels, multiply(): pl.pallas_call(multiply_kernel, out_shape=[shape, shape], in_specs=[SMEM]...  14 us
    pallas_call x1, Pallas kernels, left_panels(): pl.pallas_call(left_kernel, out_shape=[jax.ShapeDtypeStruct((3, 4, 2 * T,...  6.45 us
    pallas_call x2, Pallas kernels, edges(): pl.pallas_call(edge_kernel, out_shape=[shape, shape], in_specs=[SMEM] + [...  4.34 us
  transfers between devices with their start and end apart: 20, of which 7 were waited for; matrix products, arithmetic and copies ran while one was open for 0% of the time, Pallas kernels for 16%

profile of v1, /device:TPU:6, one launch (start us, length us, event | category | flops | bytes accessed | tf_op | source)
XLA Modules:
  0.0 167.7 jit_solution(2790394944691589904)
XLA Ops:
  0.0 0.7 copy.4.counts
  0.7 0.1 stack.27.place
  0.8 0.0 copy-start
  0.8 1.0 copy-done
  1.8 0.0 copy-start.1
  1.8 0.7 copy-done.1
  2.5 0.9 pack.1
  3.4 7.8 %collective-permute-start.6 = (bf16[1552,128]{1,0:T(8,128)(2,1)S(1)}, bf16[1552,128]{1,0:T(8,128)(2,1)S(1)}, u32[]{:S(2)}, u32[]{:S(2)}) collective-permute-start(bf16[1552,128]{1,0:T(8,128)(2,1)S(1)} %get-tuple-element.24.own), channel_id=1, source_target_pairs={{0,2},{1,3},{2,4},{3,5},{4,6},{5,7},{6,0},{7,1},{8,10},{9,11},{10,... | collective-permute-start | bytes 1191944 | tf_op jit(solution)/shard_map/ppermute | solution.py:52
  11.1 1.9 %collective-permute-start.7 = (bf16[1552,128]{1,0:T(8,128)(2,1)S(1)}, bf16[1552,128]{1,0:T(8,128)(2,1)S(1)}, u32[]{:S(2)}, u32[]{:S(2)}) collective-permute-start(bf16[1552,128]{1,0:T(8,128)(2,1)S(1)} %get-tuple-element.24.own), channel_id=1, source_target_pairs={{0,4},{1,5},{2,6},{3,7},{4,0},{5,1},{6,2},{7,3},{8,12},{9,13},{10,... | collective-permute-start | bytes 1191944 | tf_op jit(solution)/shard_map/ppermute | solution.py:52
  13.1 2.8 %collective-permute-start.8 = (bf16[1552,128]{1,0:T(8,128)(2,1)S(1)}, bf16[1552,128]{1,0:T(8,128)(2,1)S(1)}, u32[]{:S(2)}, u32[]{:S(2)}) collective-permute-start(bf16[1552,128]{1,0:T(8,128)(2,1)S(1)} %get-tuple-element.24.own), channel_id=1, source_target_pairs={{0,6},{1,7},{2,0},{3,1},{4,2},{5,3},{6,4},{7,5},{8,14},{9,15},{10,... | collective-permute-start | bytes 1191944 | tf_op jit(solution)/shard_map/ppermute | solution.py:52
  15.8 8.9 %collective-permute-start.14 = (bf16[816,128]{1,0:T(8,128)(2,1)S(1)}, bf16[816,128]{1,0:T(8,128)(2,1)S(1)}, u32[]{:S(2)}, u32[]{:S(2)}) collective-permute-start(bf16[816,128]{1,0:T(8,128)(2,1)S(1)} %get-tuple-element.32.own), channel_id=1, source_target_pairs={{0,192},{1,193},{2,194},{3,195},{4,196},{5,197},{6,198},{7,199},{8... | collective-permute-start | bytes 626696 | tf_op jit(solution)/shard_map/ppermute | solution.py:52
  24.8 0.2 collective-permute-done.6.g1
  25.0 0.0 collective-permute-done.7.g2
  25.0 3.1 %collective-permute-done.8.g3 = bf16[1552,128]{1,0:T(8,128)(2,1)S(1)} collective-permute-done((bf16[1552,128]{1,0:T(8,128)(2,1)S(1)}, bf16[1552,128]{1,0:T(8,128)(2,1)S(1)}, u32[]{:S(2)}, u32[]{:S(2)}) %collective-permute-start.8) | collective-permute-done | bytes 397344 | tf_op jit(solution)/shard_map/ppermute | solution.py:52
  28.1 1.4 sort_panels.1
  29.6 5.1 %collective-permute-start.10 = (bf16[3120,128]{1,0:T(8,128)(2,1)S(1)}, bf16[3120,128]{1,0:T(8,128)(2,1)S(1)}, u32[]{:S(2)}, u32[]{:S(2)}) collective-permute-start(bf16[3120,128]{1,0:T(8,128)(2,1)S(1)} %get-tuple-element.27), channel_id=1, source_target_pairs={{0,257},{1,256},{2,259},{3,258},{4,261},{5,260},{6,263},{7,262},{8... | collective-permute-start | bytes 2396168 | tf_op jit(solution)/shard_map/ppermute | solution.py:52
  34.7 2.5 %collective-permute-start.11 = (bf16[3104,128]{1,0:T(8,128)(2,1)S(1)}, bf16[3104,128]{1,0:T(8,128)(2,1)S(1)}, u32[]{:S(2)}, u32[]{:S(2)}) collective-permute-start(bf16[3104,128]{1,0:T(8,128)(2,1)S(1)} %get-tuple-element.26.same), channel_id=1, source_target_pairs={{0,1},{1,0},{2,3},{3,2},{4,5},{5,4},{6,7},{7,6},{8,9},{9,8},{10,11... | collective-permute-start | bytes 2383880 | tf_op jit(solution)/shard_map/ppermute | solution.py:52
  37.3 9.1 %collective-permute-start.13 = (bf16[816,128]{1,0:T(8,128)(2,1)S(1)}, bf16[816,128]{1,0:T(8,128)(2,1)S(1)}, u32[]{:S(2)}, u32[]{:S(2)}) collective-permute-start(bf16[816,128]{1,0:T(8,128)(2,1)S(1)} %get-tuple-element.32.own), channel_id=1, source_target_pairs={{0,64},{1,65},{2,66},{3,67},{4,68},{5,69},{6,70},{7,71},{8,72},{9,... | collective-permute-start | bytes 626696 | tf_op jit(solution)/shard_map/ppermute | solution.py:52
  46.4 5.6 %collective-permute-start.1 = (bf16[816,128]{1,0:T(8,128)(2,1)S(1)}, bf16[816,128]{1,0:T(8,128)(2,1)S(1)}, u32[]{:S(2)}, u32[]{:S(2)}) collective-permute-start(bf16[816,128]{1,0:T(8,128)(2,1)S(1)} %get-tuple-element.21.own), channel_id=1, source_target_pairs={{0,192},{1,193},{2,194},{3,195},{4,196},{5,197},{6,198},{7,199},{8... | collective-permute-start | bytes 626696 | tf_op jit(solution)/shard_map/ppermute | solution.py:52
  51.9 0.0 collective-permute-done.14.down
  51.9 5.5 %collective-permute-start = (bf16[816,128]{1,0:T(8,128)(2,1)S(1)}, bf16[816,128]{1,0:T(8,128)(2,1)S(1)}, u32[]{:S(2)}, u32[]{:S(2)}) collective-permute-start(bf16[816,128]{1,0:T(8,128)(2,1)S(1)} %get-tuple-element.21.own), channel_id=1, source_target_pairs={{0,64},{1,65},{2,66},{3,67},{4,68},{5,69},{6,70},{7,71},{8,72},{9,... | collective-permute-start | bytes 626696 | tf_op jit(solution)/shard_map/ppermute | solution.py:52
  57.4 0.0 collective-permute-done.13.up
  57.4 2.9 %collective-permute-start.9 = (bf16[3120,128]{1,0:T(8,128)(2,1)S(1)}, bf16[3120,128]{1,0:T(8,128)(2,1)S(1)}, u32[]{:S(2)}, u32[]{:S(2)}) collective-permute-start(bf16[3120,128]{1,0:T(8,128)(2,1)S(1)} %get-tuple-element.27), channel_id=1, source_target_pairs={{0,256},{1,257},{2,258},{3,259},{4,260},{5,261},{6,262},{7,263},{8... | collective-permute-start | bytes 2396168 | tf_op jit(solution)/shard_map/ppermute | solution.py:52
  60.3 13.2 %collective-permute-done.1.down = bf16[816,128]{1,0:T(8,128)(2,1)S(1)} collective-permute-done((bf16[816,128]{1,0:T(8,128)(2,1)S(1)}, bf16[816,128]{1,0:T(8,128)(2,1)S(1)}, u32[]{:S(2)}, u32[]{:S(2)}) %collective-permute-start.1) | collective-permute-done | bytes 208928 | tf_op jit(solution)/shard_map/ppermute | solution.py:52
  73.5 4.4 %collective-permute-start.16 = (bf16[432,128]{1,0:T(8,128)(2,1)S(1)}, bf16[432,128]{1,0:T(8,128)(2,1)S(1)}, u32[]{:S(2)}, u32[]{:S(2)}) collective-permute-start(bf16[432,128]{1,0:T(8,128)(2,1)S(1)} %slice.19), channel_id=1, source_target_pairs={{0,192},{1,193},{2,194},{3,195},{4,196},{5,197},{6,198},{7,199},{8... | collective-permute-start | bytes 331784 | tf_op jit(solution)/shard_map/ppermute | solution.py:52
  77.9 0.0 collective-permute-done.up
  77.9 13.7 %collective-permute-start.15 = (bf16[384,128]{1,0:T(8,128)(2,1)S(1)}, bf16[384,128]{1,0:T(8,128)(2,1)S(1)}, u32[]{:S(2)}, u32[]{:S(2)}) collective-permute-start(bf16[384,128]{1,0:T(8,128)(2,1)S(1)} %slice.18), channel_id=1, source_target_pairs={{0,64},{1,65},{2,66},{3,67},{4,68},{5,69},{6,70},{7,71},{8,72},{9,... | collective-permute-start | bytes 294920 | tf_op jit(solution)/shard_map/ppermute | solution.py:52
  91.6 5.6 %collective-permute-done.15.far_head = bf16[384,128]{1,0:T(8,128)(2,1)S(1)} collective-permute-done((bf16[384,128]{1,0:T(8,128)(2,1)S(1)}, bf16[384,128]{1,0:T(8,128)(2,1)S(1)}, u32[]{:S(2)}, u32[]{:S(2)}) %collective-permute-start.15) | collective-permute-done | bytes 98336 | tf_op jit(solution)/shard_map/ppermute | solution.py:52
  97.2 5.8 %collective-permute-start.3 = (bf16[432,128]{1,0:T(8,128)(2,1)S(1)}, bf16[432,128]{1,0:T(8,128)(2,1)S(1)}, u32[]{:S(2)}, u32[]{:S(2)}) collective-permute-start(bf16[432,128]{1,0:T(8,128)(2,1)S(1)} %slice.17), channel_id=1, source_target_pairs={{0,192},{1,193},{2,194},{3,195},{4,196},{5,197},{6,198},{7,199},{8... | collective-permute-start | bytes 331784 | tf_op jit(solution)/shard_map/ppermute | solution.py:52
  103.1 0.0 collective-permute-done.16.far_tail
  103.1 4.4 %collective-permute-start.2 = (bf16[384,128]{1,0:T(8,128)(2,1)S(1)}, bf16[384,128]{1,0:T(8,128)(2,1)S(1)}, u32[]{:S(2)}, u32[]{:S(2)}) collective-permute-start(bf16[384,128]{1,0:T(8,128)(2,1)S(1)} %slice.16), channel_id=1, source_target_pairs={{0,64},{1,65},{2,66},{3,67},{4,68},{5,69},{6,70},{7,71},{8,72},{9,... | collective-permute-start | bytes 294920 | tf_op jit(solution)/shard_map/ppermute | solution.py:52
  107.5 2.2 %edges.3 = (bf16[4,544,128]{2,1,0:T(8,128)(2,1)S(1)}, bf16[4,544,128]{2,1,0:T(8,128)(2,1)S(1)}) custom-call(s32[6]{0:T(128)S(1)} %stack.27.place, bf16[816,128]{1,0:T(8,128)(2,1)S(1)} %get-tuple-element.32.own, bf16[816,128]{1,0:T(8,128)(2,1)S(1)} %collective-permute-done.13.up, bf16[816,128]{1,0:T(8,128)(2,1)S(1)} %collective-permute-done.14.down, ...), custom_call_target="tpu_custom_call" | custom-call | bytes 4194304 | tf_op jit(solution)/shard_map/edges/pallas_call | solution.py:244
  109.7 4.9 %collective-permute-done.2.far_head = bf16[384,128]{1,0:T(8,128)(2,1)S(1)} collective-permute-done((bf16[384,128]{1,0:T(8,128)(2,1)S(1)}, bf16[384,128]{1,0:T(8,128)(2,1)S(1)}, u32[]{:S(2)}, u32[]{:S(2)}) %collective-permute-start.2) | collective-permute-done | bytes 98336 | tf_op jit(solution)/shard_map/ppermute | solution.py:52
  114.5 1.9 %collective-permute-start.17 = (bf16[4,544,128]{2,1,0:T(8,128)(2,1)S(1)}, bf16[4,544,128]{2,1,0:T(8,128)(2,1)S(1)}, u32[]{:S(2)}, u32[]{:S(2)}) collective-permute-start(bf16[4,544,128]{2,1,0:T(8,128)(2,1)S(1)} %get-tuple-element.33), channel_id=1, source_target_pairs={{0,8},{1,9},{2,10},{3,11},{4,12},{5,13},{6,14},{7,15},{8,0},{9,1},... | collective-permute-start | bytes 1671176 | tf_op jit(solution)/shard_map/ppermute | solution.py:52
  116.5 0.0 collective-permute-done.3.far_tail
  116.5 8.0 %collective-permute-start.18 = (bf16[4,544,128]{2,1,0:T(8,128)(2,1)S(1)}, bf16[4,544,128]{2,1,0:T(8,128)(2,1)S(1)}, u32[]{:S(2)}, u32[]{:S(2)}) collective-permute-start(bf16[4,544,128]{2,1,0:T(8,128)(2,1)S(1)} %get-tuple-element.34), channel_id=1, source_target_pairs={{0,248},{1,249},{2,250},{3,251},{4,252},{5,253},{6,254},{7,255},{8... | collective-permute-start | bytes 1671176 | tf_op jit(solution)/shard_map/ppermute | solution.py:52
  124.5 2.2 %edges.2 = (bf16[4,544,128]{2,1,0:T(8,128)(2,1)S(1)}, bf16[4,544,128]{2,1,0:T(8,128)(2,1)S(1)}) custom-call(s32[6]{0:T(128)S(1)} %stack.27.place, bf16[816,128]{1,0:T(8,128)(2,1)S(1)} %get-tuple-element.21.own, bf16[816,128]{1,0:T(8,128)(2,1)S(1)} %collective-permute-done.up, bf16[816,128]{1,0:T(8,128)(2,1)S(1)} %collective-permute-done.1.down, ...), custom_call_target="tpu_custom_call" | custom-call | bytes 4194304 | tf_op jit(solution)/shard_map/edges/pallas_call | solution.py:244
  126.7 0.0 collective-permute-done.11.r2
  126.7 1.9 %collective-permute-start.4 = (bf16[4,544,128]{2,1,0:T(8,128)(2,1)S(1)}, bf16[4,544,128]{2,1,0:T(8,128)(2,1)S(1)}, u32[]{:S(2)}, u32[]{:S(2)}) collective-permute-start(bf16[4,544,128]{2,1,0:T(8,128)(2,1)S(1)} %get-tuple-element.22), channel_id=1, source_target_pairs={{0,8},{1,9},{2,10},{3,11},{4,12},{5,13},{6,14},{7,15},{8,0},{9,1},... | collective-permute-start | bytes 1671176 | tf_op jit(solution)/shard_map/ppermute | solution.py:52
  128.6 0.0 collective-permute-done.10.rm
  128.6 1.9 %collective-permute-start.5 = (bf16[4,544,128]{2,1,0:T(8,128)(2,1)S(1)}, bf16[4,544,128]{2,1,0:T(8,128)(2,1)S(1)}, u32[]{:S(2)}, u32[]{:S(2)}) collective-permute-start(bf16[4,544,128]{2,1,0:T(8,128)(2,1)S(1)} %get-tuple-element.23), channel_id=1, source_target_pairs={{0,248},{1,249},{2,250},{3,251},{4,252},{5,253},{6,254},{7,255},{8... | collective-permute-start | bytes 1671176 | tf_op jit(solution)/shard_map/ppermute | solution.py:52
  130.6 0.0 collective-permute-done.9.r1
  130.6 6.5 %left_panels.1 = (bf16[3,4,256,640]{3,2,1,0:T(8,128)(2,1)}, bf16[16,128]{1,0:T(8,128)(2,1)S(1)}) custom-call(s32[6]{0:T(128)S(1)} %stack.27.place, bf16[3104,128]{1,0:T(8,128)(2,1)S(1)} %get-tuple-element.26.same, bf16[3120,128]{1,0:T(8,128)(2,1)S(1)} %collective-permute-done.9.r1, bf16[3120,128]{1,0:T(8,128)(2,1)S(1)} %collective-permute-done.10.rm, ...), custom_call_target="tpu_custom_call" | custom-call | flops 20971520 | bytes 8388608 | tf_op jit(solution)/shard_map/left_panels/pallas_call | solution.py:203
  137.0 0.0 collective-permute-done.17.from_core
  137.0 0.0 collective-permute-done.18.from_halo
  137.1 7.0 %multiply.3 = (f32[3,2,128,128]{3,2,1,0:T(8,128)S(1)}, f32[3,2,128,128]{3,2,1,0:T(8,128)S(1)}) custom-call(s32[6]{0:T(128)S(1)} %stack.27.place, bf16[816,128]{1,0:T(8,128)(2,1)S(1)} %get-tuple-element.32.own, bf16[816,128]{1,0:T(8,128)(2,1)S(1)} %collective-permute-done.13.up, bf16[816,128]{1,0:T(8,128)(2,1)S(1)} %collective-permute-done.14.down, ...), custom_call_target="tpu_custom_call" | custom-call | flops 3221225472 | bytes 10485760 | tf_op jit(solution)/shard_map/multiply/pallas_call | solution.py:327
  144.1 2.6 %collective-permute-start.19 = (f32[3,2,128,128]{3,2,1,0:T(8,128)S(1)}, f32[3,2,128,128]{3,2,1,0:T(8,128)S(1)}, u32[]{:S(2)}, u32[]{:S(2)}) collective-permute-start(f32[3,2,128,128]{3,2,1,0:T(8,128)S(1)} %get-tuple-element.36), channel_id=1, source_target_pairs={{0,256},{1,257},{2,258},{3,259},{4,260},{5,261},{6,262},{7,263},{8... | collective-permute-start | bytes 1179656 | tf_op jit(solution)/shard_map/ppermute | solution.py:52
  146.6 0.0 collective-permute-done.4.from_core
  146.6 0.0 collective-permute-done.5.from_halo
  146.7 7.0 %multiply.2 = (f32[3,2,128,128]{3,2,1,0:T(8,128)S(1)}, f32[3,2,128,128]{3,2,1,0:T(8,128)S(1)}) custom-call(s32[6]{0:T(128)S(1)} %stack.27.place, bf16[816,128]{1,0:T(8,128)(2,1)S(1)} %get-tuple-element.21.own, bf16[816,128]{1,0:T(8,128)(2,1)S(1)} %collective-permute-done.up, bf16[816,128]{1,0:T(8,128)(2,1)S(1)} %collective-permute-done.1.down, ...), custom_call_target="tpu_custom_call" | custom-call | flops 3221225472 | bytes 10485760 | tf_op jit(solution)/shard_map/multiply/pallas_call | solution.py:327
  153.7 3.3 %collective-permute-start.12 = (f32[3,2,128,128]{3,2,1,0:T(8,128)S(1)}, f32[3,2,128,128]{3,2,1,0:T(8,128)S(1)}, u32[]{:S(2)}, u32[]{:S(2)}) collective-permute-start(f32[3,2,128,128]{3,2,1,0:T(8,128)S(1)} %get-tuple-element.31), channel_id=1, source_target_pairs={{0,256},{1,257},{2,258},{3,259},{4,260},{5,261},{6,262},{7,263},{8... | collective-permute-start | bytes 1179656 | tf_op jit(solution)/shard_map/ppermute | solution.py:52
  156.9 0.5 collective-permute-done.19.got1
  157.5 9.3 %collective-permute-done.12.got0 = f32[3,2,128,128]{3,2,1,0:T(8,128)S(1)} collective-permute-done((f32[3,2,128,128]{3,2,1,0:T(8,128)S(1)}, f32[3,2,128,128]{3,2,1,0:T(8,128)S(1)}, u32[]{:S(2)}, u32[]{:S(2)}) %collective-permute-start.12) | collective-permute-done | bytes 393248 | tf_op jit(solution)/shard_map/ppermute | solution.py:52
  166.8 0.9 finish.1
  (4 shorter events, 0.0 us)
Async XLA Ops:
  0.8 1.0 copy-start
  1.8 0.7 copy-start.1
  3.4 21.6 %collective-permute-start.6 = (bf16[1552,128]{1,0:T(8,128)(2,1)S(1)}, bf16[1552,128]{1,0:T(8,128)(2,1)S(1)}, u32[]{:S(2)}, u32[]{:S(2)}) collective-permute-start(bf16[1552,128]{1,0:T(8,128)(2,1)S(1)} %get-tuple-element.24.own), channel_id=1, source_target_pairs={{0,2},{1,3},{2,4},{3,5},{4,6},{5,7},{6,0},{7,1},{8,10},{9,11},{10,... | collective-permute-start | bytes 1191944 | tf_op jit(solution)/shard_map/ppermute | solution.py:52
  11.1 13.9 %collective-permute-start.7 = (bf16[1552,128]{1,0:T(8,128)(2,1)S(1)}, bf16[1552,128]{1,0:T(8,128)(2,1)S(1)}, u32[]{:S(2)}, u32[]{:S(2)}) collective-permute-start(bf16[1552,128]{1,0:T(8,128)(2,1)S(1)} %get-tuple-element.24.own), channel_id=1, source_target_pairs={{0,4},{1,5},{2,6},{3,7},{4,0},{5,1},{6,2},{7,3},{8,12},{9,13},{10,... | collective-permute-start | bytes 1191944 | tf_op jit(solution)/shard_map/ppermute | solution.py:52
  13.1 15.1 %collective-permute-start.8 = (bf16[1552,128]{1,0:T(8,128)(2,1)S(1)}, bf16[1552,128]{1,0:T(8,128)(2,1)S(1)}, u32[]{:S(2)}, u32[]{:S(2)}) collective-permute-start(bf16[1552,128]{1,0:T(8,128)(2,1)S(1)} %get-tuple-element.24.own), channel_id=1, source_target_pairs={{0,6},{1,7},{2,0},{3,1},{4,2},{5,3},{6,4},{7,5},{8,14},{9,15},{10,... | collective-permute-start | bytes 1191944 | tf_op jit(solution)/shard_map/ppermute | solution.py:52
  15.8 36.1 %collective-permute-start.14 = (bf16[816,128]{1,0:T(8,128)(2,1)S(1)}, bf16[816,128]{1,0:T(8,128)(2,1)S(1)}, u32[]{:S(2)}, u32[]{:S(2)}) collective-permute-start(bf16[816,128]{1,0:T(8,128)(2,1)S(1)} %get-tuple-element.32.own), channel_id=1, source_target_pairs={{0,192},{1,193},{2,194},{3,195},{4,196},{5,197},{6,198},{7,199},{8... | collective-permute-start | bytes 626696 | tf_op jit(solution)/shard_map/ppermute | solution.py:52
  29.6 99.0 %collective-permute-start.10 = (bf16[3120,128]{1,0:T(8,128)(2,1)S(1)}, bf16[3120,128]{1,0:T(8,128)(2,1)S(1)}, u32[]{:S(2)}, u32[]{:S(2)}) collective-permute-start(bf16[3120,128]{1,0:T(8,128)(2,1)S(1)} %get-tuple-element.27), channel_id=1, source_target_pairs={{0,257},{1,256},{2,259},{3,258},{4,261},{5,260},{6,263},{7,262},{8... | collective-permute-start | bytes 2396168 | tf_op jit(solution)/shard_map/ppermute | solution.py:52
  34.7 92.0 %collective-permute-start.11 = (bf16[3104,128]{1,0:T(8,128)(2,1)S(1)}, bf16[3104,128]{1,0:T(8,128)(2,1)S(1)}, u32[]{:S(2)}, u32[]{:S(2)}) collective-permute-start(bf16[3104,128]{1,0:T(8,128)(2,1)S(1)} %get-tuple-element.26.same), channel_id=1, source_target_pairs={{0,1},{1,0},{2,3},{3,2},{4,5},{5,4},{6,7},{7,6},{8,9},{9,8},{10,11... | collective-permute-start | bytes 2383880 | tf_op jit(solution)/shard_map/ppermute | solution.py:52
  37.3 20.2 %collective-permute-start.13 = (bf16[816,128]{1,0:T(8,128)(2,1)S(1)}, bf16[816,128]{1,0:T(8,128)(2,1)S(1)}, u32[]{:S(2)}, u32[]{:S(2)}) collective-permute-start(bf16[816,128]{1,0:T(8,128)(2,1)S(1)} %get-tuple-element.32.own), channel_id=1, source_target_pairs={{0,64},{1,65},{2,66},{3,67},{4,68},{5,69},{6,70},{7,71},{8,72},{9,... | collective-permute-start | bytes 626696 | tf_op jit(solution)/shard_map/ppermute | solution.py:52
  46.4 27.1 %collective-permute-start.1 = (bf16[816,128]{1,0:T(8,128)(2,1)S(1)}, bf16[816,128]{1,0:T(8,128)(2,1)S(1)}, u32[]{:S(2)}, u32[]{:S(2)}) collective-permute-start(bf16[816,128]{1,0:T(8,128)(2,1)S(1)} %get-tuple-element.21.own), channel_id=1, source_target_pairs={{0,192},{1,193},{2,194},{3,195},{4,196},{5,197},{6,198},{7,199},{8... | collective-permute-start | bytes 626696 | tf_op jit(solution)/shard_map/ppermute | solution.py:52
  51.9 25.9 %collective-permute-start = (bf16[816,128]{1,0:T(8,128)(2,1)S(1)}, bf16[816,128]{1,0:T(8,128)(2,1)S(1)}, u32[]{:S(2)}, u32[]{:S(2)}) collective-permute-start(bf16[816,128]{1,0:T(8,128)(2,1)S(1)} %get-tuple-element.21.own), channel_id=1, source_target_pairs={{0,64},{1,65},{2,66},{3,67},{4,68},{5,69},{6,70},{7,71},{8,72},{9,... | collective-permute-start | bytes 626696 | tf_op jit(solution)/shard_map/ppermute | solution.py:52
  57.4 73.2 %collective-permute-start.9 = (bf16[3120,128]{1,0:T(8,128)(2,1)S(1)}, bf16[3120,128]{1,0:T(8,128)(2,1)S(1)}, u32[]{:S(2)}, u32[]{:S(2)}) collective-permute-start(bf16[3120,128]{1,0:T(8,128)(2,1)S(1)} %get-tuple-element.27), channel_id=1, source_target_pairs={{0,256},{1,257},{2,258},{3,259},{4,260},{5,261},{6,262},{7,263},{8... | collective-permute-start | bytes 2396168 | tf_op jit(solution)/shard_map/ppermute | solution.py:52
  73.5 29.6 %collective-permute-start.16 = (bf16[432,128]{1,0:T(8,128)(2,1)S(1)}, bf16[432,128]{1,0:T(8,128)(2,1)S(1)}, u32[]{:S(2)}, u32[]{:S(2)}) collective-permute-start(bf16[432,128]{1,0:T(8,128)(2,1)S(1)} %slice.19), channel_id=1, source_target_pairs={{0,192},{1,193},{2,194},{3,195},{4,196},{5,197},{6,198},{7,199},{8... | collective-permute-start | bytes 331784 | tf_op jit(solution)/shard_map/ppermute | solution.py:52
  77.9 19.3 %collective-permute-start.15 = (bf16[384,128]{1,0:T(8,128)(2,1)S(1)}, bf16[384,128]{1,0:T(8,128)(2,1)S(1)}, u32[]{:S(2)}, u32[]{:S(2)}) collective-permute-start(bf16[384,128]{1,0:T(8,128)(2,1)S(1)} %slice.18), channel_id=1, source_target_pairs={{0,64},{1,65},{2,66},{3,67},{4,68},{5,69},{6,70},{7,71},{8,72},{9,... | collective-permute-start | bytes 294920 | tf_op jit(solution)/shard_map/ppermute | solution.py:52
  97.2 19.2 %collective-permute-start.3 = (bf16[432,128]{1,0:T(8,128)(2,1)S(1)}, bf16[432,128]{1,0:T(8,128)(2,1)S(1)}, u32[]{:S(2)}, u32[]{:S(2)}) collective-permute-start(bf16[432,128]{1,0:T(8,128)(2,1)S(1)} %slice.17), channel_id=1, source_target_pairs={{0,192},{1,193},{2,194},{3,195},{4,196},{5,197},{6,198},{7,199},{8... | collective-permute-start | bytes 331784 | tf_op jit(solution)/shard_map/ppermute | solution.py:52
  103.1 11.5 %collective-permute-start.2 = (bf16[384,128]{1,0:T(8,128)(2,1)S(1)}, bf16[384,128]{1,0:T(8,128)(2,1)S(1)}, u32[]{:S(2)}, u32[]{:S(2)}) collective-permute-start(bf16[384,128]{1,0:T(8,128)(2,1)S(1)} %slice.16), channel_id=1, source_target_pairs={{0,64},{1,65},{2,66},{3,67},{4,68},{5,69},{6,70},{7,71},{8,72},{9,... | collective-permute-start | bytes 294920 | tf_op jit(solution)/shard_map/ppermute | solution.py:52
  114.5 22.5 %collective-permute-start.17 = (bf16[4,544,128]{2,1,0:T(8,128)(2,1)S(1)}, bf16[4,544,128]{2,1,0:T(8,128)(2,1)S(1)}, u32[]{:S(2)}, u32[]{:S(2)}) collective-permute-start(bf16[4,544,128]{2,1,0:T(8,128)(2,1)S(1)} %get-tuple-element.33), channel_id=1, source_target_pairs={{0,8},{1,9},{2,10},{3,11},{4,12},{5,13},{6,14},{7,15},{8,0},{9,1},... | collective-permute-start | bytes 1671176 | tf_op jit(solution)/shard_map/ppermute | solution.py:52
  116.5 20.6 %collective-permute-start.18 = (bf16[4,544,128]{2,1,0:T(8,128)(2,1)S(1)}, bf16[4,544,128]{2,1,0:T(8,128)(2,1)S(1)}, u32[]{:S(2)}, u32[]{:S(2)}) collective-permute-start(bf16[4,544,128]{2,1,0:T(8,128)(2,1)S(1)} %get-tuple-element.34), channel_id=1, source_target_pairs={{0,248},{1,249},{2,250},{3,251},{4,252},{5,253},{6,254},{7,255},{8... | collective-permute-start | bytes 1671176 | tf_op jit(solution)/shard_map/ppermute | solution.py:52
  126.7 19.9 %collective-permute-start.4 = (bf16[4,544,128]{2,1,0:T(8,128)(2,1)S(1)}, bf16[4,544,128]{2,1,0:T(8,128)(2,1)S(1)}, u32[]{:S(2)}, u32[]{:S(2)}) collective-permute-start(bf16[4,544,128]{2,1,0:T(8,128)(2,1)S(1)} %get-tuple-element.22), channel_id=1, source_target_pairs={{0,8},{1,9},{2,10},{3,11},{4,12},{5,13},{6,14},{7,15},{8,0},{9,1},... | collective-permute-start | bytes 1671176 | tf_op jit(solution)/shard_map/ppermute | solution.py:52
  128.6 18.0 %collective-permute-start.5 = (bf16[4,544,128]{2,1,0:T(8,128)(2,1)S(1)}, bf16[4,544,128]{2,1,0:T(8,128)(2,1)S(1)}, u32[]{:S(2)}, u32[]{:S(2)}) collective-permute-start(bf16[4,544,128]{2,1,0:T(8,128)(2,1)S(1)} %get-tuple-element.23), channel_id=1, source_target_pairs={{0,248},{1,249},{2,250},{3,251},{4,252},{5,253},{6,254},{7,255},{8... | collective-permute-start | bytes 1671176 | tf_op jit(solution)/shard_map/ppermute | solution.py:52
  144.1 13.4 %collective-permute-start.19 = (f32[3,2,128,128]{3,2,1,0:T(8,128)S(1)}, f32[3,2,128,128]{3,2,1,0:T(8,128)S(1)}, u32[]{:S(2)}, u32[]{:S(2)}) collective-permute-start(f32[3,2,128,128]{3,2,1,0:T(8,128)S(1)} %get-tuple-element.36), channel_id=1, source_target_pairs={{0,256},{1,257},{2,258},{3,259},{4,260},{5,261},{6,262},{7,263},{8... | collective-permute-start | bytes 1179656 | tf_op jit(solution)/shard_map/ppermute | solution.py:52
  153.7 13.1 %collective-permute-start.12 = (f32[3,2,128,128]{3,2,1,0:T(8,128)S(1)}, f32[3,2,128,128]{3,2,1,0:T(8,128)S(1)}, u32[]{:S(2)}, u32[]{:S(2)}) collective-permute-start(f32[3,2,128,128]{3,2,1,0:T(8,128)S(1)} %get-tuple-element.31), channel_id=1, source_target_pairs={{0,256},{1,257},{2,258},{3,259},{4,260},{5,261},{6,262},{7,263},{8... | collective-permute-start | bytes 1179656 | tf_op jit(solution)/shard_map/ppermute | solution.py:52

commit v2 on v1

--- a/solution.py
+++ b/solution.py
@@ -9,6 +9,10 @@
 
 BF16, F32, I32 = jnp.bfloat16, jnp.float32, jnp.int32
 T = 128
+EDGE = (0, 0)
+MULT = (3 << 30, 3 << 30)
+LEFT = 5700000000
+SORT = 0
 LIMIT = 48 << 20
 BLOCK = 12 * T + 16
 HEAD, TAIL = T, T + 16
@@ -64,11 +68,26 @@
     return lax.broadcasted_iota(I32, (1, T), 1)
 
 
+def flipped(v):
+    return pltpu.roll(v, T // 2, 1)
+
+
+def chosen(keys, target):
+    return jnp.where(keys == target, 1.0, 0.0).astype(BF16)
+
+
 def turned(v):
     return pltpu.roll(v, T // 2, 1)
 
 
-def pack_kernel(place, cols, counts, x, a_out, b0_out, b1_out, k_out):
+def pack_kernel(place, cols_in, counts_in, x_in, a_out, b_out, k_out, cols, counts, x, sem):
+    run_all(
+        [
+            pltpu.make_async_copy(cols_in, cols, sem.at[0]),
+            pltpu.make_async_copy(counts_in, counts, sem.at[1]),
+            pltpu.make_async_copy(x_in, x, sem.at[2]),
+        ]
+    )
     row = lax.broadcasted_iota(I32, (16, T), 0)
     left = lax.broadcasted_iota(I32, (16, T), 1) < T // 2
     plain = jnp.full((16, T), 9, I32)
@@ -78,7 +97,7 @@
         for t in range(4):
             away = (cols[r, t] - (place[0] * 3 + r) + 240) % 24
             away = jnp.where(away > 12, away - 24, away)
-            keys.append(jnp.where(t < counts[r, 0], away, 9))
+            keys.append(jnp.where(t < counts[0, r], away, 9))
             plain = jnp.where(row == r * 4 + t, keys[t], plain)
         for m in range(2):
             first, second = keys[2 * m], keys[2 * m + 1]
@@ -92,8 +111,8 @@
         tail = 3 * HEAD + r * TAIL
         keyed = jnp.concatenate([paired[4 * r : 4 * r + 4], jnp.full((12, T), 9.0, F32)], axis=0)
         keyed = keyed.astype(BF16)
-        b0_out[tail + T : tail + TAIL, :] = keyed
-        b1_out[tail + T : tail + TAIL, :] = keyed
+        b_out[tail + T : tail + TAIL, :] = keyed
+        b_out[PIECE + tail + T : PIECE + tail + TAIL, :] = keyed
         for m in range(2):
             at = r * HEAD if m == 0 else tail
             even = x[r, 2 * m]
@@ -101,21 +120,27 @@
             a_out[(4 * r + 2 * m) * T : (4 * r + 2 * m + 1) * T, :] = even
             a_out[(4 * r + 2 * m + 1) * T : (4 * r + 2 * m + 2) * T, :] = odd
             even, odd = even.astype(F32), odd.astype(F32)
-            b0_out[at : at + T, :] = jnp.where(here, even, turned(odd)).astype(BF16)
-            b1_out[at : at + T, :] = jnp.where(here, turned(even), odd).astype(BF16)
+            b_out[at : at + T, :] = jnp.where(here, even, turned(odd)).astype(BF16)
+            b_out[PIECE + at : PIECE + at + T, :] = jnp.where(here, turned(even), odd).astype(BF16)
 
 
 def pack(place, cols, counts, x):
-    shapes = ((BLOCK, T), (PIECE, T), (PIECE, T), (16, T))
+    shapes = ((BLOCK, T), (2 * PIECE, T), (16, T))
     return pl.pallas_call(
         pack_kernel,
         out_shape=[jax.ShapeDtypeStruct(s, BF16) for s in shapes],
-        in_specs=[SMEM, SMEM, SMEM, VMEM],
-        out_specs=[VMEM] * 4,
+        in_specs=[SMEM, ANY, ANY, ANY],
+        out_specs=[VMEM] * 3,
+        scratch_shapes=[
+            pltpu.SMEM((3, 4), I32),
+            pltpu.SMEM((1, 3), I32),
+            pltpu.VMEM((3, 4, T, T), BF16),
+            pltpu.SemaphoreType.DMA((3,)),
+        ],
         compiler_params=params(),
         cost_estimate=cost(1 << 20, 6 << 20),
         name="pack",
-    )(place, cols, counts, x)
+    )(place, cols, counts.T, x)
 
 
 def run_all(copies):
@@ -154,7 +179,7 @@
         out_specs=[ANY] * 2,
         scratch_shapes=[pltpu.SemaphoreType.DMA((5,))],
         compiler_params=params(),
-        cost_estimate=cost(0, 4 << 20),
+        cost_estimate=cost(SORT, 4 << 20),
         name="sort_panels",
     )(place, own, g1, g2, g3, keys)
 
@@ -186,14 +211,10 @@
         low = pl.multiple_of(q // 4 * T, T)
         keys = held[q, 12 * T :, :].astype(F32)
         for i in range(3):
-            tiles = [held[q, (4 * i + t) * T : (4 * i + t + 1) * T, :].astype(F32) for t in range(4)]
+            tiles = [held[q, (4 * i + t) * T : (4 * i + t + 1) * T, :] for t in range(4)]
             for d in range(5):
-                parts = [
-                    tiles[t] * jnp.where(keys[4 * i + t : 4 * i + t + 1] == float(d - 2), 1.0, 0.0)
-                    for t in range(4)
-                ]
-                block = (parts[0] + parts[1]) + (parts[2] + parts[3])
-                out[i, q % 4, pl.ds(low, T), d * T : (d + 1) * T] = block.astype(BF16)
+                parts = [tiles[t] * chosen(keys[4 * i + t : 4 * i + t + 1], float(d - 2)) for t in range(4)]
+                out[i, q % 4, pl.ds(low, T), d * T : (d + 1) * T] = (parts[0] + parts[1]) + (parts[2] + parts[3])
         return carry
 
     lax.fori_loop(0, 8, one, 0)
@@ -210,98 +231,100 @@
         out_specs=[VMEM, VMEM],
         scratch_shapes=[pltpu.VMEM((8, BLOCK, T), BF16), pltpu.SemaphoreType.DMA((9,))],
         compiler_params=params(),
-        cost_estimate=cost(20 << 20, 8 << 20),
+        cost_estimate=cost(LEFT, 8 << 20),
         name="left_panels",
     )(place, same, r1, rm, r2)
 
 
-def edge_kernel(place, own, up, down, far_head, far_tail, to_core, to_halo, sem):
-    b, core = place[2], place[3]
+EDGE_ROWS = 2 * (HEAD + TAIL)
+
+
+def edge_copies(place, held, base, h, panel, outs, sem):
+    core = place[3]
     copies = []
-    for n, (out, start) in enumerate(((to_core, 1 - core), (to_halo, core))):
-        for k, (source, panel) in enumerate(((own, b), (up, (b + 3) % 4), (down, (b + 1) % 4), (None, (b + 2) % 4))):
-            head, tail = (source, source) if source is not None else (far_head, far_tail)
-            base = 3 * HEAD if source is not None else 0
-            copies.append(
-                pltpu.make_async_copy(
-                    head.at[pl.ds(pl.multiple_of(start * HEAD, 16), 2 * HEAD)],
-                    out.at[panel, pl.ds(0, 2 * HEAD)],
-                    sem.at[8 * n + 2 * k],
-                )
-            )
-            copies.append(
-                pltpu.make_async_copy(
-                    tail.at[pl.ds(pl.multiple_of(base + start * TAIL, 16), 2 * TAIL)],
-                    out.at[panel, pl.ds(2 * HEAD, 2 * TAIL)],
-                    sem.at[8 * n + 2 * k + 1],
-                )
-            )
-    run_all(copies)
-
-
-def edges(place, own, up, down, far_head, far_tail):
-    shape = jax.ShapeDtypeStruct((4, 2 * (HEAD + TAIL), T), BF16)
-    return pl.pallas_call(
-        edge_kernel,
+    for out, start in zip(outs, (1 - core, core)):
+        for first, size, into in ((0, HEAD, 0), (3 * HEAD, TAIL, 2 * HEAD)):
+            begin = pl.multiple_of(base + first + start * size, 16)
+            copies.append((held.at[pl.ds(begin, 2 * size)], out.at[h, panel, pl.ds(into, 2 * size)]))
+    return copies
+
+
+def edge_kernel(near, place, *refs):
+    outs, sem, b = refs[-3:-1], refs[-1], place[2]
+    moves = []
+    for h in range(2):
+        if near:
+            for source, panel in zip(refs[:3], (b, (b + 3) % 4, (b + 1) % 4)):
+                moves += edge_copies(place, source, h * PIECE, h, panel, outs, sem)
+        else:
+            moves += edge_copies(place, refs[h], 0, h, (b + 2) % 4, outs, sem)
+    run_all([pltpu.make_async_copy(source, into, sem.at[n]) for n, (source, into) in enumerate(moves)])
+
+
+def edges(flops, place, near, sources, begun=()):
+    shape = jax.ShapeDtypeStruct((2, 4, EDGE_ROWS, T), BF16)
+    count = len(sources)
+    return pl.pallas_call(
+        functools.partial(edge_kernel, near),
         out_shape=[shape, shape],
-        in_specs=[SMEM] + [ANY] * 5,
+        in_specs=[SMEM] + [ANY] * (count + len(begun)),
         out_specs=[ANY] * 2,
-        scratch_shapes=[pltpu.SemaphoreType.DMA((16,))],
-        compiler_params=params(),
-        cost_estimate=cost(0, 4 << 20),
-        name="edges",
-    )(place, own, up, down, far_head, far_tail)
+        input_output_aliases={count + 1 + n: n for n in range(len(begun))},
+        scratch_shapes=[pltpu.SemaphoreType.DMA((24,))],
+        compiler_params=params(),
+        cost_estimate=cost(flops, 4 << 20),
+        name="near_edges" if near else "far_edges",
+    )(place, *sources, *begun)
 
 
 def multiply_kernel(
-    place, own, up, down, far_head, far_tail, from_core, from_halo, left, mine, partner,
-    keep, give, heads, tails, right, sem,
+    h, place, own, up, down, far0, far1, from_core, from_halo, left, mine, partner,
+    keep, give, heads, tails, lefts, right, sem,
 ):
     b, core = place[2], place[3]
     copies = []
-    for k, (source, panel) in enumerate(((own, b), (up, (b + 3) % 4), (down, (b + 1) % 4), (None, (b + 2) % 4))):
-        head = far_head if source is None else source.at[pl.ds(0, 3 * HEAD)]
-        tail = far_tail if source is None else source.at[pl.ds(3 * HEAD, 3 * TAIL)]
-        copies.append(pltpu.make_async_copy(head, heads.at[panel, pl.ds(2 * HEAD, 3 * HEAD)], sem.at[2 * k]))
-        copies.append(pltpu.make_async_copy(tail, tails.at[panel, pl.ds(2 * TAIL, 3 * TAIL)], sem.at[2 * k + 1]))
-    for k, (source, slot) in enumerate(((from_core, 5 * (1 - core)), (from_halo, 5 * core))):
-        copies.append(
-            pltpu.make_async_copy(
-                source.at[:, pl.ds(0, 2 * HEAD)],
-                heads.at[:, pl.ds(pl.multiple_of(slot * HEAD, 16), 2 * HEAD)],
-                sem.at[8 + 2 * k],
-            )
-        )
-        copies.append(
-            pltpu.make_async_copy(
-                source.at[:, pl.ds(2 * HEAD, 2 * TAIL)],
-                tails.at[:, pl.ds(pl.multiple_of(slot * TAIL, 16), 2 * TAIL)],
-                sem.at[9 + 2 * k],
-            )
-        )
-    run_all(copies)
+
+    def load(source, into):
+        copies.append(pltpu.make_async_copy(source, into, sem.at[len(copies)]))
+
+    for source, panel in ((own, b), (up, (b + 3) % 4), (down, (b + 1) % 4), (None, (b + 2) % 4)):
+        held = (far0, far1)[h] if source is None else source
+        base = 0 if source is None else h * PIECE
+        load(held.at[pl.ds(base, 3 * HEAD)], heads.at[panel, pl.ds(2 * HEAD, 3 * HEAD)])
+        load(held.at[pl.ds(base + 3 * HEAD, 3 * TAIL)], tails.at[panel, pl.ds(2 * TAIL, 3 * TAIL)])
+    for source, slot in ((from_core, 5 * (1 - core)), (from_halo, 5 * core)):
+        at = pl.ds(pl.multiple_of(slot * HEAD, 16), 2 * HEAD)
+        load(source.at[h, :, pl.ds(0, 2 * HEAD)], heads.at[:, at])
+        at = pl.ds(pl.multiple_of(slot * TAIL, 16), 2 * TAIL)
+        load(source.at[h, :, pl.ds(2 * HEAD, 2 * TAIL)], tails.at[:, at])
+    for p in range(4):
+        load(left.at[:, p], lefts.at[p])
+    for copy in copies:
+        copy.start()
+    for copy in copies[:12]:
+        copy.wait()
     half = (lanes() >= T // 2).astype(F32)
     zero = jnp.zeros((T, T), BF16)
     sums = [None] * 3
     for p in range(4):
         for k in range(7):
             keys = tails[p, k * TAIL + T : (k + 1) * TAIL, :].astype(F32) + float(k)
-            v0 = heads[p, k * HEAD : (k + 1) * HEAD, :].astype(F32)
-            v1 = tails[p, k * TAIL : k * TAIL + T, :].astype(F32)
-            w0, w1 = turned(v0), turned(v1)
+            v0 = heads[p, k * HEAD : (k + 1) * HEAD, :]
+            v1 = tails[p, k * TAIL : k * TAIL + T, :]
+            w0, w1 = flipped(v0), flipped(v1)
             for w in range(4):
                 into = (p % 2, slice(k * T, (k + 1) * T), slice(w * T, (w + 1) * T))
                 if 2 * w + 1 < k - 2 or 2 * w > k + 2:
                     right[into] = zero
                     continue
                 target = half + float(2 * w)
-                pick = [jnp.where(keys[n : n + 1] == target, 1.0, 0.0) for n in range(4)]
-                block = (v0 * pick[0] + w0 * pick[1]) + (v1 * pick[2] + w1 * pick[3])
-                right[into] = block.astype(BF16)
+                pick = [chosen(keys[n : n + 1], target) for n in range(4)]
+                right[into] = (v0 * pick[0] + w0 * pick[1]) + (v1 * pick[2] + w1 * pick[3])
+        copies[12 + p].wait()
         for i in range(3):
             first = i // 2 * T
             part = jnp.dot(
-                left[i, p],
+                lefts[p, i],
                 right[p % 2, i * T : (i + 5) * T, first : first + 3 * T],
                 preferred_element_type=F32,
             )
@@ -322,23 +345,24 @@
                 out[i, m] = total
 
 
-def multiply(place, pieces, received, left, mine, partner):
+def multiply(flops, h, place, sources, left, mine, partner):
     shape = jax.ShapeDtypeStruct((3, 2, T, T), F32)
     return pl.pallas_call(
-        multiply_kernel,
+        functools.partial(multiply_kernel, h),
         out_shape=[shape, shape],
-        in_specs=[SMEM] + [ANY] * 7 + [VMEM] * 3,
+        in_specs=[SMEM] + [ANY] * 8 + [VMEM] * 2,
         out_specs=[VMEM, VMEM],
         scratch_shapes=[
             pltpu.VMEM((4, 7 * HEAD, T), BF16),
             pltpu.VMEM((4, 7 * TAIL, T), BF16),
+            pltpu.VMEM((4, 3, 2 * T, 5 * T), BF16),
             pltpu.VMEM((2, 7 * T, 4 * T), BF16),
-            pltpu.SemaphoreType.DMA((12,)),
+            pltpu.SemaphoreType.DMA((16,)),
         ],
         compiler_params=params(),
-        cost_estimate=cost(3 << 30, 10 << 20),
+        cost_estimate=cost(flops, 10 << 20),
         name="multiply",
-    )(place, *pieces, *received, left, mine, partner)
+    )(place, *sources, left, mine, partner)
 
 
 def finish_kernel(own0, got0, own1, got1, out):
@@ -370,27 +394,20 @@
 def body(x_tiles, tile_cols, tile_counts):
     row, col = lax.axis_index("row"), lax.axis_index("col")
     place = jnp.stack([row, row // 32, row // 8 % 4, row % 2, col // 2, col % 2]).astype(I32)
-    block, piece0, piece1, keys = pack(place, tile_cols, tile_counts, x_tiles)
-    own = (piece0, piece1)
-    up = [None, None]
-    down = [None, None]
-    far_head = [None, None]
-    far_tail = [None, None]
-    for h in range(2):
-        up[h], down[h] = send(own[h], along_z(4)), send(own[h], along_z(-4))
+    block, whole, keys = pack(place, tile_cols, tile_counts, x_tiles)
+    up, down = send(whole, along_z(4)), send(whole, along_z(-4))
     g1, g3, g2 = send(block, along_x(1)), send(block, along_x(-1)), send(block, along_x(2))
-    for h in range(2):
-        far_head[h] = send(up[h][: 3 * HEAD], along_z(4))
-        far_tail[h] = send(down[h][3 * HEAD :], along_z(-4))
     same, other = sort_panels(place, block, g1, g2, g3, keys)
+    far = (send(after(up[:PIECE], other), along_z(4)), send(after(down[PIECE:], other), along_z(-4)))
+    begun = edges(EDGE[0], place, True, (whole, up, down))
     r1, rm, r2 = send(other, along_y(1)), send(other, along_y(-1)), send(same, along_y(2))
     left, partner = left_panels(place, same, r1, rm, r2)
+    pieces = (whole, up, down, *far)
+    to_core, to_halo = edges(EDGE[1], place, False, far, begun)
+    pieces += (send(to_core, CORE), send(to_halo, HALO))
     kept, got = [], []
     for h in range(2):
-        pieces = (own[h], up[h], down[h], far_head[h], far_tail[h])
-        to_core, to_halo = edges(place, *pieces)
-        received = (send(to_core, CORE), send(to_halo, HALO))
-        keep, give = multiply(place, pieces, received, left, keys, partner)
+        keep, give = multiply(MULT[h], h, place, pieces, left, keys, partner)
         kept.append(keep)
         got.append(send(give, PLANE))
     return finish(kept[0], got[0], kept[1], got[1])

time: 170 us -> 141 us (0.83)
  the two profiles are of different devices: /device:TPU:6 before, /device:TPU:97 now
where the time goes in v2:
time: 141 us
  waiting for transfers between devices  59.2 us (42%)
  starting transfers between devices  50.8 us (36%)
  Pallas kernels  28.3 us (20%)
  local copies, waits for them, and re-layouts  2.45 us (2%)
    ppermute x14, waiting for transfers between devices, send(): return lax.ppermute(block, ('row', 'col'), pairs)  59.2 us
    ppermute x14, starting transfers between devices, send(): return lax.ppermute(block, ('row', 'col'), pairs)  50.8 us
    pallas_call x2, Pallas kernels, multiply(): pl.pallas_call(functools.partial(multiply_kernel, h), out_shape=[shape, s...  13.9 us
    pallas_call x1, Pallas kernels, left_panels(): pl.pallas_call(left_kernel, out_shape=[jax.ShapeDtypeStruct((3, 4, 2 * T,...  6.22 us
    pallas_call x2, Pallas kernels, edges(): pl.pallas_call(functools.partial(edge_kernel, near), out_shape=[shape, sh...  4.47 us
  transfers between devices with their start and end apart: 14, of which 7 were waited for; matrix products, arithmetic and copies ran while one was open for 0% of the time, Pallas kernels for 14%

profile of v2, /device:TPU:97, one launch (start us, length us, event | category | flops | bytes accessed | tf_op | source)
XLA Modules:
  0.0 140.9 jit_solution(11125716285262805512)
XLA Ops:
  0.0 0.1 stack.27.place
  0.1 0.0 copy-start
  0.1 1.0 copy-done
  1.1 0.0 copy-start.1
  1.1 0.7 copy-done.1
  1.8 0.0 copy-start.2
  1.8 0.7 copy-done.2
  2.4 1.4 pack.1
  3.8 9.8 %collective-permute-start.1 = (bf16[1632,128]{1,0:T(8,128)(2,1)S(1)}, bf16[1632,128]{1,0:T(8,128)(2,1)S(1)}, u32[]{:S(2)}, u32[]{:S(2)}) collective-permute-start(bf16[1632,128]{1,0:T(8,128)(2,1)S(1)} %get-tuple-element.22.refs_0_.own), channel_id=1, source_target_pairs={{0,192},{1,193},{2,194},{3,195},{4,196},{5,197},{6,198},{7,199},{8... | collective-permute-start | bytes 1253384 | tf_op jit(solution)/shard_map/ppermute | solution.py:56
  13.6 1.9 %collective-permute-start = (bf16[1632,128]{1,0:T(8,128)(2,1)S(1)}, bf16[1632,128]{1,0:T(8,128)(2,1)S(1)}, u32[]{:S(2)}, u32[]{:S(2)}) collective-permute-start(bf16[1632,128]{1,0:T(8,128)(2,1)S(1)} %get-tuple-element.22.refs_0_.own), channel_id=1, source_target_pairs={{0,64},{1,65},{2,66},{3,67},{4,68},{5,69},{6,70},{7,71},{8,72},{9,... | collective-permute-start | bytes 1253384 | tf_op jit(solution)/shard_map/ppermute | solution.py:56
  15.5 4.4 %collective-permute-start.4 = (bf16[1552,128]{1,0:T(8,128)(2,1)S(1)}, bf16[1552,128]{1,0:T(8,128)(2,1)S(1)}, u32[]{:S(2)}, u32[]{:S(2)}) collective-permute-start(bf16[1552,128]{1,0:T(8,128)(2,1)S(1)} %get-tuple-element.23.own), channel_id=1, source_target_pairs={{0,6},{1,7},{2,0},{3,1},{4,2},{5,3},{6,4},{7,5},{8,14},{9,15},{10,... | collective-permute-start | bytes 1191944 | tf_op jit(solution)/shard_map/ppermute | solution.py:56
  19.9 2.4 %collective-permute-start.3 = (bf16[1552,128]{1,0:T(8,128)(2,1)S(1)}, bf16[1552,128]{1,0:T(8,128)(2,1)S(1)}, u32[]{:S(2)}, u32[]{:S(2)}) collective-permute-start(bf16[1552,128]{1,0:T(8,128)(2,1)S(1)} %get-tuple-element.23.own), channel_id=1, source_target_pairs={{0,4},{1,5},{2,6},{3,7},{4,0},{5,1},{6,2},{7,3},{8,12},{9,13},{10,... | collective-permute-start | bytes 1191944 | tf_op jit(solution)/shard_map/ppermute | solution.py:56
  22.3 2.5 %collective-permute-start.2 = (bf16[1552,128]{1,0:T(8,128)(2,1)S(1)}, bf16[1552,128]{1,0:T(8,128)(2,1)S(1)}, u32[]{:S(2)}, u32[]{:S(2)}) collective-permute-start(bf16[1552,128]{1,0:T(8,128)(2,1)S(1)} %get-tuple-element.23.own), channel_id=1, source_target_pairs={{0,2},{1,3},{2,4},{3,5},{4,6},{5,7},{6,0},{7,1},{8,10},{9,11},{10,... | collective-permute-start | bytes 1191944 | tf_op jit(solution)/shard_map/ppermute | solution.py:56
  24.9 3.4 %collective-permute-done.4.g3 = bf16[1552,128]{1,0:T(8,128)(2,1)S(1)} collective-permute-done((bf16[1552,128]{1,0:T(8,128)(2,1)S(1)}, bf16[1552,128]{1,0:T(8,128)(2,1)S(1)}, u32[]{:S(2)}, u32[]{:S(2)}) %collective-permute-start.4) | collective-permute-done | bytes 397344 | tf_op jit(solution)/shard_map/ppermute | solution.py:56
  28.2 4.6 %collective-permute-done.3.g2 = bf16[1552,128]{1,0:T(8,128)(2,1)S(1)} collective-permute-done((bf16[1552,128]{1,0:T(8,128)(2,1)S(1)}, bf16[1552,128]{1,0:T(8,128)(2,1)S(1)}, u32[]{:S(2)}, u32[]{:S(2)}) %collective-permute-start.3) | collective-permute-done | bytes 397344 | tf_op jit(solution)/shard_map/ppermute | solution.py:56
  32.8 10.1 %collective-permute-done.2.g1 = bf16[1552,128]{1,0:T(8,128)(2,1)S(1)} collective-permute-done((bf16[1552,128]{1,0:T(8,128)(2,1)S(1)}, bf16[1552,128]{1,0:T(8,128)(2,1)S(1)}, u32[]{:S(2)}, u32[]{:S(2)}) %collective-permute-start.2) | collective-permute-done | bytes 397344 | tf_op jit(solution)/shard_map/ppermute | solution.py:56
  42.9 1.4 %sort_panels.1 = (bf16[3104,128]{1,0:T(8,128)(2,1)S(1)}, bf16[3120,128]{1,0:T(8,128)(2,1)S(1)}) custom-call(s32[6]{0:T(128)S(1)} %stack.27.place, bf16[1552,128]{1,0:T(8,128)(2,1)S(1)} %get-tuple-element.23.own, bf16[1552,128]{1,0:T(8,128)(2,1)S(1)} %collective-permute-done.2.g1, bf16[1552,128]{1,0:T(8,128)(2,1)S(1)} %collective-permute-done.3.g2, ...), custom_call_target="tpu_custom_call" | custom-call | bytes 4194304 | tf_op jit(solution)/shard_map/sort_panels/pallas_call | solution.py:172
  44.4 4.6 %collective-permute-start.10 = (bf16[3120,128]{1,0:T(8,128)(2,1)S(1)}, bf16[3120,128]{1,0:T(8,128)(2,1)S(1)}, u32[]{:S(2)}, u32[]{:S(2)}) collective-permute-start(bf16[3120,128]{1,0:T(8,128)(2,1)S(1)} %get-tuple-element.25), channel_id=1, source_target_pairs={{0,257},{1,256},{2,259},{3,258},{4,261},{5,260},{6,263},{7,262},{8... | collective-permute-start | bytes 2396168 | tf_op jit(solution)/shard_map/ppermute | solution.py:56
  49.0 1.9 %collective-permute-start.9 = (bf16[3120,128]{1,0:T(8,128)(2,1)S(1)}, bf16[3120,128]{1,0:T(8,128)(2,1)S(1)}, u32[]{:S(2)}, u32[]{:S(2)}) collective-permute-start(bf16[3120,128]{1,0:T(8,128)(2,1)S(1)} %get-tuple-element.25), channel_id=1, source_target_pairs={{0,256},{1,257},{2,258},{3,259},{4,260},{5,261},{6,262},{7,263},{8... | collective-permute-start | bytes 2396168 | tf_op jit(solution)/shard_map/ppermute | solution.py:56
  51.0 3.5 %collective-permute-start.11 = (bf16[3104,128]{1,0:T(8,128)(2,1)S(1)}, bf16[3104,128]{1,0:T(8,128)(2,1)S(1)}, u32[]{:S(2)}, u32[]{:S(2)}) collective-permute-start(bf16[3104,128]{1,0:T(8,128)(2,1)S(1)} %get-tuple-element.32.same), channel_id=1, source_target_pairs={{0,1},{1,0},{2,3},{3,2},{4,5},{5,4},{6,7},{7,6},{8,9},{9,8},{10,11... | collective-permute-start | bytes 2383880 | tf_op jit(solution)/shard_map/ppermute | solution.py:56
  54.5 0.0 collective-permute-done.1.refs_2_.down
  54.6 7.3 %collective-permute-start.6 = (bf16[816,128]{1,0:T(8,128)(2,1)S(1)}, bf16[816,128]{1,0:T(8,128)(2,1)S(1)}, u32[]{:S(2)}, u32[]{:S(2)}) collective-permute-start(bf16[816,128]{1,0:T(8,128)(2,1)S(1)} %slice.9), channel_id=1, source_target_pairs={{0,192},{1,193},{2,194},{3,195},{4,196},{5,197},{6,198},{7,199},{8... | collective-permute-start | bytes 626696 | tf_op jit(solution)/shard_map/ppermute | solution.py:56
  61.8 0.0 collective-permute-done.refs_1_.up
  61.9 1.9 %collective-permute-start.5 = (bf16[816,128]{1,0:T(8,128)(2,1)S(1)}, bf16[816,128]{1,0:T(8,128)(2,1)S(1)}, u32[]{:S(2)}, u32[]{:S(2)}) collective-permute-start(bf16[816,128]{1,0:T(8,128)(2,1)S(1)} %slice.8), channel_id=1, source_target_pairs={{0,64},{1,65},{2,66},{3,67},{4,68},{5,69},{6,70},{7,71},{8,72},{9,... | collective-permute-start | bytes 626696 | tf_op jit(solution)/shard_map/ppermute | solution.py:56
  63.8 3.0 %near_edges.1 = (bf16[2,4,544,128]{3,2,1,0:T(8,128)(2,1)S(1)}, bf16[2,4,544,128]{3,2,1,0:T(8,128)(2,1)S(1)}) custom-call(s32[6]{0:T(128)S(1)} %stack.27.place, bf16[1632,128]{1,0:T(8,128)(2,1)S(1)} %get-tuple-element.22.refs_0_.own, bf16[1632,128]{1,0:T(8,128)(2,1)S(1)} %collective-permute-done.refs_1_.up, ...), custom_call_target="tpu_custom_call" | custom-call | bytes 4194304 | tf_op jit(solution)/shard_map/near_edges/pallas_call | solution.py:267
  66.8 2.2 %collective-permute-done.6.refs_1_.far1 = bf16[816,128]{1,0:T(8,128)(2,1)S(1)} collective-permute-done((bf16[816,128]{1,0:T(8,128)(2,1)S(1)}, bf16[816,128]{1,0:T(8,128)(2,1)S(1)}, u32[]{:S(2)}, u32[]{:S(2)}) %collective-permute-start.6) | collective-permute-done | bytes 208928 | tf_op jit(solution)/shard_map/ppermute | solution.py:56
  69.0 18.7 %collective-permute-done.5.refs_0_.far0 = bf16[816,128]{1,0:T(8,128)(2,1)S(1)} collective-permute-done((bf16[816,128]{1,0:T(8,128)(2,1)S(1)}, bf16[816,128]{1,0:T(8,128)(2,1)S(1)}, u32[]{:S(2)}, u32[]{:S(2)}) %collective-permute-start.5) | collective-permute-done | bytes 208928 | tf_op jit(solution)/shard_map/ppermute | solution.py:56
  87.7 1.5 %far_edges.1 = (bf16[2,4,544,128]{3,2,1,0:T(8,128)(2,1)S(1)}, bf16[2,4,544,128]{3,2,1,0:T(8,128)(2,1)S(1)}) custom-call(s32[6]{0:T(128)S(1)} %stack.27.place, bf16[816,128]{1,0:T(8,128)(2,1)S(1)} %collective-permute-done.5.refs_0_.far0, bf16[816,128]{1,0:T(8,128)(2,1)S(1)} %collective-permute-done.6.refs_1_.far1, ...), custom_call_target="tpu_custom_call", output_to_operand_aliasing={{0}: (3, {}), {1}: (4, {})} | custom-call | bytes 4194304 | tf_op jit(solution)/shard_map/far_edges/pallas_call | solution.py:267
  89.2 2.9 %collective-permute-start.7 = (bf16[2,4,544,128]{3,2,1,0:T(8,128)(2,1)S(1)}, bf16[2,4,544,128]{3,2,1,0:T(8,128)(2,1)S(1)}, u32[]{:S(2)}, u32[]{:S(2)}) collective-permute-start(bf16[2,4,544,128]{3,2,1,0:T(8,128)(2,1)S(1)} %get-tuple-element.30), channel_id=1, source_target_pairs={{0,8},{1,9},{2,10},{3,11},{4,12},{5,13},{6,14},{7,15},{8,0},{9,1},... | collective-permute-start | bytes 3342344 | tf_op jit(solution)/shard_map/ppermute | solution.py:56
  92.1 1.9 %collective-permute-start.8 = (bf16[2,4,544,128]{3,2,1,0:T(8,128)(2,1)S(1)}, bf16[2,4,544,128]{3,2,1,0:T(8,128)(2,1)S(1)}, u32[]{:S(2)}, u32[]{:S(2)}) collective-permute-start(bf16[2,4,544,128]{3,2,1,0:T(8,128)(2,1)S(1)} %get-tuple-element.31), channel_id=1, source_target_pairs={{0,248},{1,249},{2,250},{3,251},{4,252},{5,253},{6,254},{7,255},{8... | collective-permute-start | bytes 3342344 | tf_op jit(solution)/shard_map/ppermute | solution.py:56
  94.0 0.0 collective-permute-done.11.r2
  94.0 0.0 collective-permute-done.10.rm
  94.0 0.0 collective-permute-done.9.r1
  94.1 6.2 %left_panels.1 = (bf16[3,4,256,640]{3,2,1,0:T(8,128)(2,1)}, bf16[16,128]{1,0:T(8,128)(2,1)S(1)}) custom-call(s32[6]{0:T(128)S(1)} %stack.27.place, bf16[3104,128]{1,0:T(8,128)(2,1)S(1)} %get-tuple-element.32.same, bf16[3120,128]{1,0:T(8,128)(2,1)S(1)} %collective-permute-done.9.r1, bf16[3120,128]{1,0:T(8,128)(2,1)S(1)} %collective-permute-done.10.rm, ...), custom_call_target="tpu_custom_call" | custom-call | flops 5699999744 | bytes 8388608 | tf_op jit(solution)/shard_map/left_panels/pallas_call | solution.py:224
  100.3 0.0 collective-permute-done.7.from_core
  100.3 9.8 %collective-permute-done.8.from_halo = bf16[2,4,544,128]{3,2,1,0:T(8,128)(2,1)S(1)} collective-permute-done((bf16[2,4,544,128]{3,2,1,0:T(8,128)(2,1)S(1)}, bf16[2,4,544,128]{3,2,1,0:T(8,128)(2,1)S(1)}, u32[]{:S(2)}, u32[]{:S(2)}) %collective-permute-start.8) | collective-permute-done | bytes 1114144 | tf_op jit(solution)/shard_map/ppermute | solution.py:56
  110.1 6.9 %multiply.3 = (f32[3,2,128,128]{3,2,1,0:T(8,128)S(1)}, f32[3,2,128,128]{3,2,1,0:T(8,128)S(1)}) custom-call(s32[6]{0:T(128)S(1)} %stack.27.place, bf16[1632,128]{1,0:T(8,128)(2,1)S(1)} %get-tuple-element.22.refs_0_.own, bf16[1632,128]{1,0:T(8,128)(2,1)S(1)} %collective-permute-done.refs_1_.up, bf16[1632,128]{1,0:T(8,128)(2,1)S(1)} %collective-permute-done.1.refs_2_.down, ...), custom_call_target="tpu_custom_call" | custom-call | flops 3221225472 | bytes 10485760 | tf_op jit(solution)/shard_map/multiply/pallas_call | solution.py:350
  117.1 3.7 %collective-permute-start.13 = (f32[3,2,128,128]{3,2,1,0:T(8,128)S(1)}, f32[3,2,128,128]{3,2,1,0:T(8,128)S(1)}, u32[]{:S(2)}, u32[]{:S(2)}) collective-permute-start(f32[3,2,128,128]{3,2,1,0:T(8,128)S(1)} %get-tuple-element.38), channel_id=1, source_target_pairs={{0,256},{1,257},{2,258},{3,259},{4,260},{5,261},{6,262},{7,263},{8... | collective-permute-start | bytes 1179656 | tf_op jit(solution)/shard_map/ppermute | solution.py:56
  120.8 6.9 %multiply.2 = (f32[3,2,128,128]{3,2,1,0:T(8,128)S(1)}, f32[3,2,128,128]{3,2,1,0:T(8,128)S(1)}) custom-call(s32[6]{0:T(128)S(1)} %stack.27.place, bf16[1632,128]{1,0:T(8,128)(2,1)S(1)} %get-tuple-element.22.refs_0_.own, bf16[1632,128]{1,0:T(8,128)(2,1)S(1)} %collective-permute-done.refs_1_.up, bf16[1632,128]{1,0:T(8,128)(2,1)S(1)} %collective-permute-done.1.refs_2_.down, ...), custom_call_target="tpu_custom_call" | custom-call | flops 3221225472 | bytes 10485760 | tf_op jit(solution)/shard_map/multiply/pallas_call | solution.py:350
  127.7 1.9 %collective-permute-start.12 = (f32[3,2,128,128]{3,2,1,0:T(8,128)S(1)}, f32[3,2,128,128]{3,2,1,0:T(8,128)S(1)}, u32[]{:S(2)}, u32[]{:S(2)}) collective-permute-start(f32[3,2,128,128]{3,2,1,0:T(8,128)S(1)} %get-tuple-element.36), channel_id=1, source_target_pairs={{0,256},{1,257},{2,258},{3,259},{4,260},{5,261},{6,262},{7,263},{8... | collective-permute-start | bytes 1179656 | tf_op jit(solution)/shard_map/ppermute | solution.py:56
  129.6 0.0 collective-permute-done.13.got1
  129.6 10.3 %collective-permute-done.12.got0 = f32[3,2,128,128]{3,2,1,0:T(8,128)S(1)} collective-permute-done((f32[3,2,128,128]{3,2,1,0:T(8,128)S(1)}, f32[3,2,128,128]{3,2,1,0:T(8,128)S(1)}, u32[]{:S(2)}, u32[]{:S(2)}) %collective-permute-start.12) | collective-permute-done | bytes 393248 | tf_op jit(solution)/shard_map/ppermute | solution.py:56
  140.0 0.9 finish.1
  (2 shorter events, 0.0 us)
Async XLA Ops:
  0.1 1.0 copy-start
  1.1 0.7 copy-start.1
  1.8 0.7 copy-start.2
  3.8 50.7 %collective-permute-start.1 = (bf16[1632,128]{1,0:T(8,128)(2,1)S(1)}, bf16[1632,128]{1,0:T(8,128)(2,1)S(1)}, u32[]{:S(2)}, u32[]{:S(2)}) collective-permute-start(bf16[1632,128]{1,0:T(8,128)(2,1)S(1)} %get-tuple-element.22.refs_0_.own), channel_id=1, source_target_pairs={{0,192},{1,193},{2,194},{3,195},{4,196},{5,197},{6,198},{7,199},{8... | collective-permute-start | bytes 1253384 | tf_op jit(solution)/shard_map/ppermute | solution.py:56
  13.6 48.3 %collective-permute-start = (bf16[1632,128]{1,0:T(8,128)(2,1)S(1)}, bf16[1632,128]{1,0:T(8,128)(2,1)S(1)}, u32[]{:S(2)}, u32[]{:S(2)}) collective-permute-start(bf16[1632,128]{1,0:T(8,128)(2,1)S(1)} %get-tuple-element.22.refs_0_.own), channel_id=1, source_target_pairs={{0,64},{1,65},{2,66},{3,67},{4,68},{5,69},{6,70},{7,71},{8,72},{9,... | collective-permute-start | bytes 1253384 | tf_op jit(solution)/shard_map/ppermute | solution.py:56
  15.5 12.7 %collective-permute-start.4 = (bf16[1552,128]{1,0:T(8,128)(2,1)S(1)}, bf16[1552,128]{1,0:T(8,128)(2,1)S(1)}, u32[]{:S(2)}, u32[]{:S(2)}) collective-permute-start(bf16[1552,128]{1,0:T(8,128)(2,1)S(1)} %get-tuple-element.23.own), channel_id=1, source_target_pairs={{0,6},{1,7},{2,0},{3,1},{4,2},{5,3},{6,4},{7,5},{8,14},{9,15},{10,... | collective-permute-start | bytes 1191944 | tf_op jit(solution)/shard_map/ppermute | solution.py:56
  19.9 12.9 %collective-permute-start.3 = (bf16[1552,128]{1,0:T(8,128)(2,1)S(1)}, bf16[1552,128]{1,0:T(8,128)(2,1)S(1)}, u32[]{:S(2)}, u32[]{:S(2)}) collective-permute-start(bf16[1552,128]{1,0:T(8,128)(2,1)S(1)} %get-tuple-element.23.own), channel_id=1, source_target_pairs={{0,4},{1,5},{2,6},{3,7},{4,0},{5,1},{6,2},{7,3},{8,12},{9,13},{10,... | collective-permute-start | bytes 1191944 | tf_op jit(solution)/shard_map/ppermute | solution.py:56
  22.3 20.6 %collective-permute-start.2 = (bf16[1552,128]{1,0:T(8,128)(2,1)S(1)}, bf16[1552,128]{1,0:T(8,128)(2,1)S(1)}, u32[]{:S(2)}, u32[]{:S(2)}) collective-permute-start(bf16[1552,128]{1,0:T(8,128)(2,1)S(1)} %get-tuple-element.23.own), channel_id=1, source_target_pairs={{0,2},{1,3},{2,4},{3,5},{4,6},{5,7},{6,0},{7,1},{8,10},{9,11},{10,... | collective-permute-start | bytes 1191944 | tf_op jit(solution)/shard_map/ppermute | solution.py:56
  44.4 49.6 %collective-permute-start.10 = (bf16[3120,128]{1,0:T(8,128)(2,1)S(1)}, bf16[3120,128]{1,0:T(8,128)(2,1)S(1)}, u32[]{:S(2)}, u32[]{:S(2)}) collective-permute-start(bf16[3120,128]{1,0:T(8,128)(2,1)S(1)} %get-tuple-element.25), channel_id=1, source_target_pairs={{0,257},{1,256},{2,259},{3,258},{4,261},{5,260},{6,263},{7,262},{8... | collective-permute-start | bytes 2396168 | tf_op jit(solution)/shard_map/ppermute | solution.py:56
  49.0 45.0 %collective-permute-start.9 = (bf16[3120,128]{1,0:T(8,128)(2,1)S(1)}, bf16[3120,128]{1,0:T(8,128)(2,1)S(1)}, u32[]{:S(2)}, u32[]{:S(2)}) collective-permute-start(bf16[3120,128]{1,0:T(8,128)(2,1)S(1)} %get-tuple-element.25), channel_id=1, source_target_pairs={{0,256},{1,257},{2,258},{3,259},{4,260},{5,261},{6,262},{7,263},{8... | collective-permute-start | bytes 2396168 | tf_op jit(solution)/shard_map/ppermute | solution.py:56
  51.0 43.1 %collective-permute-start.11 = (bf16[3104,128]{1,0:T(8,128)(2,1)S(1)}, bf16[3104,128]{1,0:T(8,128)(2,1)S(1)}, u32[]{:S(2)}, u32[]{:S(2)}) collective-permute-start(bf16[3104,128]{1,0:T(8,128)(2,1)S(1)} %get-tuple-element.32.same), channel_id=1, source_target_pairs={{0,1},{1,0},{2,3},{3,2},{4,5},{5,4},{6,7},{7,6},{8,9},{9,8},{10,11... | collective-permute-start | bytes 2383880 | tf_op jit(solution)/shard_map/ppermute | solution.py:56
  54.6 14.4 %collective-permute-start.6 = (bf16[816,128]{1,0:T(8,128)(2,1)S(1)}, bf16[816,128]{1,0:T(8,128)(2,1)S(1)}, u32[]{:S(2)}, u32[]{:S(2)}) collective-permute-start(bf16[816,128]{1,0:T(8,128)(2,1)S(1)} %slice.9), channel_id=1, source_target_pairs={{0,192},{1,193},{2,194},{3,195},{4,196},{5,197},{6,198},{7,199},{8... | collective-permute-start | bytes 626696 | tf_op jit(solution)/shard_map/ppermute | solution.py:56
  61.9 25.8 %collective-permute-start.5 = (bf16[816,128]{1,0:T(8,128)(2,1)S(1)}, bf16[816,128]{1,0:T(8,128)(2,1)S(1)}, u32[]{:S(2)}, u32[]{:S(2)}) collective-permute-start(bf16[816,128]{1,0:T(8,128)(2,1)S(1)} %slice.8), channel_id=1, source_target_pairs={{0,64},{1,65},{2,66},{3,67},{4,68},{5,69},{6,70},{7,71},{8,72},{9,... | collective-permute-start | bytes 626696 | tf_op jit(solution)/shard_map/ppermute | solution.py:56
  89.2 11.1 %collective-permute-start.7 = (bf16[2,4,544,128]{3,2,1,0:T(8,128)(2,1)S(1)}, bf16[2,4,544,128]{3,2,1,0:T(8,128)(2,1)S(1)}, u32[]{:S(2)}, u32[]{:S(2)}) collective-permute-start(bf16[2,4,544,128]{3,2,1,0:T(8,128)(2,1)S(1)} %get-tuple-element.30), channel_id=1, source_target_pairs={{0,8},{1,9},{2,10},{3,11},{4,12},{5,13},{6,14},{7,15},{8,0},{9,1},... | collective-permute-start | bytes 3342344 | tf_op jit(solution)/shard_map/ppermute | solution.py:56
  92.1 18.0 %collective-permute-start.8 = (bf16[2,4,544,128]{3,2,1,0:T(8,128)(2,1)S(1)}, bf16[2,4,544,128]{3,2,1,0:T(8,128)(2,1)S(1)}, u32[]{:S(2)}, u32[]{:S(2)}) collective-permute-start(bf16[2,4,544,128]{3,2,1,0:T(8,128)(2,1)S(1)} %get-tuple-element.31), channel_id=1, source_target_pairs={{0,248},{1,249},{2,250},{3,251},{4,252},{5,253},{6,254},{7,255},{8... | collective-permute-start | bytes 3342344 | tf_op jit(solution)/shard_map/ppermute | solution.py:56
  117.1 12.6 %collective-permute-start.13 = (f32[3,2,128,128]{3,2,1,0:T(8,128)S(1)}, f32[3,2,128,128]{3,2,1,0:T(8,128)S(1)}, u32[]{:S(2)}, u32[]{:S(2)}) collective-permute-start(f32[3,2,128,128]{3,2,1,0:T(8,128)S(1)} %get-tuple-element.38), channel_id=1, source_target_pairs={{0,256},{1,257},{2,258},{3,259},{4,260},{5,261},{6,262},{7,263},{8... | collective-permute-start | bytes 1179656 | tf_op jit(solution)/shard_map/ppermute | solution.py:56
  127.7 12.3 %collective-permute-start.12 = (f32[3,2,128,128]{3,2,1,0:T(8,128)S(1)}, f32[3,2,128,128]{3,2,1,0:T(8,128)S(1)}, u32[]{:S(2)}, u32[]{:S(2)}) collective-permute-start(f32[3,2,128,128]{3,2,1,0:T(8,128)S(1)} %get-tuple-element.36), channel_id=1, source_target_pairs={{0,256},{1,257},{2,258},{3,259},{4,260},{5,261},{6,262},{7,263},{8... | collective-permute-start | bytes 1179656 | tf_op jit(solution)/shard_map/ppermute | solution.py:56

commit v3 on v2

v3 whole, which is shorter than its diff:
```python
import functools

import jax
import jax.numpy as jnp
from jax import lax
from jax.experimental import pallas as pl
from jax.experimental.pallas import tpu as pltpu
from jax.sharding import PartitionSpec as P

BF16, F32, I32 = jnp.bfloat16, jnp.float32, jnp.int32
T = 128
EDGE = (0, 0)
MULT = (3 << 30, 3 << 30)
LEFT = 5700000000
SORT = 0
LIMIT = 48 << 20
BLOCK = 12 * T + 16
HEAD, TAIL = T, T + 16
PIECE = 3 * (HEAD + TAIL)
VMEM = pl.BlockSpec(memory_space=pltpu.VMEM)
SMEM = pl.BlockSpec(memory_space=pltpu.SMEM)


def routes(move):
    pairs = []
    for row in range(64):
        for col in range(8):
            a, z, k, x, h = move(row // 32, row // 2 % 16, row % 2, col // 2, col % 2)
            pairs.append((row * 8 + col, (a * 32 + z % 16 * 2 + k) * 8 + x % 4 * 2 + h))
    return pairs


def along_z(n):
    return routes(lambda a, z, k, x, h: (a, z + n, k, x, h))


def along_x(n):
    return routes(lambda a, z, k, x, h: (a, z, k, x + n, h))


def along_y(n):
    def move(a, z, k, x, h):
        y = (2 * h + a + n) % 4
        return y % 2, z, k, x, y // 2

    return routes(move)


CORE = routes(lambda a, z, k, x, h: (a, z, 1 - k, x, h))
HALO = routes(lambda a, z, k, x, h: (a, z + 2 * k - 1, 1 - k, x, h))
PLANE = routes(lambda a, z, k, x, h: (1 - a, z, k, x, h))


def send(block, pairs):
    return lax.ppermute(block, ("row", "col"), pairs)


def params():
    return pltpu.CompilerParams(vmem_limit_bytes=LIMIT)


def cost(flops, moved):
    return pl.CostEstimate(flops=flops, bytes_accessed=moved, transcendentals=0)


def lanes():
    return lax.broadcasted_iota(I32, (1, T), 1)


def flipped(v):
    return pltpu.roll(v, T // 2, 1)


def chosen(keys, target):
    return jnp.where(keys == target, 1.0, 0.0).astype(BF16)


def turned(v):
    return pltpu.roll(v, T // 2, 1)


def pack_kernel(place, cols, counts, x, a_out, b_out, k_out):
    row = lax.broadcasted_iota(I32, (16, T), 0)
    left = lax.broadcasted_iota(I32, (16, T), 1) < T // 2
    plain = jnp.full((16, T), 9, I32)
    paired = jnp.full((16, T), 9, I32)
    for r in range(3):
        keys = []
        for t in range(4):
            away = (cols[r, t] - (place[0] * 3 + r) + 240) % 24
            away = jnp.where(away > 12, away - 24, away)
            keys.append(jnp.where(t < counts[0, r], away, 9))
            plain = jnp.where(row == r * 4 + t, keys[t], plain)
        for m in range(2):
            first, second = keys[2 * m], keys[2 * m + 1]
            paired = jnp.where(row == r * 4 + 2 * m, jnp.where(left, first, second), paired)
            paired = jnp.where(row == r * 4 + 2 * m + 1, jnp.where(left, second, first), paired)
    a_out[12 * T :, :] = plain.astype(F32).astype(BF16)
    paired = paired.astype(F32)
    k_out[...] = paired.astype(BF16)
    here = lanes() < T // 2
    for r in range(3):
        tail = 3 * HEAD + r * TAIL
        keyed = jnp.concatenate([paired[4 * r : 4 * r + 4], jnp.full((12, T), 9.0, F32)], axis=0)
        keyed = keyed.astype(BF16)
        b_out[tail + T : tail + TAIL, :] = keyed
        b_out[PIECE + tail + T : PIECE + tail + TAIL, :] = keyed
        for m in range(2):
            at = r * HEAD if m == 0 else tail
            even = x[r, 2 * m]
            odd = x[r, 2 * m + 1]
            a_out[(4 * r + 2 * m) * T : (4 * r + 2 * m + 1) * T, :] = even
            a_out[(4 * r + 2 * m + 1) * T : (4 * r + 2 * m + 2) * T, :] = odd
            even, odd = even.astype(F32), odd.astype(F32)
            b_out[at : at + T, :] = jnp.where(here, even, turned(odd)).astype(BF16)
            b_out[PIECE + at : PIECE + at + T, :] = jnp.where(here, turned(even), odd).astype(BF16)


def pack(place, cols, counts, x):
    shapes = ((BLOCK, T), (2 * PIECE, T), (16, T))
    return pl.pallas_call(
        pack_kernel,
        out_shape=[jax.ShapeDtypeStruct(s, BF16) for s in shapes],
        in_specs=[SMEM, SMEM, SMEM, VMEM],
        out_specs=[VMEM] * 3,
        compiler_params=params(),
        cost_estimate=cost(1 << 20, 6 << 20),
        name="pack",
    )(place, cols, counts.T, x)


def sort_kernel(place, own, g1, g2, g3, keys, same, other):
    a, x = place[1], place[4]
    other[2 * BLOCK :, :] = keys[...]
    for k, source in enumerate((own, g1, g2, g3)):
        panel = (x - k + 4) % 4
        at = pl.multiple_of(panel % 2 * BLOCK, 16)

        @pl.when(panel // 2 == a)
        def _(source=source, at=at):
            same[pl.ds(at, BLOCK), :] = source[...]

        @pl.when(panel // 2 != a)
        def _(source=source, at=at):
            other[pl.ds(at, BLOCK), :] = source[...]


def sort_panels(place, own, g1, g2, g3, keys):
    return pl.pallas_call(
        sort_kernel,
        out_shape=[
            jax.ShapeDtypeStruct((2 * BLOCK, T), BF16),
            jax.ShapeDtypeStruct((2 * BLOCK + 16, T), BF16),
        ],
        in_specs=[SMEM] + [VMEM] * 5,
        out_specs=[VMEM] * 2,
        compiler_params=params(),
        cost_estimate=cost(SORT, 4 << 20),
        name="sort_panels",
    )(place, own, g1, g2, g3, keys)


def left_kernel(place, same, r1, rm, r2, out, partner):
    a, h = place[1], place[5]
    near = jnp.where(a == 1, h, 1 - h)
    keys = slice(2 * BLOCK, 2 * BLOCK + 16)
    partner[...] = jnp.where(a == 1, r1[keys, :].astype(F32), rm[keys, :].astype(F32)).astype(BF16)
    for n, (source, half) in enumerate(((same, h), (r2, 1 - h), (r1, near), (rm, 1 - near))):
        rows = slice(n // 2 * T, (n // 2 + 1) * T)

        def one(e, carry, source=source, half=half, rows=rows):
            base = pl.multiple_of(e * BLOCK, 16)
            keys = source[pl.ds(base + 12 * T, 16), :].astype(F32)
            for i in range(3):
                tiles = [source[pl.ds(base + (4 * i + t) * T, T), :] for t in range(4)]
                for d in range(5):
                    parts = [tiles[t] * chosen(keys[4 * i + t : 4 * i + t + 1], float(d - 2)) for t in range(4)]
                    block = (parts[0] + parts[1]) + (parts[2] + parts[3])
                    out[i, 2 * e + half, rows, d * T : (d + 1) * T] = block
            return carry

        lax.fori_loop(0, 2, one, 0)


def left_panels(place, same, r1, rm, r2):
    return pl.pallas_call(
        left_kernel,
        out_shape=[
            jax.ShapeDtypeStruct((3, 4, 2 * T, 5 * T), BF16),
            jax.ShapeDtypeStruct((16, T), BF16),
        ],
        in_specs=[SMEM] + [VMEM] * 4,
        out_specs=[VMEM, VMEM],
        compiler_params=params(),
        cost_estimate=cost(LEFT, 8 << 20),
        name="left_panels",
    )(place, same, r1, rm, r2)


EDGE_ROWS = 2 * (HEAD + TAIL)


def edge_kernel(place, own, up, down, far0, far1, to_core, to_halo):
    b, core = place[2], place[3]
    for out, start in ((to_core, 1 - core), (to_halo, core)):
        for source, panel in ((own, b), (up, (b + 3) % 4), (down, (b + 1) % 4), (None, (b + 2) % 4)):
            for h in range(2):
                held = (far0, far1)[h] if source is None else source
                base = 0 if source is None else h * PIECE
                for first, size, into in ((0, HEAD, 0), (3 * HEAD, TAIL, 2 * HEAD)):
                    begin = pl.multiple_of(base + first + start * size, 16)
                    out[h, panel, into : into + 2 * size, :] = held[pl.ds(begin, 2 * size), :]


def edges(flops, place, *sources):
    shape = jax.ShapeDtypeStruct((2, 4, EDGE_ROWS, T), BF16)
    return pl.pallas_call(
        edge_kernel,
        out_shape=[shape, shape],
        in_specs=[SMEM] + [VMEM] * 5,
        out_specs=[VMEM] * 2,
        compiler_params=params(),
        cost_estimate=cost(flops, 4 << 20),
        name="edges",
    )(place, *sources)


def multiply_kernel(
    h, place, own, up, down, far0, far1, from_core, from_halo, left, mine, partner, keep, give, right
):
    b, core = place[2], place[3]
    half = (lanes() >= T // 2).astype(F32)
    zero = jnp.zeros((T, T), BF16)
    sums = [None] * 3
    for p, (source, shift) in enumerate(((own, 0), (up, 3), (down, 1), (None, 2))):
        panel = (b + shift) % 4
        held = (far0, far1)[h] if source is None else source
        base = 0 if source is None else h * PIECE

        def edge(first, size, low):
            rows = slice(first, first + size)
            above, below = (from_halo, from_core) if low else (from_core, from_halo)
            return jnp.where(core == 0, above[h, panel, rows, :], below[h, panel, rows, :])

        for k in range(7):
            if 2 <= k < 5:
                head = base + (k - 2) * HEAD
                tail = base + 3 * HEAD + (k - 2) * TAIL
                v0 = held[head : head + T, :]
                v1 = held[tail : tail + T, :]
                keys = held[tail + T : tail + TAIL, :]
            else:
                row, low = (k, True) if k < 2 else (k - 5, False)
                v0 = edge(row * HEAD, T, low)
                v1 = edge(2 * HEAD + row * TAIL, T, low)
                keys = edge(2 * HEAD + row * TAIL + T, 16, low)
            keys = keys.astype(F32) + float(k)
            w0, w1 = flipped(v0), flipped(v1)
            for w in range(4):
                into = (p % 2, slice(k * T, (k + 1) * T), slice(w * T, (w + 1) * T))
                if 2 * w + 1 < k - 2 or 2 * w > k + 2:
                    if p < 2:
                        right[into] = zero
                    continue
                target = half + float(2 * w)
                pick = [chosen(keys[n : n + 1], target) for n in range(4)]
                right[into] = (v0 * pick[0] + w0 * pick[1]) + (v1 * pick[2] + w1 * pick[3])
        for i in range(3):
            first = i // 2 * T
            part = jnp.dot(
                left[i, panel],
                right[p % 2, i * T : (i + 5) * T, first : first + 3 * T],
                preferred_element_type=F32,
            )
            sums[i] = part if sums[i] is None else sums[i] + part
    for i in range(3):
        for side, (out, source) in enumerate(((keep, mine), (give, partner))):
            keys = source[...].astype(F32)[4 * i : 4 * i + 4] + float(i + 2)
            for m in range(2):
                total = None
                for w in range(3):
                    v = sums[i][side * T : (side + 1) * T, w * T : (w + 1) * T]
                    target = half + float(2 * (w + i // 2))
                    swap = (1.0 - half) + float(2 * (w + i // 2))
                    key = keys[2 * m : 2 * m + 1]
                    part = v * jnp.where(key == target, 1.0, 0.0)
                    part = part + turned(v) * jnp.where(key == swap, 1.0, 0.0)
                    total = part if total is None else total + part
                out[i, m] = total


def multiply(flops, h, place, sources, left, mine, partner):
    shape = jax.ShapeDtypeStruct((3, 2, T, T), F32)
    return pl.pallas_call(
        functools.partial(multiply_kernel, h),
        out_shape=[shape, shape],
        in_specs=[SMEM] + [VMEM] * 10,
        out_specs=[VMEM, VMEM],
        scratch_shapes=[pltpu.VMEM((2, 7 * T, 4 * T), BF16)],
        compiler_params=params(),
        cost_estimate=cost(flops, 10 << 20),
        name="multiply",
    )(place, *sources, left, mine, partner)


def finish_kernel(own0, got0, own1, got1, out):
    here = lanes() < T // 2
    for i in range(3):
        for m in range(2):
            low = own0[i, m] + got0[i, m]
            high = own1[i, m] + got1[i, m]
            out[i, 2 * m] = jnp.where(here, low, turned(high)).astype(BF16)
            out[i, 2 * m + 1] = jnp.where(here, turned(low), high).astype(BF16)


def finish(own0, got0, own1, got1):
    return pl.pallas_call(
        finish_kernel,
        out_shape=jax.ShapeDtypeStruct((3, 4, T, T), BF16),
        in_specs=[VMEM] * 4,
        out_specs=VMEM,
        compiler_params=params(),
        cost_estimate=cost(1 << 20, 2 << 20),
        name="finish",
    )(own0, got0, own1, got1)


def after(value, *others):
    return lax.optimization_barrier((value,) + others)[0]


def body(x_tiles, tile_cols, tile_counts):
    row, col = lax.axis_index("row"), lax.axis_index("col")
    place = jnp.stack([row, row // 32, row // 8 % 4, row % 2, col // 2, col % 2]).astype(I32)
    block, whole, keys = pack(place, tile_cols, tile_counts, x_tiles)
    up, down = send(whole, along_z(4)), send(whole, along_z(-4))
    g1, g3, g2 = send(block, along_x(1)), send(block, along_x(-1)), send(block, along_x(2))
    same, other = sort_panels(place, block, g1, g2, g3, keys)
    far = (send(after(up[:PIECE], other), along_z(4)), send(after(down[PIECE:], other), along_z(-4)))
    r1, rm, r2 = send(other, along_y(1)), send(other, along_y(-1)), send(same, along_y(2))
    left, partner = left_panels(place, same, r1, rm, r2)
    pieces = (whole, up, down, *far)
    to_core, to_halo = edges(EDGE[0], place, *pieces)
    pieces += (send(to_core, CORE), send(to_halo, HALO))
    kept, got = [], []
    for h in range(2):
        keep, give = multiply(MULT[h], h, place, pieces, left, keys, partner)
        kept.append(keep)
        got.append(send(give, PLANE))
    return finish(kept[0], got[0], kept[1], got[1])


def solution(mesh):
    placed = (P("row", "col", None, None), P("row", "col"), P("row", "col"))
    return jax.shard_map(
        body, mesh=mesh, in_specs=placed, out_specs=P("row", "col", None, None), check_vma=False
    )
```

time: 141 us -> 136 us (0.965)
  the two profiles are of different devices: /device:TPU:97 before, /device:TPU:6 now
where the time goes in v3:
time: 136 us; the launch traced here: 133 us
  starting transfers between devices  63.2 us (46%)
  waiting for transfers between devices  48 us (35%)
  Pallas kernels  19.3 us (14%)
  local copies, waits for them, and re-layouts  2.45 us (2%)
    ppermute x14, starting transfers between devices, send(): return lax.ppermute(block, ('row', 'col'), pairs)  63.2 us
    ppermute x14, waiting for transfers between devices, send(): return lax.ppermute(block, ('row', 'col'), pairs)  48 us
    pallas_call x2, Pallas kernels, multiply(): pl.pallas_call(functools.partial(multiply_kernel, h), out_shape=[shape, s...  11.5 us
    pallas_call x1, Pallas kernels, left_panels(): pl.pallas_call(left_kernel, out_shape=[jax.ShapeDtypeStruct((3, 4, 2 * T,...  4.58 us
  transfers between devices with their start and end apart: 14, of which 7 were waited for; matrix products, arithmetic and copies ran while one was open for 0% of the time, Pallas kernels for 9%

profile of v3, /device:TPU:6, one launch (start us, length us, event | category | flops | bytes accessed | tf_op | source)
XLA Modules:
  0.0 133.0 jit_solution(782044198319056858)
XLA Ops:
  0.0 0.1 stack.27.place
  0.1 0.0 copy-start
  0.1 1.0 copy-done
  1.1 0.0 copy-start.1
  1.1 0.7 copy-done.1
  1.8 0.0 copy-start.2
  1.8 0.7 copy-done.2
  2.4 0.8 pack.1
  3.3 12.7 %collective-permute-start.1 = (bf16[1632,128]{1,0:T(8,128)(2,1)S(1)}, bf16[1632,128]{1,0:T(8,128)(2,1)S(1)}, u32[]{:S(2)}, u32[]{:S(2)}) collective-permute-start(bf16[1632,128]{1,0:T(8,128)(2,1)S(1)} %get-tuple-element.20.own), channel_id=1, source_target_pairs={{0,192},{1,193},{2,194},{3,195},{4,196},{5,197},{6,198},{7,199},{8... | collective-permute-start | bytes 1253384 | tf_op jit(solution)/shard_map/ppermute | solution.py:55
  16.0 1.9 %collective-permute-start = (bf16[1632,128]{1,0:T(8,128)(2,1)S(1)}, bf16[1632,128]{1,0:T(8,128)(2,1)S(1)}, u32[]{:S(2)}, u32[]{:S(2)}) collective-permute-start(bf16[1632,128]{1,0:T(8,128)(2,1)S(1)} %get-tuple-element.20.own), channel_id=1, source_target_pairs={{0,64},{1,65},{2,66},{3,67},{4,68},{5,69},{6,70},{7,71},{8,72},{9,... | collective-permute-start | bytes 1253384 | tf_op jit(solution)/shard_map/ppermute | solution.py:55
  17.9 2.9 %collective-permute-start.2 = (bf16[1552,128]{1,0:T(8,128)(2,1)S(1)}, bf16[1552,128]{1,0:T(8,128)(2,1)S(1)}, u32[]{:S(2)}, u32[]{:S(2)}) collective-permute-start(bf16[1552,128]{1,0:T(8,128)(2,1)S(1)} %get-tuple-element.21.own), channel_id=1, source_target_pairs={{0,2},{1,3},{2,4},{3,5},{4,6},{5,7},{6,0},{7,1},{8,10},{9,11},{10,... | collective-permute-start | bytes 1191944 | tf_op jit(solution)/shard_map/ppermute | solution.py:55
  20.8 3.9 %collective-permute-start.3 = (bf16[1552,128]{1,0:T(8,128)(2,1)S(1)}, bf16[1552,128]{1,0:T(8,128)(2,1)S(1)}, u32[]{:S(2)}, u32[]{:S(2)}) collective-permute-start(bf16[1552,128]{1,0:T(8,128)(2,1)S(1)} %get-tuple-element.21.own), channel_id=1, source_target_pairs={{0,4},{1,5},{2,6},{3,7},{4,0},{5,1},{6,2},{7,3},{8,12},{9,13},{10,... | collective-permute-start | bytes 1191944 | tf_op jit(solution)/shard_map/ppermute | solution.py:55
  24.7 1.9 %collective-permute-start.4 = (bf16[1552,128]{1,0:T(8,128)(2,1)S(1)}, bf16[1552,128]{1,0:T(8,128)(2,1)S(1)}, u32[]{:S(2)}, u32[]{:S(2)}) collective-permute-start(bf16[1552,128]{1,0:T(8,128)(2,1)S(1)} %get-tuple-element.21.own), channel_id=1, source_target_pairs={{0,6},{1,7},{2,0},{3,1},{4,2},{5,3},{6,4},{7,5},{8,14},{9,15},{10,... | collective-permute-start | bytes 1191944 | tf_op jit(solution)/shard_map/ppermute | solution.py:55
  26.6 5.4 %collective-permute-done.2.g1 = bf16[1552,128]{1,0:T(8,128)(2,1)S(1)} collective-permute-done((bf16[1552,128]{1,0:T(8,128)(2,1)S(1)}, bf16[1552,128]{1,0:T(8,128)(2,1)S(1)}, u32[]{:S(2)}, u32[]{:S(2)}) %collective-permute-start.2) | collective-permute-done | bytes 397344 | tf_op jit(solution)/shard_map/ppermute | solution.py:55
  31.9 4.4 %collective-permute-done.3.g2 = bf16[1552,128]{1,0:T(8,128)(2,1)S(1)} collective-permute-done((bf16[1552,128]{1,0:T(8,128)(2,1)S(1)}, bf16[1552,128]{1,0:T(8,128)(2,1)S(1)}, u32[]{:S(2)}, u32[]{:S(2)}) %collective-permute-start.3) | collective-permute-done | bytes 397344 | tf_op jit(solution)/shard_map/ppermute | solution.py:55
  36.4 6.2 %collective-permute-done.4.g3 = bf16[1552,128]{1,0:T(8,128)(2,1)S(1)} collective-permute-done((bf16[1552,128]{1,0:T(8,128)(2,1)S(1)}, bf16[1552,128]{1,0:T(8,128)(2,1)S(1)}, u32[]{:S(2)}, u32[]{:S(2)}) %collective-permute-start.4) | collective-permute-done | bytes 397344 | tf_op jit(solution)/shard_map/ppermute | solution.py:55
  42.6 0.7 sort_panels.1
  43.3 4.9 %collective-permute-start.10 = (bf16[3120,128]{1,0:T(8,128)(2,1)S(1)}, bf16[3120,128]{1,0:T(8,128)(2,1)S(1)}, u32[]{:S(2)}, u32[]{:S(2)}) collective-permute-start(bf16[3120,128]{1,0:T(8,128)(2,1)S(1)} %get-tuple-element.23), channel_id=1, source_target_pairs={{0,257},{1,256},{2,259},{3,258},{4,261},{5,260},{6,263},{7,262},{8... | collective-permute-start | bytes 2396168 | tf_op jit(solution)/shard_map/ppermute | solution.py:55
  48.3 1.9 %collective-permute-start.9 = (bf16[3120,128]{1,0:T(8,128)(2,1)S(1)}, bf16[3120,128]{1,0:T(8,128)(2,1)S(1)}, u32[]{:S(2)}, u32[]{:S(2)}) collective-permute-start(bf16[3120,128]{1,0:T(8,128)(2,1)S(1)} %get-tuple-element.23), channel_id=1, source_target_pairs={{0,256},{1,257},{2,258},{3,259},{4,260},{5,261},{6,262},{7,263},{8... | collective-permute-start | bytes 2396168 | tf_op jit(solution)/shard_map/ppermute | solution.py:55
  50.2 4.1 %collective-permute-start.11 = (bf16[3104,128]{1,0:T(8,128)(2,1)S(1)}, bf16[3104,128]{1,0:T(8,128)(2,1)S(1)}, u32[]{:S(2)}, u32[]{:S(2)}) collective-permute-start(bf16[3104,128]{1,0:T(8,128)(2,1)S(1)} %get-tuple-element.28.same), channel_id=1, source_target_pairs={{0,1},{1,0},{2,3},{3,2},{4,5},{5,4},{6,7},{7,6},{8,9},{9,8},{10,11... | collective-permute-start | bytes 2383880 | tf_op jit(solution)/shard_map/ppermute | solution.py:55
  54.3 0.0 collective-permute-done.1.down
  54.3 7.5 %collective-permute-start.6 = (bf16[816,128]{1,0:T(8,128)(2,1)S(1)}, bf16[816,128]{1,0:T(8,128)(2,1)S(1)}, u32[]{:S(2)}, u32[]{:S(2)}) collective-permute-start(bf16[816,128]{1,0:T(8,128)(2,1)S(1)} %slice.9), channel_id=1, source_target_pairs={{0,192},{1,193},{2,194},{3,195},{4,196},{5,197},{6,198},{7,199},{8... | collective-permute-start | bytes 626696 | tf_op jit(solution)/shard_map/ppermute | solution.py:55
  61.9 0.0 collective-permute-done.up
  61.9 2.2 %collective-permute-start.5 = (bf16[816,128]{1,0:T(8,128)(2,1)S(1)}, bf16[816,128]{1,0:T(8,128)(2,1)S(1)}, u32[]{:S(2)}, u32[]{:S(2)}) collective-permute-start(bf16[816,128]{1,0:T(8,128)(2,1)S(1)} %slice.8), channel_id=1, source_target_pairs={{0,64},{1,65},{2,66},{3,67},{4,68},{5,69},{6,70},{7,71},{8,72},{9,... | collective-permute-start | bytes 626696 | tf_op jit(solution)/shard_map/ppermute | solution.py:55
  64.1 15.8 %collective-permute-done.6.far1 = bf16[816,128]{1,0:T(8,128)(2,1)S(1)} collective-permute-done((bf16[816,128]{1,0:T(8,128)(2,1)S(1)}, bf16[816,128]{1,0:T(8,128)(2,1)S(1)}, u32[]{:S(2)}, u32[]{:S(2)}) %collective-permute-start.6) | collective-permute-done | bytes 208928 | tf_op jit(solution)/shard_map/ppermute | solution.py:55
  79.9 0.0 collective-permute-done.5.far0
  79.9 0.7 edges.1
  80.6 1.9 %collective-permute-start.7 = (bf16[2,4,544,128]{3,2,1,0:T(8,128)(2,1)S(1)}, bf16[2,4,544,128]{3,2,1,0:T(8,128)(2,1)S(1)}, u32[]{:S(2)}, u32[]{:S(2)}) collective-permute-start(bf16[2,4,544,128]{3,2,1,0:T(8,128)(2,1)S(1)} %get-tuple-element.26), channel_id=1, source_target_pairs={{0,8},{1,9},{2,10},{3,11},{4,12},{5,13},{6,14},{7,15},{8,0},{9,1},... | collective-permute-start | bytes 3342344 | tf_op jit(solution)/shard_map/ppermute | solution.py:55
  82.5 11.4 %collective-permute-start.8 = (bf16[2,4,544,128]{3,2,1,0:T(8,128)(2,1)S(1)}, bf16[2,4,544,128]{3,2,1,0:T(8,128)(2,1)S(1)}, u32[]{:S(2)}, u32[]{:S(2)}) collective-permute-start(bf16[2,4,544,128]{3,2,1,0:T(8,128)(2,1)S(1)} %get-tuple-element.27), channel_id=1, source_target_pairs={{0,248},{1,249},{2,250},{3,251},{4,252},{5,253},{6,254},{7,255},{8... | collective-permute-start | bytes 3342344 | tf_op jit(solution)/shard_map/ppermute | solution.py:55
  94.0 0.0 collective-permute-done.11.r2
  94.0 0.0 collective-permute-done.10.rm
  94.0 0.0 collective-permute-done.9.r1
  94.0 4.6 %left_panels.1 = (bf16[3,4,256,640]{3,2,1,0:T(8,128)(2,1)}, bf16[16,128]{1,0:T(8,128)(2,1)S(1)}) custom-call(s32[6]{0:T(128)S(1)} %stack.27.place, bf16[3104,128]{1,0:T(8,128)(2,1)S(1)} %get-tuple-element.28.same, bf16[3120,128]{1,0:T(8,128)(2,1)S(1)} %collective-permute-done.9.r1, bf16[3120,128]{1,0:T(8,128)(2,1)S(1)} %collective-permute-done.10.rm, ...), custom_call_target="tpu_custom_call" | custom-call | flops 5699999744 | bytes 8388608 | tf_op jit(solution)/shard_map/left_panels/pallas_call | solution.py:186
  98.6 0.0 collective-permute-done.7.from_core
  98.6 8.6 %collective-permute-done.8.from_halo = bf16[2,4,544,128]{3,2,1,0:T(8,128)(2,1)S(1)} collective-permute-done((bf16[2,4,544,128]{3,2,1,0:T(8,128)(2,1)S(1)}, bf16[2,4,544,128]{3,2,1,0:T(8,128)(2,1)S(1)}, u32[]{:S(2)}, u32[]{:S(2)}) %collective-permute-start.8) | collective-permute-done | bytes 1114144 | tf_op jit(solution)/shard_map/ppermute | solution.py:55
  107.1 5.7 %multiply.3 = (f32[3,2,128,128]{3,2,1,0:T(8,128)S(1)}, f32[3,2,128,128]{3,2,1,0:T(8,128)S(1)}) custom-call(s32[6]{0:T(128)S(1)} %stack.27.place, bf16[1632,128]{1,0:T(8,128)(2,1)S(1)} %get-tuple-element.20.own, bf16[1632,128]{1,0:T(8,128)(2,1)S(1)} %collective-permute-done.up, bf16[1632,128]{1,0:T(8,128)(2,1)S(1)} %collective-permute-done.1.down, ...), custom_call_target="tpu_custom_call" | custom-call | flops 3221225472 | bytes 10485760 | tf_op jit(solution)/shard_map/multiply/pallas_call | solution.py:294
  112.9 3.8 %collective-permute-start.13 = (f32[3,2,128,128]{3,2,1,0:T(8,128)S(1)}, f32[3,2,128,128]{3,2,1,0:T(8,128)S(1)}, u32[]{:S(2)}, u32[]{:S(2)}) collective-permute-start(f32[3,2,128,128]{3,2,1,0:T(8,128)S(1)} %get-tuple-element.34), channel_id=1, source_target_pairs={{0,256},{1,257},{2,258},{3,259},{4,260},{5,261},{6,262},{7,263},{8... | collective-permute-start | bytes 1179656 | tf_op jit(solution)/shard_map/ppermute | solution.py:55
  116.7 5.7 %multiply.2 = (f32[3,2,128,128]{3,2,1,0:T(8,128)S(1)}, f32[3,2,128,128]{3,2,1,0:T(8,128)S(1)}) custom-call(s32[6]{0:T(128)S(1)} %stack.27.place, bf16[1632,128]{1,0:T(8,128)(2,1)S(1)} %get-tuple-element.20.own, bf16[1632,128]{1,0:T(8,128)(2,1)S(1)} %collective-permute-done.up, bf16[1632,128]{1,0:T(8,128)(2,1)S(1)} %collective-permute-done.1.down, ...), custom_call_target="tpu_custom_call" | custom-call | flops 3221225472 | bytes 10485760 | tf_op jit(solution)/shard_map/multiply/pallas_call | solution.py:294
  122.4 2.1 %collective-permute-start.12 = (f32[3,2,128,128]{3,2,1,0:T(8,128)S(1)}, f32[3,2,128,128]{3,2,1,0:T(8,128)S(1)}, u32[]{:S(2)}, u32[]{:S(2)}) collective-permute-start(f32[3,2,128,128]{3,2,1,0:T(8,128)S(1)} %get-tuple-element.32), channel_id=1, source_target_pairs={{0,256},{1,257},{2,258},{3,259},{4,260},{5,261},{6,262},{7,263},{8... | collective-permute-start | bytes 1179656 | tf_op jit(solution)/shard_map/ppermute | solution.py:55
  124.5 0.3 collective-permute-done.13.got1
  124.8 7.3 %collective-permute-done.12.got0 = f32[3,2,128,128]{3,2,1,0:T(8,128)S(1)} collective-permute-done((f32[3,2,128,128]{3,2,1,0:T(8,128)S(1)}, f32[3,2,128,128]{3,2,1,0:T(8,128)S(1)}, u32[]{:S(2)}, u32[]{:S(2)}) %collective-permute-start.12) | collective-permute-done | bytes 393248 | tf_op jit(solution)/shard_map/ppermute | solution.py:55
  132.1 0.9 finish.1
  (2 shorter events, 0.0 us)
Async XLA Ops:
  0.1 1.0 copy-start
  1.1 0.7 copy-start.1
  1.8 0.7 copy-start.2
  3.3 51.1 %collective-permute-start.1 = (bf16[1632,128]{1,0:T(8,128)(2,1)S(1)}, bf16[1632,128]{1,0:T(8,128)(2,1)S(1)}, u32[]{:S(2)}, u32[]{:S(2)}) collective-permute-start(bf16[1632,128]{1,0:T(8,128)(2,1)S(1)} %get-tuple-element.20.own), channel_id=1, source_target_pairs={{0,192},{1,193},{2,194},{3,195},{4,196},{5,197},{6,198},{7,199},{8... | collective-permute-start | bytes 1253384 | tf_op jit(solution)/shard_map/ppermute | solution.py:55
  16.0 45.9 %collective-permute-start = (bf16[1632,128]{1,0:T(8,128)(2,1)S(1)}, bf16[1632,128]{1,0:T(8,128)(2,1)S(1)}, u32[]{:S(2)}, u32[]{:S(2)}) collective-permute-start(bf16[1632,128]{1,0:T(8,128)(2,1)S(1)} %get-tuple-element.20.own), channel_id=1, source_target_pairs={{0,64},{1,65},{2,66},{3,67},{4,68},{5,69},{6,70},{7,71},{8,72},{9,... | collective-permute-start | bytes 1253384 | tf_op jit(solution)/shard_map/ppermute | solution.py:55
  17.9 14.0 %collective-permute-start.2 = (bf16[1552,128]{1,0:T(8,128)(2,1)S(1)}, bf16[1552,128]{1,0:T(8,128)(2,1)S(1)}, u32[]{:S(2)}, u32[]{:S(2)}) collective-permute-start(bf16[1552,128]{1,0:T(8,128)(2,1)S(1)} %get-tuple-element.21.own), channel_id=1, source_target_pairs={{0,2},{1,3},{2,4},{3,5},{4,6},{5,7},{6,0},{7,1},{8,10},{9,11},{10,... | collective-permute-start | bytes 1191944 | tf_op jit(solution)/shard_map/ppermute | solution.py:55
  20.8 15.6 %collective-permute-start.3 = (bf16[1552,128]{1,0:T(8,128)(2,1)S(1)}, bf16[1552,128]{1,0:T(8,128)(2,1)S(1)}, u32[]{:S(2)}, u32[]{:S(2)}) collective-permute-start(bf16[1552,128]{1,0:T(8,128)(2,1)S(1)} %get-tuple-element.21.own), channel_id=1, source_target_pairs={{0,4},{1,5},{2,6},{3,7},{4,0},{5,1},{6,2},{7,3},{8,12},{9,13},{10,... | collective-permute-start | bytes 1191944 | tf_op jit(solution)/shard_map/ppermute | solution.py:55
  24.7 18.0 %collective-permute-start.4 = (bf16[1552,128]{1,0:T(8,128)(2,1)S(1)}, bf16[1552,128]{1,0:T(8,128)(2,1)S(1)}, u32[]{:S(2)}, u32[]{:S(2)}) collective-permute-start(bf16[1552,128]{1,0:T(8,128)(2,1)S(1)} %get-tuple-element.21.own), channel_id=1, source_target_pairs={{0,6},{1,7},{2,0},{3,1},{4,2},{5,3},{6,4},{7,5},{8,14},{9,15},{10,... | collective-permute-start | bytes 1191944 | tf_op jit(solution)/shard_map/ppermute | solution.py:55
  43.3 50.6 %collective-permute-start.10 = (bf16[3120,128]{1,0:T(8,128)(2,1)S(1)}, bf16[3120,128]{1,0:T(8,128)(2,1)S(1)}, u32[]{:S(2)}, u32[]{:S(2)}) collective-permute-start(bf16[3120,128]{1,0:T(8,128)(2,1)S(1)} %get-tuple-element.23), channel_id=1, source_target_pairs={{0,257},{1,256},{2,259},{3,258},{4,261},{5,260},{6,263},{7,262},{8... | collective-permute-start | bytes 2396168 | tf_op jit(solution)/shard_map/ppermute | solution.py:55
  48.3 45.7 %collective-permute-start.9 = (bf16[3120,128]{1,0:T(8,128)(2,1)S(1)}, bf16[3120,128]{1,0:T(8,128)(2,1)S(1)}, u32[]{:S(2)}, u32[]{:S(2)}) collective-permute-start(bf16[3120,128]{1,0:T(8,128)(2,1)S(1)} %get-tuple-element.23), channel_id=1, source_target_pairs={{0,256},{1,257},{2,258},{3,259},{4,260},{5,261},{6,262},{7,263},{8... | collective-permute-start | bytes 2396168 | tf_op jit(solution)/shard_map/ppermute | solution.py:55
  50.2 43.8 %collective-permute-start.11 = (bf16[3104,128]{1,0:T(8,128)(2,1)S(1)}, bf16[3104,128]{1,0:T(8,128)(2,1)S(1)}, u32[]{:S(2)}, u32[]{:S(2)}) collective-permute-start(bf16[3104,128]{1,0:T(8,128)(2,1)S(1)} %get-tuple-element.28.same), channel_id=1, source_target_pairs={{0,1},{1,0},{2,3},{3,2},{4,5},{5,4},{6,7},{7,6},{8,9},{9,8},{10,11... | collective-permute-start | bytes 2383880 | tf_op jit(solution)/shard_map/ppermute | solution.py:55
  54.3 25.6 %collective-permute-start.6 = (bf16[816,128]{1,0:T(8,128)(2,1)S(1)}, bf16[816,128]{1,0:T(8,128)(2,1)S(1)}, u32[]{:S(2)}, u32[]{:S(2)}) collective-permute-start(bf16[816,128]{1,0:T(8,128)(2,1)S(1)} %slice.9), channel_id=1, source_target_pairs={{0,192},{1,193},{2,194},{3,195},{4,196},{5,197},{6,198},{7,199},{8... | collective-permute-start | bytes 626696 | tf_op jit(solution)/shard_map/ppermute | solution.py:55
  61.9 18.0 %collective-permute-start.5 = (bf16[816,128]{1,0:T(8,128)(2,1)S(1)}, bf16[816,128]{1,0:T(8,128)(2,1)S(1)}, u32[]{:S(2)}, u32[]{:S(2)}) collective-permute-start(bf16[816,128]{1,0:T(8,128)(2,1)S(1)} %slice.8), channel_id=1, source_target_pairs={{0,64},{1,65},{2,66},{3,67},{4,68},{5,69},{6,70},{7,71},{8,72},{9,... | collective-permute-start | bytes 626696 | tf_op jit(solution)/shard_map/ppermute | solution.py:55
  80.6 18.0 %collective-permute-start.7 = (bf16[2,4,544,128]{3,2,1,0:T(8,128)(2,1)S(1)}, bf16[2,4,544,128]{3,2,1,0:T(8,128)(2,1)S(1)}, u32[]{:S(2)}, u32[]{:S(2)}) collective-permute-start(bf16[2,4,544,128]{3,2,1,0:T(8,128)(2,1)S(1)} %get-tuple-element.26), channel_id=1, source_target_pairs={{0,8},{1,9},{2,10},{3,11},{4,12},{5,13},{6,14},{7,15},{8,0},{9,1},... | collective-permute-start | bytes 3342344 | tf_op jit(solution)/shard_map/ppermute | solution.py:55
  82.5 24.6 %collective-permute-start.8 = (bf16[2,4,544,128]{3,2,1,0:T(8,128)(2,1)S(1)}, bf16[2,4,544,128]{3,2,1,0:T(8,128)(2,1)S(1)}, u32[]{:S(2)}, u32[]{:S(2)}) collective-permute-start(bf16[2,4,544,128]{3,2,1,0:T(8,128)(2,1)S(1)} %get-tuple-element.27), channel_id=1, source_target_pairs={{0,248},{1,249},{2,250},{3,251},{4,252},{5,253},{6,254},{7,255},{8... | collective-permute-start | bytes 3342344 | tf_op jit(solution)/shard_map/ppermute | solution.py:55
  112.9 11.9 %collective-permute-start.13 = (f32[3,2,128,128]{3,2,1,0:T(8,128)S(1)}, f32[3,2,128,128]{3,2,1,0:T(8,128)S(1)}, u32[]{:S(2)}, u32[]{:S(2)}) collective-permute-start(f32[3,2,128,128]{3,2,1,0:T(8,128)S(1)} %get-tuple-element.34), channel_id=1, source_target_pairs={{0,256},{1,257},{2,258},{3,259},{4,260},{5,261},{6,262},{7,263},{8... | collective-permute-start | bytes 1179656 | tf_op jit(solution)/shard_map/ppermute | solution.py:55
  122.4 9.7 %collective-permute-start.12 = (f32[3,2,128,128]{3,2,1,0:T(8,128)S(1)}, f32[3,2,128,128]{3,2,1,0:T(8,128)S(1)}, u32[]{:S(2)}, u32[]{:S(2)}) collective-permute-start(f32[3,2,128,128]{3,2,1,0:T(8,128)S(1)} %get-tuple-element.32), channel_id=1, source_target_pairs={{0,256},{1,257},{2,258},{3,259},{4,260},{5,261},{6,262},{7,263},{8... | collective-permute-start | bytes 1179656 | tf_op jit(solution)/shard_map/ppermute | solution.py:55

commit v4 on v3

--- a/solution.py
+++ b/solution.py
@@ -13,6 +13,7 @@
 MULT = (3 << 30, 3 << 30)
 LEFT = 5700000000
 SORT = 0
+BEGIN = 0
 LIMIT = 48 << 20
 BLOCK = 12 * T + 16
 HEAD, TAIL = T, T + 16
@@ -225,54 +226,84 @@
     )(place, *sources)
 
 
-def multiply_kernel(
-    h, place, own, up, down, far0, far1, from_core, from_halo, left, mine, partner, keep, give, right
-):
+def place_row(k, v0, v1, keys, right, at, row, clear):
+    half = (lanes() >= T // 2).astype(F32)
+    keys = keys.astype(F32) + float(k)
+    w0, w1 = flipped(v0), flipped(v1)
+    for w in range(4):
+        into = (at, slice(row * T, (row + 1) * T), slice(w * T, (w + 1) * T))
+        if 2 * w + 1 < k - 2 or 2 * w > k + 2:
+            if clear:
+                right[into] = jnp.zeros((T, T), BF16)
+            continue
+        pick = [chosen(keys[n : n + 1], half + float(2 * w)) for n in range(4)]
+        right[into] = (v0 * pick[0] + w0 * pick[1]) + (v1 * pick[2] + w1 * pick[3])
+
+
+def begin_kernel(h, place, own, up, down, far0, far1, left, out, right):
+    sums = [None] * 3
+    for p, (source, shift) in enumerate(((own, 0), (up, 3), (down, 1), (None, 2))):
+        panel = (place[2] + shift) % 4
+        held = (far0, far1)[h] if source is None else source
+        base = 0 if source is None else h * PIECE
+        for r in range(3):
+            head = base + r * HEAD
+            tail = base + 3 * HEAD + r * TAIL
+            keys = held[tail + T : tail + TAIL, :]
+            place_row(r + 2, held[head : head + T, :], held[tail : tail + T, :], keys, right, p % 2, r, p < 2)
+        for i in range(3):
+            first = i // 2 * T
+            part = jnp.dot(
+                left[i, panel, :, (2 - i) * T : (5 - i) * T],
+                right[p % 2, :, first : first + 3 * T],
+                preferred_element_type=F32,
+            )
+            sums[i] = part if sums[i] is None else sums[i] + part
+    for i in range(3):
+        out[i] = sums[i]
+
+
+def begin(flops, h, place, pieces, left):
+    return pl.pallas_call(
+        functools.partial(begin_kernel, h),
+        out_shape=jax.ShapeDtypeStruct((3, 2 * T, 3 * T), F32),
+        in_specs=[SMEM] + [VMEM] * 6,
+        out_specs=VMEM,
+        scratch_shapes=[pltpu.VMEM((2, 3 * T, 4 * T), BF16)],
+        compiler_params=params(),
+        cost_estimate=cost(flops, 6 << 20),
+        name="begin",
+    )(place, *pieces, left)
+
+
+def multiply_kernel(h, place, from_core, from_halo, begun, left, mine, partner, keep, give, right):
     b, core = place[2], place[3]
     half = (lanes() >= T // 2).astype(F32)
-    zero = jnp.zeros((T, T), BF16)
-    sums = [None] * 3
-    for p, (source, shift) in enumerate(((own, 0), (up, 3), (down, 1), (None, 2))):
-        panel = (b + shift) % 4
-        held = (far0, far1)[h] if source is None else source
-        base = 0 if source is None else h * PIECE
-
-        def edge(first, size, low):
+    sums = [begun[i] for i in range(3)]
+    for panel in range(4):
+
+        def edge(first, size, low, panel=panel):
             rows = slice(first, first + size)
             above, below = (from_halo, from_core) if low else (from_core, from_halo)
             return jnp.where(core == 0, above[h, panel, rows, :], below[h, panel, rows, :])
 
-        for k in range(7):
-            if 2 <= k < 5:
-                head = base + (k - 2) * HEAD
-                tail = base + 3 * HEAD + (k - 2) * TAIL
-                v0 = held[head : head + T, :]
-                v1 = held[tail : tail + T, :]
-                keys = held[tail + T : tail + TAIL, :]
-            else:
-                row, low = (k, True) if k < 2 else (k - 5, False)
-                v0 = edge(row * HEAD, T, low)
-                v1 = edge(2 * HEAD + row * TAIL, T, low)
-                keys = edge(2 * HEAD + row * TAIL + T, 16, low)
-            keys = keys.astype(F32) + float(k)
-            w0, w1 = flipped(v0), flipped(v1)
-            for w in range(4):
-                into = (p % 2, slice(k * T, (k + 1) * T), slice(w * T, (w + 1) * T))
-                if 2 * w + 1 < k - 2 or 2 * w > k + 2:
-                    if p < 2:
-                        right[into] = zero
-                    continue
-                target = half + float(2 * w)
-                pick = [chosen(keys[n : n + 1], target) for n in range(4)]
-                right[into] = (v0 * pick[0] + w0 * pick[1]) + (v1 * pick[2] + w1 * pick[3])
+        for n, k in enumerate((0, 1, 5, 6)):
+            row, low = n % 2, n < 2
+            tail = 2 * HEAD + row * TAIL
+            keys = edge(tail + T, 16, low)
+            place_row(k, edge(row * HEAD, T, low), edge(tail, T, low), keys, right, panel % 2, n, panel < 2)
         for i in range(3):
             first = i // 2 * T
-            part = jnp.dot(
-                left[i, panel],
-                right[p % 2, i * T : (i + 5) * T, first : first + 3 * T],
+            side = left[i, panel]
+            if i == 1:
+                side = jnp.concatenate([side[:, :T], side[:, 4 * T :]], axis=1)
+            else:
+                side = side[:, : 2 * T] if i == 0 else side[:, 3 * T :]
+            sums[i] = sums[i] + jnp.dot(
+                side,
+                right[panel % 2, i * T : (i + 2) * T, first : first + 3 * T],
                 preferred_element_type=F32,
             )
-            sums[i] = part if sums[i] is None else sums[i] + part
     for i in range(3):
         for side, (out, source) in enumerate(((keep, mine), (give, partner))):
             keys = source[...].astype(F32)[4 * i : 4 * i + 4] + float(i + 2)
@@ -289,18 +320,18 @@
                 out[i, m] = total
 
 
-def multiply(flops, h, place, sources, left, mine, partner):
+def multiply(flops, h, place, received, begun, left, mine, partner):
     shape = jax.ShapeDtypeStruct((3, 2, T, T), F32)
     return pl.pallas_call(
         functools.partial(multiply_kernel, h),
         out_shape=[shape, shape],
-        in_specs=[SMEM] + [VMEM] * 10,
+        in_specs=[SMEM] + [VMEM] * 6,
         out_specs=[VMEM, VMEM],
-        scratch_shapes=[pltpu.VMEM((2, 7 * T, 4 * T), BF16)],
+        scratch_shapes=[pltpu.VMEM((2, 4 * T, 4 * T), BF16)],
         compiler_params=params(),
         cost_estimate=cost(flops, 10 << 20),
         name="multiply",
-    )(place, *sources, left, mine, partner)
+    )(place, *received, begun, left, mine, partner)
 
 
 def finish_kernel(own0, got0, own1, got1, out):
@@ -341,10 +372,11 @@
     left, partner = left_panels(place, same, r1, rm, r2)
     pieces = (whole, up, down, *far)
     to_core, to_halo = edges(EDGE[0], place, *pieces)
-    pieces += (send(to_core, CORE), send(to_halo, HALO))
+    received = (send(to_core, CORE), send(to_halo, HALO))
+    begun = [begin(BEGIN, h, place, pieces, left) for h in range(2)]
     kept, got = [], []
     for h in range(2):
-        keep, give = multiply(MULT[h], h, place, pieces, left, keys, partner)
+        keep, give = multiply(MULT[h], h, place, received, begun[h], left, keys, partner)
         kept.append(keep)
         got.append(send(give, PLANE))
     return finish(kept[0], got[0], kept[1], got[1])

time: 136 us -> 133 us (0.978)
  the two profiles are of different devices: /device:TPU:6 before, /device:TPU:107 now
where the time goes in v4:
time: 133 us; the launch traced here: 132 us
  waiting for transfers between devices  54.6 us (41%)
  starting transfers between devices  51 us (38%)
  Pallas kernels  24.1 us (18%)
  local copies, waits for them, and re-layouts  2.45 us (2%)
    ppermute x14, waiting for transfers between devices, send(): return lax.ppermute(block, ('row', 'col'), pairs)  54.6 us
    ppermute x14, starting transfers between devices, send(): return lax.ppermute(block, ('row', 'col'), pairs)  51 us
    pallas_call x2, Pallas kernels, begin(): pl.pallas_call(functools.partial(begin_kernel, h), out_shape=jax.ShapeDty...  8.32 us
    pallas_call x2, Pallas kernels, multiply(): pl.pallas_call(functools.partial(multiply_kernel, h), out_shape=[shape, s...  8.04 us
    pallas_call x1, Pallas kernels, left_panels(): pl.pallas_call(left_kernel, out_shape=[jax.ShapeDtypeStruct((3, 4, 2 * T,...  4.58 us
  transfers between devices with their start and end apart: 14, of which 8 were waited for; matrix products, arithmetic and copies ran while one was open for 0% of the time, Pallas kernels for 14%

profile of v4, /device:TPU:107, one launch (start us, length us, event | category | flops | bytes accessed | tf_op | source)
XLA Modules:
  0.0 132.5 jit_solution(18005501842958352974)
XLA Ops:
  0.0 0.1 stack.27.place
  0.1 0.0 copy-start
  0.1 1.0 copy-done
  1.1 0.0 copy-start.1
  1.1 0.7 copy-done.1
  1.8 0.0 copy-start.2
  1.8 0.7 copy-done.2
  2.4 0.8 pack.1
  3.3 9.8 %collective-permute-start.1 = (bf16[1632,128]{1,0:T(8,128)(2,1)S(1)}, bf16[1632,128]{1,0:T(8,128)(2,1)S(1)}, u32[]{:S(2)}, u32[]{:S(2)}) collective-permute-start(bf16[1632,128]{1,0:T(8,128)(2,1)S(1)} %get-tuple-element.20.own), channel_id=1, source_target_pairs={{0,192},{1,193},{2,194},{3,195},{4,196},{5,197},{6,198},{7,199},{8... | collective-permute-start | bytes 1253384 | tf_op jit(solution)/shard_map/ppermute | solution.py:56
  13.0 1.9 %collective-permute-start = (bf16[1632,128]{1,0:T(8,128)(2,1)S(1)}, bf16[1632,128]{1,0:T(8,128)(2,1)S(1)}, u32[]{:S(2)}, u32[]{:S(2)}) collective-permute-start(bf16[1632,128]{1,0:T(8,128)(2,1)S(1)} %get-tuple-element.20.own), channel_id=1, source_target_pairs={{0,64},{1,65},{2,66},{3,67},{4,68},{5,69},{6,70},{7,71},{8,72},{9,... | collective-permute-start | bytes 1253384 | tf_op jit(solution)/shard_map/ppermute | solution.py:56
  14.9 3.1 %collective-permute-start.2 = (bf16[1552,128]{1,0:T(8,128)(2,1)S(1)}, bf16[1552,128]{1,0:T(8,128)(2,1)S(1)}, u32[]{:S(2)}, u32[]{:S(2)}) collective-permute-start(bf16[1552,128]{1,0:T(8,128)(2,1)S(1)} %get-tuple-element.21.own), channel_id=1, source_target_pairs={{0,2},{1,3},{2,4},{3,5},{4,6},{5,7},{6,0},{7,1},{8,10},{9,11},{10,... | collective-permute-start | bytes 1191944 | tf_op jit(solution)/shard_map/ppermute | solution.py:56
  18.1 2.7 %collective-permute-start.3 = (bf16[1552,128]{1,0:T(8,128)(2,1)S(1)}, bf16[1552,128]{1,0:T(8,128)(2,1)S(1)}, u32[]{:S(2)}, u32[]{:S(2)}) collective-permute-start(bf16[1552,128]{1,0:T(8,128)(2,1)S(1)} %get-tuple-element.21.own), channel_id=1, source_target_pairs={{0,4},{1,5},{2,6},{3,7},{4,0},{5,1},{6,2},{7,3},{8,12},{9,13},{10,... | collective-permute-start | bytes 1191944 | tf_op jit(solution)/shard_map/ppermute | solution.py:56
  20.8 3.8 %collective-permute-start.4 = (bf16[1552,128]{1,0:T(8,128)(2,1)S(1)}, bf16[1552,128]{1,0:T(8,128)(2,1)S(1)}, u32[]{:S(2)}, u32[]{:S(2)}) collective-permute-start(bf16[1552,128]{1,0:T(8,128)(2,1)S(1)} %get-tuple-element.21.own), channel_id=1, source_target_pairs={{0,6},{1,7},{2,0},{3,1},{4,2},{5,3},{6,4},{7,5},{8,14},{9,15},{10,... | collective-permute-start | bytes 1191944 | tf_op jit(solution)/shard_map/ppermute | solution.py:56
  24.6 2.0 %collective-permute-done.2.g1 = bf16[1552,128]{1,0:T(8,128)(2,1)S(1)} collective-permute-done((bf16[1552,128]{1,0:T(8,128)(2,1)S(1)}, bf16[1552,128]{1,0:T(8,128)(2,1)S(1)}, u32[]{:S(2)}, u32[]{:S(2)}) %collective-permute-start.2) | collective-permute-done | bytes 397344 | tf_op jit(solution)/shard_map/ppermute | solution.py:56
  26.6 4.4 %collective-permute-done.3.g2 = bf16[1552,128]{1,0:T(8,128)(2,1)S(1)} collective-permute-done((bf16[1552,128]{1,0:T(8,128)(2,1)S(1)}, bf16[1552,128]{1,0:T(8,128)(2,1)S(1)}, u32[]{:S(2)}, u32[]{:S(2)}) %collective-permute-start.3) | collective-permute-done | bytes 397344 | tf_op jit(solution)/shard_map/ppermute | solution.py:56
  31.0 10.1 %collective-permute-done.4.g3 = bf16[1552,128]{1,0:T(8,128)(2,1)S(1)} collective-permute-done((bf16[1552,128]{1,0:T(8,128)(2,1)S(1)}, bf16[1552,128]{1,0:T(8,128)(2,1)S(1)}, u32[]{:S(2)}, u32[]{:S(2)}) %collective-permute-start.4) | collective-permute-done | bytes 397344 | tf_op jit(solution)/shard_map/ppermute | solution.py:56
  41.1 0.7 sort_panels.1
  41.8 2.1 %collective-permute-start.10 = (bf16[3120,128]{1,0:T(8,128)(2,1)S(1)}, bf16[3120,128]{1,0:T(8,128)(2,1)S(1)}, u32[]{:S(2)}, u32[]{:S(2)}) collective-permute-start(bf16[3120,128]{1,0:T(8,128)(2,1)S(1)} %get-tuple-element.23), channel_id=1, source_target_pairs={{0,257},{1,256},{2,259},{3,258},{4,261},{5,260},{6,263},{7,262},{8... | collective-permute-start | bytes 2396168 | tf_op jit(solution)/shard_map/ppermute | solution.py:56
  43.9 3.2 %collective-permute-start.9 = (bf16[3120,128]{1,0:T(8,128)(2,1)S(1)}, bf16[3120,128]{1,0:T(8,128)(2,1)S(1)}, u32[]{:S(2)}, u32[]{:S(2)}) collective-permute-start(bf16[3120,128]{1,0:T(8,128)(2,1)S(1)} %get-tuple-element.23), channel_id=1, source_target_pairs={{0,256},{1,257},{2,258},{3,259},{4,260},{5,261},{6,262},{7,263},{8... | collective-permute-start | bytes 2396168 | tf_op jit(solution)/shard_map/ppermute | solution.py:56
  47.1 5.1 %collective-permute-start.11 = (bf16[3104,128]{1,0:T(8,128)(2,1)S(1)}, bf16[3104,128]{1,0:T(8,128)(2,1)S(1)}, u32[]{:S(2)}, u32[]{:S(2)}) collective-permute-start(bf16[3104,128]{1,0:T(8,128)(2,1)S(1)} %get-tuple-element.28.same), channel_id=1, source_target_pairs={{0,1},{1,0},{2,3},{3,2},{4,5},{5,4},{6,7},{7,6},{8,9},{9,8},{10,11... | collective-permute-start | bytes 2383880 | tf_op jit(solution)/shard_map/ppermute | solution.py:56
  52.3 0.0 collective-permute-done.1.down
  52.3 7.3 %collective-permute-start.6 = (bf16[816,128]{1,0:T(8,128)(2,1)S(1)}, bf16[816,128]{1,0:T(8,128)(2,1)S(1)}, u32[]{:S(2)}, u32[]{:S(2)}) collective-permute-start(bf16[816,128]{1,0:T(8,128)(2,1)S(1)} %slice.9), channel_id=1, source_target_pairs={{0,192},{1,193},{2,194},{3,195},{4,196},{5,197},{6,198},{7,199},{8... | collective-permute-start | bytes 626696 | tf_op jit(solution)/shard_map/ppermute | solution.py:56
  59.6 0.0 collective-permute-done.up
  59.6 1.9 %collective-permute-start.5 = (bf16[816,128]{1,0:T(8,128)(2,1)S(1)}, bf16[816,128]{1,0:T(8,128)(2,1)S(1)}, u32[]{:S(2)}, u32[]{:S(2)}) collective-permute-start(bf16[816,128]{1,0:T(8,128)(2,1)S(1)} %slice.8), channel_id=1, source_target_pairs={{0,64},{1,65},{2,66},{3,67},{4,68},{5,69},{6,70},{7,71},{8,72},{9,... | collective-permute-start | bytes 626696 | tf_op jit(solution)/shard_map/ppermute | solution.py:56
  61.6 5.2 %collective-permute-done.6.far1 = bf16[816,128]{1,0:T(8,128)(2,1)S(1)} collective-permute-done((bf16[816,128]{1,0:T(8,128)(2,1)S(1)}, bf16[816,128]{1,0:T(8,128)(2,1)S(1)}, u32[]{:S(2)}, u32[]{:S(2)}) %collective-permute-start.6) | collective-permute-done | bytes 208928 | tf_op jit(solution)/shard_map/ppermute | solution.py:56
  66.7 18.7 %collective-permute-done.5.far0 = bf16[816,128]{1,0:T(8,128)(2,1)S(1)} collective-permute-done((bf16[816,128]{1,0:T(8,128)(2,1)S(1)}, bf16[816,128]{1,0:T(8,128)(2,1)S(1)}, u32[]{:S(2)}, u32[]{:S(2)}) %collective-permute-start.5) | collective-permute-done | bytes 208928 | tf_op jit(solution)/shard_map/ppermute | solution.py:56
  85.4 0.7 edges.1
  86.1 2.9 %collective-permute-start.7 = (bf16[2,4,544,128]{3,2,1,0:T(8,128)(2,1)S(1)}, bf16[2,4,544,128]{3,2,1,0:T(8,128)(2,1)S(1)}, u32[]{:S(2)}, u32[]{:S(2)}) collective-permute-start(bf16[2,4,544,128]{3,2,1,0:T(8,128)(2,1)S(1)} %get-tuple-element.26), channel_id=1, source_target_pairs={{0,8},{1,9},{2,10},{3,11},{4,12},{5,13},{6,14},{7,15},{8,0},{9,1},... | collective-permute-start | bytes 3342344 | tf_op jit(solution)/shard_map/ppermute | solution.py:56
  89.1 1.9 %collective-permute-start.8 = (bf16[2,4,544,128]{3,2,1,0:T(8,128)(2,1)S(1)}, bf16[2,4,544,128]{3,2,1,0:T(8,128)(2,1)S(1)}, u32[]{:S(2)}, u32[]{:S(2)}) collective-permute-start(bf16[2,4,544,128]{3,2,1,0:T(8,128)(2,1)S(1)} %get-tuple-element.27), channel_id=1, source_target_pairs={{0,248},{1,249},{2,250},{3,251},{4,252},{5,253},{6,254},{7,255},{8... | collective-permute-start | bytes 3342344 | tf_op jit(solution)/shard_map/ppermute | solution.py:56
  91.0 0.0 collective-permute-done.11.r2
  91.0 0.0 collective-permute-done.10.rm
  91.0 0.0 collective-permute-done.9.r1
  91.0 4.6 %left_panels.1 = (bf16[3,4,256,640]{3,2,1,0:T(8,128)(2,1)}, bf16[16,128]{1,0:T(8,128)(2,1)S(1)}) custom-call(s32[6]{0:T(128)S(1)} %stack.27.place, bf16[3104,128]{1,0:T(8,128)(2,1)S(1)} %get-tuple-element.28.same, bf16[3120,128]{1,0:T(8,128)(2,1)S(1)} %collective-permute-done.9.r1, bf16[3120,128]{1,0:T(8,128)(2,1)S(1)} %collective-permute-done.10.rm, ...), custom_call_target="tpu_custom_call" | custom-call | flops 5699999744 | bytes 8388608 | tf_op jit(solution)/shard_map/left_panels/pallas_call | solution.py:187
  95.6 4.2 %begin.3.begun = f32[3,256,384]{2,1,0:T(8,128)S(1)} custom-call(s32[6]{0:T(128)S(1)} %stack.27.place, bf16[1632,128]{1,0:T(8,128)(2,1)S(1)} %get-tuple-element.20.own, bf16[1632,128]{1,0:T(8,128)(2,1)S(1)} %collective-permute-done.up, bf16[1632,128]{1,0:T(8,128)(2,1)S(1)} %collective-permute-done.1.down, bf16[816,128]{1,0:T(8,128)(2,1)S(1)} %collective-permute-done.5.far0, ...), custom_call_target="tpu_custom_call" | custom-call | bytes 6291456 | tf_op jit(solution)/shard_map/begin/pallas_call | solution.py:267
  99.8 4.2 %begin.2.begun = f32[3,256,384]{2,1,0:T(8,128)S(1)} custom-call(s32[6]{0:T(128)S(1)} %stack.27.place, bf16[1632,128]{1,0:T(8,128)(2,1)S(1)} %get-tuple-element.20.own, bf16[1632,128]{1,0:T(8,128)(2,1)S(1)} %collective-permute-done.up, bf16[1632,128]{1,0:T(8,128)(2,1)S(1)} %collective-permute-done.1.down, bf16[816,128]{1,0:T(8,128)(2,1)S(1)} %collective-permute-done.5.far0, ...), custom_call_target="tpu_custom_call" | custom-call | bytes 6291456 | tf_op jit(solution)/shard_map/begin/pallas_call | solution.py:267
  103.9 0.0 collective-permute-done.7.from_core
  103.9 3.1 %collective-permute-done.8.from_halo = bf16[2,4,544,128]{3,2,1,0:T(8,128)(2,1)S(1)} collective-permute-done((bf16[2,4,544,128]{3,2,1,0:T(8,128)(2,1)S(1)}, bf16[2,4,544,128]{3,2,1,0:T(8,128)(2,1)S(1)}, u32[]{:S(2)}, u32[]{:S(2)}) %collective-permute-start.8) | collective-permute-done | bytes 1114144 | tf_op jit(solution)/shard_map/ppermute | solution.py:56
  107.1 4.0 %multiply.3 = (f32[3,2,128,128]{3,2,1,0:T(8,128)S(1)}, f32[3,2,128,128]{3,2,1,0:T(8,128)S(1)}) custom-call(s32[6]{0:T(128)S(1)} %stack.27.place, bf16[2,4,544,128]{3,2,1,0:T(8,128)(2,1)S(1)} %collective-permute-done.7.from_core, bf16[2,4,544,128]{3,2,1,0:T(8,128)(2,1)S(1)} %collective-permute-done.8.from_halo, f32[3,256,384]{2,1,0:T(8,128)S(1)} %begin.3.begun, ...), custom_call_target="tpu_custom_call" | custom-call | flops 3221225472 | bytes 10485760 | tf_op jit(solution)/shard_map/multiply/pallas_call | solution.py:325
  111.1 1.9 %collective-permute-start.13 = (f32[3,2,128,128]{3,2,1,0:T(8,128)S(1)}, f32[3,2,128,128]{3,2,1,0:T(8,128)S(1)}, u32[]{:S(2)}, u32[]{:S(2)}) collective-permute-start(f32[3,2,128,128]{3,2,1,0:T(8,128)S(1)} %get-tuple-element.34), channel_id=1, source_target_pairs={{0,256},{1,257},{2,258},{3,259},{4,260},{5,261},{6,262},{7,263},{8... | collective-permute-start | bytes 1179656 | tf_op jit(solution)/shard_map/ppermute | solution.py:56
  113.0 4.0 %multiply.2 = (f32[3,2,128,128]{3,2,1,0:T(8,128)S(1)}, f32[3,2,128,128]{3,2,1,0:T(8,128)S(1)}) custom-call(s32[6]{0:T(128)S(1)} %stack.27.place, bf16[2,4,544,128]{3,2,1,0:T(8,128)(2,1)S(1)} %collective-permute-done.7.from_core, bf16[2,4,544,128]{3,2,1,0:T(8,128)(2,1)S(1)} %collective-permute-done.8.from_halo, f32[3,256,384]{2,1,0:T(8,128)S(1)} %begin.2.begun, ...), custom_call_target="tpu_custom_call" | custom-call | flops 3221225472 | bytes 10485760 | tf_op jit(solution)/shard_map/multiply/pallas_call | solution.py:325
  117.1 3.4 %collective-permute-start.12 = (f32[3,2,128,128]{3,2,1,0:T(8,128)S(1)}, f32[3,2,128,128]{3,2,1,0:T(8,128)S(1)}, u32[]{:S(2)}, u32[]{:S(2)}) collective-permute-start(f32[3,2,128,128]{3,2,1,0:T(8,128)S(1)} %get-tuple-element.32), channel_id=1, source_target_pairs={{0,256},{1,257},{2,258},{3,259},{4,260},{5,261},{6,262},{7,263},{8... | collective-permute-start | bytes 1179656 | tf_op jit(solution)/shard_map/ppermute | solution.py:56
  120.4 3.7 %collective-permute-done.13.got1 = f32[3,2,128,128]{3,2,1,0:T(8,128)S(1)} collective-permute-done((f32[3,2,128,128]{3,2,1,0:T(8,128)S(1)}, f32[3,2,128,128]{3,2,1,0:T(8,128)S(1)}, u32[]{:S(2)}, u32[]{:S(2)}) %collective-permute-start.13) | collective-permute-done | bytes 393248 | tf_op jit(solution)/shard_map/ppermute | solution.py:56
  124.1 7.4 %collective-permute-done.12.got0 = f32[3,2,128,128]{3,2,1,0:T(8,128)S(1)} collective-permute-done((f32[3,2,128,128]{3,2,1,0:T(8,128)S(1)}, f32[3,2,128,128]{3,2,1,0:T(8,128)S(1)}, u32[]{:S(2)}, u32[]{:S(2)}) %collective-permute-start.12) | collective-permute-done | bytes 393248 | tf_op jit(solution)/shard_map/ppermute | solution.py:56
  131.5 1.0 finish.1
  (2 shorter events, 0.0 us)
Async XLA Ops:
  0.1 1.0 copy-start
  1.1 0.7 copy-start.1
  1.8 0.7 copy-start.2
  3.3 49.0 %collective-permute-start.1 = (bf16[1632,128]{1,0:T(8,128)(2,1)S(1)}, bf16[1632,128]{1,0:T(8,128)(2,1)S(1)}, u32[]{:S(2)}, u32[]{:S(2)}) collective-permute-start(bf16[1632,128]{1,0:T(8,128)(2,1)S(1)} %get-tuple-element.20.own), channel_id=1, source_target_pairs={{0,192},{1,193},{2,194},{3,195},{4,196},{5,197},{6,198},{7,199},{8... | collective-permute-start | bytes 1253384 | tf_op jit(solution)/shard_map/ppermute | solution.py:56
  13.0 46.6 %collective-permute-start = (bf16[1632,128]{1,0:T(8,128)(2,1)S(1)}, bf16[1632,128]{1,0:T(8,128)(2,1)S(1)}, u32[]{:S(2)}, u32[]{:S(2)}) collective-permute-start(bf16[1632,128]{1,0:T(8,128)(2,1)S(1)} %get-tuple-element.20.own), channel_id=1, source_target_pairs={{0,64},{1,65},{2,66},{3,67},{4,68},{5,69},{6,70},{7,71},{8,72},{9,... | collective-permute-start | bytes 1253384 | tf_op jit(solution)/shard_map/ppermute | solution.py:56
  14.9 11.6 %collective-permute-start.2 = (bf16[1552,128]{1,0:T(8,128)(2,1)S(1)}, bf16[1552,128]{1,0:T(8,128)(2,1)S(1)}, u32[]{:S(2)}, u32[]{:S(2)}) collective-permute-start(bf16[1552,128]{1,0:T(8,128)(2,1)S(1)} %get-tuple-element.21.own), channel_id=1, source_target_pairs={{0,2},{1,3},{2,4},{3,5},{4,6},{5,7},{6,0},{7,1},{8,10},{9,11},{10,... | collective-permute-start | bytes 1191944 | tf_op jit(solution)/shard_map/ppermute | solution.py:56
  18.1 12.9 %collective-permute-start.3 = (bf16[1552,128]{1,0:T(8,128)(2,1)S(1)}, bf16[1552,128]{1,0:T(8,128)(2,1)S(1)}, u32[]{:S(2)}, u32[]{:S(2)}) collective-permute-start(bf16[1552,128]{1,0:T(8,128)(2,1)S(1)} %get-tuple-element.21.own), channel_id=1, source_target_pairs={{0,4},{1,5},{2,6},{3,7},{4,0},{5,1},{6,2},{7,3},{8,12},{9,13},{10,... | collective-permute-start | bytes 1191944 | tf_op jit(solution)/shard_map/ppermute | solution.py:56
  20.8 20.3 %collective-permute-start.4 = (bf16[1552,128]{1,0:T(8,128)(2,1)S(1)}, bf16[1552,128]{1,0:T(8,128)(2,1)S(1)}, u32[]{:S(2)}, u32[]{:S(2)}) collective-permute-start(bf16[1552,128]{1,0:T(8,128)(2,1)S(1)} %get-tuple-element.21.own), channel_id=1, source_target_pairs={{0,6},{1,7},{2,0},{3,1},{4,2},{5,3},{6,4},{7,5},{8,14},{9,15},{10,... | collective-permute-start | bytes 1191944 | tf_op jit(solution)/shard_map/ppermute | solution.py:56
  41.8 49.2 %collective-permute-start.10 = (bf16[3120,128]{1,0:T(8,128)(2,1)S(1)}, bf16[3120,128]{1,0:T(8,128)(2,1)S(1)}, u32[]{:S(2)}, u32[]{:S(2)}) collective-permute-start(bf16[3120,128]{1,0:T(8,128)(2,1)S(1)} %get-tuple-element.23), channel_id=1, source_target_pairs={{0,257},{1,256},{2,259},{3,258},{4,261},{5,260},{6,263},{7,262},{8... | collective-permute-start | bytes 2396168 | tf_op jit(solution)/shard_map/ppermute | solution.py:56
  43.9 47.1 %collective-permute-start.9 = (bf16[3120,128]{1,0:T(8,128)(2,1)S(1)}, bf16[3120,128]{1,0:T(8,128)(2,1)S(1)}, u32[]{:S(2)}, u32[]{:S(2)}) collective-permute-start(bf16[3120,128]{1,0:T(8,128)(2,1)S(1)} %get-tuple-element.23), channel_id=1, source_target_pairs={{0,256},{1,257},{2,258},{3,259},{4,260},{5,261},{6,262},{7,263},{8... | collective-permute-start | bytes 2396168 | tf_op jit(solution)/shard_map/ppermute | solution.py:56
  47.1 43.8 %collective-permute-start.11 = (bf16[3104,128]{1,0:T(8,128)(2,1)S(1)}, bf16[3104,128]{1,0:T(8,128)(2,1)S(1)}, u32[]{:S(2)}, u32[]{:S(2)}) collective-permute-start(bf16[3104,128]{1,0:T(8,128)(2,1)S(1)} %get-tuple-element.28.same), channel_id=1, source_target_pairs={{0,1},{1,0},{2,3},{3,2},{4,5},{5,4},{6,7},{7,6},{8,9},{9,8},{10,11... | collective-permute-start | bytes 2383880 | tf_op jit(solution)/shard_map/ppermute | solution.py:56
  52.3 14.4 %collective-permute-start.6 = (bf16[816,128]{1,0:T(8,128)(2,1)S(1)}, bf16[816,128]{1,0:T(8,128)(2,1)S(1)}, u32[]{:S(2)}, u32[]{:S(2)}) collective-permute-start(bf16[816,128]{1,0:T(8,128)(2,1)S(1)} %slice.9), channel_id=1, source_target_pairs={{0,192},{1,193},{2,194},{3,195},{4,196},{5,197},{6,198},{7,199},{8... | collective-permute-start | bytes 626696 | tf_op jit(solution)/shard_map/ppermute | solution.py:56
  59.6 25.8 %collective-permute-start.5 = (bf16[816,128]{1,0:T(8,128)(2,1)S(1)}, bf16[816,128]{1,0:T(8,128)(2,1)S(1)}, u32[]{:S(2)}, u32[]{:S(2)}) collective-permute-start(bf16[816,128]{1,0:T(8,128)(2,1)S(1)} %slice.8), channel_id=1, source_target_pairs={{0,64},{1,65},{2,66},{3,67},{4,68},{5,69},{6,70},{7,71},{8,72},{9,... | collective-permute-start | bytes 626696 | tf_op jit(solution)/shard_map/ppermute | solution.py:56
  86.1 17.8 %collective-permute-start.7 = (bf16[2,4,544,128]{3,2,1,0:T(8,128)(2,1)S(1)}, bf16[2,4,544,128]{3,2,1,0:T(8,128)(2,1)S(1)}, u32[]{:S(2)}, u32[]{:S(2)}) collective-permute-start(bf16[2,4,544,128]{3,2,1,0:T(8,128)(2,1)S(1)} %get-tuple-element.26), channel_id=1, source_target_pairs={{0,8},{1,9},{2,10},{3,11},{4,12},{5,13},{6,14},{7,15},{8,0},{9,1},... | collective-permute-start | bytes 3342344 | tf_op jit(solution)/shard_map/ppermute | solution.py:56
  89.1 18.0 %collective-permute-start.8 = (bf16[2,4,544,128]{3,2,1,0:T(8,128)(2,1)S(1)}, bf16[2,4,544,128]{3,2,1,0:T(8,128)(2,1)S(1)}, u32[]{:S(2)}, u32[]{:S(2)}) collective-permute-start(bf16[2,4,544,128]{3,2,1,0:T(8,128)(2,1)S(1)} %get-tuple-element.27), channel_id=1, source_target_pairs={{0,248},{1,249},{2,250},{3,251},{4,252},{5,253},{6,254},{7,255},{8... | collective-permute-start | bytes 3342344 | tf_op jit(solution)/shard_map/ppermute | solution.py:56
  111.1 13.0 %collective-permute-start.13 = (f32[3,2,128,128]{3,2,1,0:T(8,128)S(1)}, f32[3,2,128,128]{3,2,1,0:T(8,128)S(1)}, u32[]{:S(2)}, u32[]{:S(2)}) collective-permute-start(f32[3,2,128,128]{3,2,1,0:T(8,128)S(1)} %get-tuple-element.34), channel_id=1, source_target_pairs={{0,256},{1,257},{2,258},{3,259},{4,260},{5,261},{6,262},{7,263},{8... | collective-permute-start | bytes 1179656 | tf_op jit(solution)/shard_map/ppermute | solution.py:56
  117.1 14.5 %collective-permute-start.12 = (f32[3,2,128,128]{3,2,1,0:T(8,128)S(1)}, f32[3,2,128,128]{3,2,1,0:T(8,128)S(1)}, u32[]{:S(2)}, u32[]{:S(2)}) collective-permute-start(f32[3,2,128,128]{3,2,1,0:T(8,128)S(1)} %get-tuple-element.32), channel_id=1, source_target_pairs={{0,256},{1,257},{2,258},{3,259},{4,260},{5,261},{6,262},{7,263},{8... | collective-permute-start | bytes 1179656 | tf_op jit(solution)/shard_map/ppermute | solution.py:56

commit v5 on v4

--- a/solution.py
+++ b/solution.py
@@ -9,10 +9,10 @@
 
 BF16, F32, I32 = jnp.bfloat16, jnp.float32, jnp.int32
 T = 128
-EDGE = (0, 0)
 MULT = (3 << 30, 3 << 30)
-LEFT = 5700000000
+LEFT = 4 * 10**9
 SORT = 0
+EDGE = 0
 BEGIN = 0
 LIMIT = 48 << 20
 BLOCK = 12 * T + 16
@@ -201,29 +201,49 @@
 EDGE_ROWS = 2 * (HEAD + TAIL)
 
 
-def edge_kernel(place, own, up, down, far0, far1, to_core, to_halo):
-    b, core = place[2], place[3]
-    for out, start in ((to_core, 1 - core), (to_halo, core)):
-        for source, panel in ((own, b), (up, (b + 3) % 4), (down, (b + 1) % 4), (None, (b + 2) % 4)):
-            for h in range(2):
-                held = (far0, far1)[h] if source is None else source
-                base = 0 if source is None else h * PIECE
+def edge_kernel(near, place, *refs):
+    core = place[3]
+    for out, start in ((refs[-2], 1 - core), (refs[-1], core)):
+        for h in range(2):
+            for n, held in enumerate(refs[:3] if near else refs[h : h + 1]):
+                base = h * PIECE if near else 0
                 for first, size, into in ((0, HEAD, 0), (3 * HEAD, TAIL, 2 * HEAD)):
                     begin = pl.multiple_of(base + first + start * size, 16)
-                    out[h, panel, into : into + 2 * size, :] = held[pl.ds(begin, 2 * size), :]
-
-
-def edges(flops, place, *sources):
-    shape = jax.ShapeDtypeStruct((2, 4, EDGE_ROWS, T), BF16)
-    return pl.pallas_call(
-        edge_kernel,
+                    out[h, n, into : into + 2 * size, :] = held[pl.ds(begin, 2 * size), :]
+
+
+def edges(near, place, *sources):
+    shape = jax.ShapeDtypeStruct((2, 3 if near else 1, EDGE_ROWS, T), BF16)
+    return pl.pallas_call(
+        functools.partial(edge_kernel, near),
         out_shape=[shape, shape],
-        in_specs=[SMEM] + [VMEM] * 5,
+        in_specs=[SMEM] + [VMEM] * len(sources),
         out_specs=[VMEM] * 2,
         compiler_params=params(),
-        cost_estimate=cost(flops, 4 << 20),
-        name="edges",
+        cost_estimate=cost(EDGE if near else 0, 4 << 20),
+        name="near_edges" if near else "far_edges",
     )(place, *sources)
+
+
+def edge_panels(place, shift):
+    core, b = place[3], place[2]
+    beside = ((place[6] + 2 * core + 15) % 16 // 4 + shift) % 4
+    inside = (b + shift) % 4
+    return jnp.where(core == 0, beside, inside), jnp.where(core == 0, inside, beside)
+
+
+def place_edges(place, h, n, from_core, from_halo, right, at, slots, clear):
+    core = place[3]
+    for k, slot in zip((0, 1, 5, 6), slots):
+        row, low = (k, True) if k < 2 else (k - 5, False)
+        above, below = (from_halo, from_core) if low else (from_core, from_halo)
+
+        def edge(first, size, above=above, below=below):
+            rows = slice(first, first + size)
+            return jnp.where(core == 0, above[h, n, rows, :], below[h, n, rows, :])
+
+        tail = 2 * HEAD + row * TAIL
+        place_row(k, edge(row * HEAD, T), edge(tail, T), edge(tail + T, 16), right, at, slot, clear)
 
 
 def place_row(k, v0, v1, keys, right, at, row, clear):
@@ -240,70 +260,63 @@
         right[into] = (v0 * pick[0] + w0 * pick[1]) + (v1 * pick[2] + w1 * pick[3])
 
 
-def begin_kernel(h, place, own, up, down, far0, far1, left, out, right):
+def begin_kernel(h, place, own, up, down, far0, far1, near_core, near_halo, left, out, right):
     sums = [None] * 3
-    for p, (source, shift) in enumerate(((own, 0), (up, 3), (down, 1), (None, 2))):
+    for n, (source, shift) in enumerate(((own, 0), (up, 3), (down, 1), (None, 2))):
         panel = (place[2] + shift) % 4
         held = (far0, far1)[h] if source is None else source
         base = 0 if source is None else h * PIECE
+        low, high = edge_panels(place, shift)
         for r in range(3):
             head = base + r * HEAD
             tail = base + 3 * HEAD + r * TAIL
             keys = held[tail + T : tail + TAIL, :]
-            place_row(r + 2, held[head : head + T, :], held[tail : tail + T, :], keys, right, p % 2, r, p < 2)
+            place_row(r + 2, held[head : head + T, :], held[tail : tail + T, :], keys, right, n % 2, r + 2, n < 2)
+        if n < 3:
+            place_edges(place, h, n, near_core, near_halo, right, n % 2, (0, 1, 5, 6), n < 2)
         for i in range(3):
             first = i // 2 * T
-            part = jnp.dot(
-                left[i, panel, :, (2 - i) * T : (5 - i) * T],
-                right[p % 2, :, first : first + 3 * T],
-                preferred_element_type=F32,
-            )
+            side = left[i, panel, :, (2 - i) * T : (5 - i) * T]
+            rows = slice(2 * T, 5 * T)
+            if n < 3:
+                parts = [side]
+                if i < 2:
+                    parts = [left[i, low, :, : (2 - i) * T]] + parts
+                if i > 0:
+                    parts = parts + [left[i, high, :, (5 - i) * T :]]
+                side = jnp.concatenate(parts, axis=1)
+                rows = slice(i * T, (i + 5) * T)
+            part = jnp.dot(side, right[n % 2, rows, first : first + 3 * T], preferred_element_type=F32)
             sums[i] = part if sums[i] is None else sums[i] + part
     for i in range(3):
         out[i] = sums[i]
 
 
-def begin(flops, h, place, pieces, left):
+def begin(flops, h, place, pieces, near, left):
     return pl.pallas_call(
         functools.partial(begin_kernel, h),
         out_shape=jax.ShapeDtypeStruct((3, 2 * T, 3 * T), F32),
-        in_specs=[SMEM] + [VMEM] * 6,
+        in_specs=[SMEM] + [VMEM] * 8,
         out_specs=VMEM,
-        scratch_shapes=[pltpu.VMEM((2, 3 * T, 4 * T), BF16)],
+        scratch_shapes=[pltpu.VMEM((2, 7 * T, 4 * T), BF16)],
         compiler_params=params(),
         cost_estimate=cost(flops, 6 << 20),
         name="begin",
-    )(place, *pieces, left)
+    )(place, *pieces, *near, left)
 
 
 def multiply_kernel(h, place, from_core, from_halo, begun, left, mine, partner, keep, give, right):
-    b, core = place[2], place[3]
     half = (lanes() >= T // 2).astype(F32)
-    sums = [begun[i] for i in range(3)]
-    for panel in range(4):
-
-        def edge(first, size, low, panel=panel):
-            rows = slice(first, first + size)
-            above, below = (from_halo, from_core) if low else (from_core, from_halo)
-            return jnp.where(core == 0, above[h, panel, rows, :], below[h, panel, rows, :])
-
-        for n, k in enumerate((0, 1, 5, 6)):
-            row, low = n % 2, n < 2
-            tail = 2 * HEAD + row * TAIL
-            keys = edge(tail + T, 16, low)
-            place_row(k, edge(row * HEAD, T, low), edge(tail, T, low), keys, right, panel % 2, n, panel < 2)
-        for i in range(3):
-            first = i // 2 * T
-            side = left[i, panel]
-            if i == 1:
-                side = jnp.concatenate([side[:, :T], side[:, 4 * T :]], axis=1)
-            else:
-                side = side[:, : 2 * T] if i == 0 else side[:, 3 * T :]
-            sums[i] = sums[i] + jnp.dot(
-                side,
-                right[panel % 2, i * T : (i + 2) * T, first : first + 3 * T],
-                preferred_element_type=F32,
-            )
+    low, high = edge_panels(place, 2)
+    place_edges(place, h, 0, from_core, from_halo, right, 0, (0, 1, 2, 3), True)
+    sums = []
+    for i in range(3):
+        first = i // 2 * T
+        parts = [left[i, low, :, : (2 - i) * T]] if i < 2 else []
+        parts += [left[i, high, :, (5 - i) * T :]] if i > 0 else []
+        side = jnp.concatenate(parts, axis=1) if len(parts) > 1 else parts[0]
+        part = jnp.dot(side, right[0, i * T : (i + 2) * T, first : first + 3 * T], preferred_element_type=F32)
+        sums.append(begun[i] + part)
     for i in range(3):
         for side, (out, source) in enumerate(((keep, mine), (give, partner))):
             keys = source[...].astype(F32)[4 * i : 4 * i + 4] + float(i + 2)
@@ -327,7 +340,7 @@
         out_shape=[shape, shape],
         in_specs=[SMEM] + [VMEM] * 6,
         out_specs=[VMEM, VMEM],
-        scratch_shapes=[pltpu.VMEM((2, 4 * T, 4 * T), BF16)],
+        scratch_shapes=[pltpu.VMEM((1, 4 * T, 4 * T), BF16)],
         compiler_params=params(),
         cost_estimate=cost(flops, 10 << 20),
         name="multiply",
@@ -362,7 +375,7 @@
 
 def body(x_tiles, tile_cols, tile_counts):
     row, col = lax.axis_index("row"), lax.axis_index("col")
-    place = jnp.stack([row, row // 32, row // 8 % 4, row % 2, col // 2, col % 2]).astype(I32)
+    place = jnp.stack([row, row // 32, row // 8 % 4, row % 2, col // 2, col % 2, row // 2 % 16]).astype(I32)
     block, whole, keys = pack(place, tile_cols, tile_counts, x_tiles)
     up, down = send(whole, along_z(4)), send(whole, along_z(-4))
     g1, g3, g2 = send(block, along_x(1)), send(block, along_x(-1)), send(block, along_x(2))
@@ -371,9 +384,11 @@
     r1, rm, r2 = send(other, along_y(1)), send(other, along_y(-1)), send(same, along_y(2))
     left, partner = left_panels(place, same, r1, rm, r2)
     pieces = (whole, up, down, *far)
-    to_core, to_halo = edges(EDGE[0], place, *pieces)
-    received = (send(to_core, CORE), send(to_halo, HALO))
-    begun = [begin(BEGIN, h, place, pieces, left) for h in range(2)]
+    near_core, near_halo = edges(True, place, whole, up, down)
+    near = (send(near_core, CORE), send(near_halo, HALO))
+    far_core, far_halo = edges(False, place, *far)
+    received = (send(far_core, CORE), send(far_halo, HALO))
+    begun = [begin(BEGIN, h, place, pieces, near, left) for h in range(2)]
     kept, got = [], []
     for h in range(2):
         keep, give = multiply(MULT[h], h, place, received, begun[h], left, keys, partner)

time: 133 us -> 142 us (1.068)
  the two profiles are of different devices: /device:TPU:107 before, /device:TPU:33 now
where the time goes in v5:
time: 142 us; the launch traced here: 141 us
  starting transfers between devices  68.9 us (49%)
  waiting for transfers between devices  44.8 us (32%)
  Pallas kernels  24.6 us (17%)
  local copies, waits for them, and re-layouts  2.45 us (2%)
    ppermute x16, starting transfers between devices, send(): return lax.ppermute(block, ('row', 'col'), pairs)  68.9 us
    ppermute x16, waiting for transfers between devices, send(): return lax.ppermute(block, ('row', 'col'), pairs)  44.8 us
    pallas_call x2, Pallas kernels, begin(): pl.pallas_call(functools.partial(begin_kernel, h), out_shape=jax.ShapeDty...  10.4 us
    pallas_call x2, Pallas kernels, multiply(): pl.pallas_call(functools.partial(multiply_kernel, h), out_shape=[shape, s...  5.97 us
    pallas_call x1, Pallas kernels, left_panels(): pl.pallas_call(left_kernel, out_shape=[jax.ShapeDtypeStruct((3, 4, 2 * T,...  4.59 us
  transfers between devices with their start and end apart: 16, of which 5 were waited for; matrix products, arithmetic and copies ran while one was open for 0% of the time, Pallas kernels for 14%

profile of v5, /device:TPU:33, one launch (start us, length us, event | category | flops | bytes accessed | tf_op | source)
XLA Modules:
  0.0 141.0 jit_solution(8093498988704448412)
XLA Ops:
  0.0 0.1 stack.31.place
  0.1 0.0 copy-start
  0.1 1.0 copy-done
  1.1 0.0 copy-start.1
  1.1 0.7 copy-done.1
  1.8 0.0 copy-start.2
  1.8 0.7 copy-done.2
  2.4 0.8 pack.1
  3.3 3.1 %collective-permute-start.1 = (bf16[1552,128]{1,0:T(8,128)(2,1)S(1)}, bf16[1552,128]{1,0:T(8,128)(2,1)S(1)}, u32[]{:S(2)}, u32[]{:S(2)}) collective-permute-start(bf16[1552,128]{1,0:T(8,128)(2,1)S(1)} %get-tuple-element.23.own), channel_id=1, source_target_pairs={{0,2},{1,3},{2,4},{3,5},{4,6},{5,7},{6,0},{7,1},{8,10},{9,11},{10,... | collective-permute-start | bytes 1191944 | tf_op jit(solution)/shard_map/ppermute | solution.py:56
  6.4 4.4 %collective-permute-start.2 = (bf16[1552,128]{1,0:T(8,128)(2,1)S(1)}, bf16[1552,128]{1,0:T(8,128)(2,1)S(1)}, u32[]{:S(2)}, u32[]{:S(2)}) collective-permute-start(bf16[1552,128]{1,0:T(8,128)(2,1)S(1)} %get-tuple-element.23.own), channel_id=1, source_target_pairs={{0,4},{1,5},{2,6},{3,7},{4,0},{5,1},{6,2},{7,3},{8,12},{9,13},{10,... | collective-permute-start | bytes 1191944 | tf_op jit(solution)/shard_map/ppermute | solution.py:56
  10.7 3.1 %collective-permute-start.3 = (bf16[1552,128]{1,0:T(8,128)(2,1)S(1)}, bf16[1552,128]{1,0:T(8,128)(2,1)S(1)}, u32[]{:S(2)}, u32[]{:S(2)}) collective-permute-start(bf16[1552,128]{1,0:T(8,128)(2,1)S(1)} %get-tuple-element.23.own), channel_id=1, source_target_pairs={{0,6},{1,7},{2,0},{3,1},{4,2},{5,3},{6,4},{7,5},{8,14},{9,15},{10,... | collective-permute-start | bytes 1191944 | tf_op jit(solution)/shard_map/ppermute | solution.py:56
  13.8 11.6 %collective-permute-start.5 = (bf16[1632,128]{1,0:T(8,128)(2,1)S(1)}, bf16[1632,128]{1,0:T(8,128)(2,1)S(1)}, u32[]{:S(2)}, u32[]{:S(2)}) collective-permute-start(bf16[1632,128]{1,0:T(8,128)(2,1)S(1)} %get-tuple-element.22.refs_0_.own), channel_id=1, source_target_pairs={{0,192},{1,193},{2,194},{3,195},{4,196},{5,197},{6,198},{7,199},{8... | collective-permute-start | bytes 1253384 | tf_op jit(solution)/shard_map/ppermute | solution.py:56
  25.4 1.9 %collective-permute-start = (bf16[1632,128]{1,0:T(8,128)(2,1)S(1)}, bf16[1632,128]{1,0:T(8,128)(2,1)S(1)}, u32[]{:S(2)}, u32[]{:S(2)}) collective-permute-start(bf16[1632,128]{1,0:T(8,128)(2,1)S(1)} %get-tuple-element.22.refs_0_.own), channel_id=1, source_target_pairs={{0,64},{1,65},{2,66},{3,67},{4,68},{5,69},{6,70},{7,71},{8,72},{9,... | collective-permute-start | bytes 1253384 | tf_op jit(solution)/shard_map/ppermute | solution.py:56
  27.3 0.0 collective-permute-done.1.g1
  27.3 0.0 collective-permute-done.2.g2
  27.3 0.1 collective-permute-done.3.g3
  27.5 0.7 sort_panels.1
  28.2 3.2 %collective-permute-start.11 = (bf16[3120,128]{1,0:T(8,128)(2,1)S(1)}, bf16[3120,128]{1,0:T(8,128)(2,1)S(1)}, u32[]{:S(2)}, u32[]{:S(2)}) collective-permute-start(bf16[3120,128]{1,0:T(8,128)(2,1)S(1)} %get-tuple-element.25), channel_id=1, source_target_pairs={{0,256},{1,257},{2,258},{3,259},{4,260},{5,261},{6,262},{7,263},{8... | collective-permute-start | bytes 2396168 | tf_op jit(solution)/shard_map/ppermute | solution.py:56
  31.4 3.4 %collective-permute-start.12 = (bf16[3120,128]{1,0:T(8,128)(2,1)S(1)}, bf16[3120,128]{1,0:T(8,128)(2,1)S(1)}, u32[]{:S(2)}, u32[]{:S(2)}) collective-permute-start(bf16[3120,128]{1,0:T(8,128)(2,1)S(1)} %get-tuple-element.25), channel_id=1, source_target_pairs={{0,257},{1,256},{2,259},{3,258},{4,261},{5,260},{6,263},{7,262},{8... | collective-permute-start | bytes 2396168 | tf_op jit(solution)/shard_map/ppermute | solution.py:56
  34.8 3.5 %collective-permute-start.13 = (bf16[3104,128]{1,0:T(8,128)(2,1)S(1)}, bf16[3104,128]{1,0:T(8,128)(2,1)S(1)}, u32[]{:S(2)}, u32[]{:S(2)}) collective-permute-start(bf16[3104,128]{1,0:T(8,128)(2,1)S(1)} %get-tuple-element.32.same), channel_id=1, source_target_pairs={{0,1},{1,0},{2,3},{3,2},{4,5},{5,4},{6,7},{7,6},{8,9},{9,8},{10,11... | collective-permute-start | bytes 2383880 | tf_op jit(solution)/shard_map/ppermute | solution.py:56
  38.3 15.8 %collective-permute-done.5.refs_2_.down = bf16[1632,128]{1,0:T(8,128)(2,1)S(1)} collective-permute-done((bf16[1632,128]{1,0:T(8,128)(2,1)S(1)}, bf16[1632,128]{1,0:T(8,128)(2,1)S(1)}, u32[]{:S(2)}, u32[]{:S(2)}) %collective-permute-start.5) | collective-permute-done | bytes 417824 | tf_op jit(solution)/shard_map/ppermute | solution.py:56
  54.2 15.8 %collective-permute-start.6 = (bf16[816,128]{1,0:T(8,128)(2,1)S(1)}, bf16[816,128]{1,0:T(8,128)(2,1)S(1)}, u32[]{:S(2)}, u32[]{:S(2)}) collective-permute-start(bf16[816,128]{1,0:T(8,128)(2,1)S(1)} %slice.9), channel_id=1, source_target_pairs={{0,192},{1,193},{2,194},{3,195},{4,196},{5,197},{6,198},{7,199},{8... | collective-permute-start | bytes 626696 | tf_op jit(solution)/shard_map/ppermute | solution.py:56
  70.0 0.0 collective-permute-done.refs_1_.up
  70.0 1.9 %collective-permute-start.4 = (bf16[816,128]{1,0:T(8,128)(2,1)S(1)}, bf16[816,128]{1,0:T(8,128)(2,1)S(1)}, u32[]{:S(2)}, u32[]{:S(2)}) collective-permute-start(bf16[816,128]{1,0:T(8,128)(2,1)S(1)} %slice.8), channel_id=1, source_target_pairs={{0,64},{1,65},{2,66},{3,67},{4,68},{5,69},{6,70},{7,71},{8,72},{9,... | collective-permute-start | bytes 626696 | tf_op jit(solution)/shard_map/ppermute | solution.py:56
  71.9 0.7 near_edges.1
  72.6 11.9 %collective-permute-done.6.refs_1_.far1 = bf16[816,128]{1,0:T(8,128)(2,1)S(1)} collective-permute-done((bf16[816,128]{1,0:T(8,128)(2,1)S(1)}, bf16[816,128]{1,0:T(8,128)(2,1)S(1)}, u32[]{:S(2)}, u32[]{:S(2)}) %collective-permute-start.6) | collective-permute-done | bytes 208928 | tf_op jit(solution)/shard_map/ppermute | solution.py:56
  84.5 2.1 %collective-permute-start.10 = (bf16[2,3,544,128]{3,2,1,0:T(8,128)(2,1)S(1)}, bf16[2,3,544,128]{3,2,1,0:T(8,128)(2,1)S(1)}, u32[]{:S(2)}, u32[]{:S(2)}) collective-permute-start(bf16[2,3,544,128]{3,2,1,0:T(8,128)(2,1)S(1)} %get-tuple-element.31), channel_id=1, source_target_pairs={{0,248},{1,249},{2,250},{3,251},{4,252},{5,253},{6,254},{7,255},{8... | collective-permute-start | bytes 2506760 | tf_op jit(solution)/shard_map/ppermute | solution.py:56
  86.6 6.5 %collective-permute-done.4.refs_0_.far0 = bf16[816,128]{1,0:T(8,128)(2,1)S(1)} collective-permute-done((bf16[816,128]{1,0:T(8,128)(2,1)S(1)}, bf16[816,128]{1,0:T(8,128)(2,1)S(1)}, u32[]{:S(2)}, u32[]{:S(2)}) %collective-permute-start.4) | collective-permute-done | bytes 208928 | tf_op jit(solution)/shard_map/ppermute | solution.py:56
  93.1 4.3 %collective-permute-start.9 = (bf16[2,3,544,128]{3,2,1,0:T(8,128)(2,1)S(1)}, bf16[2,3,544,128]{3,2,1,0:T(8,128)(2,1)S(1)}, u32[]{:S(2)}, u32[]{:S(2)}) collective-permute-start(bf16[2,3,544,128]{3,2,1,0:T(8,128)(2,1)S(1)} %get-tuple-element.30), channel_id=1, source_target_pairs={{0,8},{1,9},{2,10},{3,11},{4,12},{5,13},{6,14},{7,15},{8,0},{9,1},... | collective-permute-start | bytes 2506760 | tf_op jit(solution)/shard_map/ppermute | solution.py:56
  97.4 0.6 far_edges.1
  98.0 0.0 collective-permute-done.13.r2
  98.0 1.9 %collective-permute-start.7 = (bf16[2,1,544,128]{3,2,1,0:T(8,128)(2,1)S(1)}, bf16[2,1,544,128]{3,2,1,0:T(8,128)(2,1)S(1)}, u32[]{:S(2)}, u32[]{:S(2)}) collective-permute-start(bf16[2,1,544,128]{3,2,1,0:T(8,128)(2,1)S(1)} %get-tuple-element.28), channel_id=1, source_target_pairs={{0,8},{1,9},{2,10},{3,11},{4,12},{5,13},{6,14},{7,15},{8,0},{9,1},... | collective-permute-start | bytes 835592 | tf_op jit(solution)/shard_map/ppermute | solution.py:56
  100.0 0.0 collective-permute-done.11.r1
  100.0 3.4 %collective-permute-start.8 = (bf16[2,1,544,128]{3,2,1,0:T(8,128)(2,1)S(1)}, bf16[2,1,544,128]{3,2,1,0:T(8,128)(2,1)S(1)}, u32[]{:S(2)}, u32[]{:S(2)}) collective-permute-start(bf16[2,1,544,128]{3,2,1,0:T(8,128)(2,1)S(1)} %get-tuple-element.29), channel_id=1, source_target_pairs={{0,248},{1,249},{2,250},{3,251},{4,252},{5,253},{6,254},{7,255},{8... | collective-permute-start | bytes 835592 | tf_op jit(solution)/shard_map/ppermute | solution.py:56
  103.4 0.0 collective-permute-done.12.rm
  103.4 4.6 %left_panels.1 = (bf16[3,4,256,640]{3,2,1,0:T(8,128)(2,1)}, bf16[16,128]{1,0:T(8,128)(2,1)S(1)}) custom-call(s32[7]{0:T(128)S(1)} %stack.31.place, bf16[3104,128]{1,0:T(8,128)(2,1)S(1)} %get-tuple-element.32.same, bf16[3120,128]{1,0:T(8,128)(2,1)S(1)} %collective-permute-done.11.r1, bf16[3120,128]{1,0:T(8,128)(2,1)S(1)} %collective-permute-done.12.rm, ...), custom_call_target="tpu_custom_call" | custom-call | flops 4000000000 | bytes 8388608 | tf_op jit(solution)/shard_map/left_panels/pallas_call | solution.py:187
  108.0 0.0 collective-permute-done.10.near_halo
  108.0 0.0 collective-permute-done.9.near_core
  108.0 5.2 %begin.3.begun = f32[3,256,384]{2,1,0:T(8,128)S(1)} custom-call(s32[7]{0:T(128)S(1)} %stack.31.place, bf16[1632,128]{1,0:T(8,128)(2,1)S(1)} %get-tuple-element.22.refs_0_.own, bf16[1632,128]{1,0:T(8,128)(2,1)S(1)} %collective-permute-done.refs_1_.up, bf16[1632,128]{1,0:T(8,128)(2,1)S(1)} %collective-permute-done.5.refs_2_.down, ...), custom_call_target="tpu_custom_call" | custom-call | bytes 6291456 | tf_op jit(solution)/shard_map/begin/pallas_call | solution.py:296
  113.2 0.0 collective-permute-done.7.from_core
  113.2 0.0 collective-permute-done.8.from_halo
  113.2 3.0 %multiply.3 = (f32[3,2,128,128]{3,2,1,0:T(8,128)S(1)}, f32[3,2,128,128]{3,2,1,0:T(8,128)S(1)}) custom-call(s32[7]{0:T(128)S(1)} %stack.31.place, bf16[2,1,544,128]{3,2,1,0:T(8,128)(2,1)S(1)} %collective-permute-done.7.from_core, bf16[2,1,544,128]{3,2,1,0:T(8,128)(2,1)S(1)} %collective-permute-done.8.from_halo, f32[3,256,384]{2,1,0:T(8,128)S(1)} %begin.3.begun, ...), custom_call_target="tpu_custom_call" | custom-call | flops 3221225472 | bytes 10485760 | tf_op jit(solution)/shard_map/multiply/pallas_call | solution.py:338
  116.2 3.2 %collective-permute-start.15 = (f32[3,2,128,128]{3,2,1,0:T(8,128)S(1)}, f32[3,2,128,128]{3,2,1,0:T(8,128)S(1)}, u32[]{:S(2)}, u32[]{:S(2)}) collective-permute-start(f32[3,2,128,128]{3,2,1,0:T(8,128)S(1)} %get-tuple-element.38), channel_id=1, source_target_pairs={{0,256},{1,257},{2,258},{3,259},{4,260},{5,261},{6,262},{7,263},{8... | collective-permute-start | bytes 1179656 | tf_op jit(solution)/shard_map/ppermute | solution.py:56
  119.4 5.2 %begin.2.begun = f32[3,256,384]{2,1,0:T(8,128)S(1)} custom-call(s32[7]{0:T(128)S(1)} %stack.31.place, bf16[1632,128]{1,0:T(8,128)(2,1)S(1)} %get-tuple-element.22.refs_0_.own, bf16[1632,128]{1,0:T(8,128)(2,1)S(1)} %collective-permute-done.refs_1_.up, bf16[1632,128]{1,0:T(8,128)(2,1)S(1)} %collective-permute-done.5.refs_2_.down, ...), custom_call_target="tpu_custom_call" | custom-call | bytes 6291456 | tf_op jit(solution)/shard_map/begin/pallas_call | solution.py:296
  124.6 3.0 %multiply.2 = (f32[3,2,128,128]{3,2,1,0:T(8,128)S(1)}, f32[3,2,128,128]{3,2,1,0:T(8,128)S(1)}) custom-call(s32[7]{0:T(128)S(1)} %stack.31.place, bf16[2,1,544,128]{3,2,1,0:T(8,128)(2,1)S(1)} %collective-permute-done.7.from_core, bf16[2,1,544,128]{3,2,1,0:T(8,128)(2,1)S(1)} %collective-permute-done.8.from_halo, f32[3,256,384]{2,1,0:T(8,128)S(1)} %begin.2.begun, ...), custom_call_target="tpu_custom_call" | custom-call | flops 3221225472 | bytes 10485760 | tf_op jit(solution)/shard_map/multiply/pallas_call | solution.py:338
  127.6 2.1 %collective-permute-start.14 = (f32[3,2,128,128]{3,2,1,0:T(8,128)S(1)}, f32[3,2,128,128]{3,2,1,0:T(8,128)S(1)}, u32[]{:S(2)}, u32[]{:S(2)}) collective-permute-start(f32[3,2,128,128]{3,2,1,0:T(8,128)S(1)} %get-tuple-element.36), channel_id=1, source_target_pairs={{0,256},{1,257},{2,258},{3,259},{4,260},{5,261},{6,262},{7,263},{8... | collective-permute-start | bytes 1179656 | tf_op jit(solution)/shard_map/ppermute | solution.py:56
  129.7 0.0 collective-permute-done.15.got1
  129.7 10.4 %collective-permute-done.14.got0 = f32[3,2,128,128]{3,2,1,0:T(8,128)S(1)} collective-permute-done((f32[3,2,128,128]{3,2,1,0:T(8,128)S(1)}, f32[3,2,128,128]{3,2,1,0:T(8,128)S(1)}, u32[]{:S(2)}, u32[]{:S(2)}) %collective-permute-start.14) | collective-permute-done | bytes 393248 | tf_op jit(solution)/shard_map/ppermute | solution.py:56
  140.1 0.9 finish.1
  (2 shorter events, 0.0 us)
Async XLA Ops:
  0.1 1.0 copy-start
  1.1 0.7 copy-start.1
  1.8 0.7 copy-start.2
  3.3 24.1 %collective-permute-start.1 = (bf16[1552,128]{1,0:T(8,128)(2,1)S(1)}, bf16[1552,128]{1,0:T(8,128)(2,1)S(1)}, u32[]{:S(2)}, u32[]{:S(2)}) collective-permute-start(bf16[1552,128]{1,0:T(8,128)(2,1)S(1)} %get-tuple-element.23.own), channel_id=1, source_target_pairs={{0,2},{1,3},{2,4},{3,5},{4,6},{5,7},{6,0},{7,1},{8,10},{9,11},{10,... | collective-permute-start | bytes 1191944 | tf_op jit(solution)/shard_map/ppermute | solution.py:56
  6.4 20.9 %collective-permute-start.2 = (bf16[1552,128]{1,0:T(8,128)(2,1)S(1)}, bf16[1552,128]{1,0:T(8,128)(2,1)S(1)}, u32[]{:S(2)}, u32[]{:S(2)}) collective-permute-start(bf16[1552,128]{1,0:T(8,128)(2,1)S(1)} %get-tuple-element.23.own), channel_id=1, source_target_pairs={{0,4},{1,5},{2,6},{3,7},{4,0},{5,1},{6,2},{7,3},{8,12},{9,13},{10,... | collective-permute-start | bytes 1191944 | tf_op jit(solution)/shard_map/ppermute | solution.py:56
  10.7 16.7 %collective-permute-start.3 = (bf16[1552,128]{1,0:T(8,128)(2,1)S(1)}, bf16[1552,128]{1,0:T(8,128)(2,1)S(1)}, u32[]{:S(2)}, u32[]{:S(2)}) collective-permute-start(bf16[1552,128]{1,0:T(8,128)(2,1)S(1)} %get-tuple-element.23.own), channel_id=1, source_target_pairs={{0,6},{1,7},{2,0},{3,1},{4,2},{5,3},{6,4},{7,5},{8,14},{9,15},{10,... | collective-permute-start | bytes 1191944 | tf_op jit(solution)/shard_map/ppermute | solution.py:56
  13.8 40.3 %collective-permute-start.5 = (bf16[1632,128]{1,0:T(8,128)(2,1)S(1)}, bf16[1632,128]{1,0:T(8,128)(2,1)S(1)}, u32[]{:S(2)}, u32[]{:S(2)}) collective-permute-start(bf16[1632,128]{1,0:T(8,128)(2,1)S(1)} %get-tuple-element.22.refs_0_.own), channel_id=1, source_target_pairs={{0,192},{1,193},{2,194},{3,195},{4,196},{5,197},{6,198},{7,199},{8... | collective-permute-start | bytes 1253384 | tf_op jit(solution)/shard_map/ppermute | solution.py:56
  25.4 44.6 %collective-permute-start = (bf16[1632,128]{1,0:T(8,128)(2,1)S(1)}, bf16[1632,128]{1,0:T(8,128)(2,1)S(1)}, u32[]{:S(2)}, u32[]{:S(2)}) collective-permute-start(bf16[1632,128]{1,0:T(8,128)(2,1)S(1)} %get-tuple-element.22.refs_0_.own), channel_id=1, source_target_pairs={{0,64},{1,65},{2,66},{3,67},{4,68},{5,69},{6,70},{7,71},{8,72},{9,... | collective-permute-start | bytes 1253384 | tf_op jit(solution)/shard_map/ppermute | solution.py:56
  28.2 71.8 %collective-permute-start.11 = (bf16[3120,128]{1,0:T(8,128)(2,1)S(1)}, bf16[3120,128]{1,0:T(8,128)(2,1)S(1)}, u32[]{:S(2)}, u32[]{:S(2)}) collective-permute-start(bf16[3120,128]{1,0:T(8,128)(2,1)S(1)} %get-tuple-element.25), channel_id=1, source_target_pairs={{0,256},{1,257},{2,258},{3,259},{4,260},{5,261},{6,262},{7,263},{8... | collective-permute-start | bytes 2396168 | tf_op jit(solution)/shard_map/ppermute | solution.py:56
  31.4 72.0 %collective-permute-start.12 = (bf16[3120,128]{1,0:T(8,128)(2,1)S(1)}, bf16[3120,128]{1,0:T(8,128)(2,1)S(1)}, u32[]{:S(2)}, u32[]{:S(2)}) collective-permute-start(bf16[3120,128]{1,0:T(8,128)(2,1)S(1)} %get-tuple-element.25), channel_id=1, source_target_pairs={{0,257},{1,256},{2,259},{3,258},{4,261},{5,260},{6,263},{7,262},{8... | collective-permute-start | bytes 2396168 | tf_op jit(solution)/shard_map/ppermute | solution.py:56
  34.8 63.2 %collective-permute-start.13 = (bf16[3104,128]{1,0:T(8,128)(2,1)S(1)}, bf16[3104,128]{1,0:T(8,128)(2,1)S(1)}, u32[]{:S(2)}, u32[]{:S(2)}) collective-permute-start(bf16[3104,128]{1,0:T(8,128)(2,1)S(1)} %get-tuple-element.32.same), channel_id=1, source_target_pairs={{0,1},{1,0},{2,3},{3,2},{4,5},{5,4},{6,7},{7,6},{8,9},{9,8},{10,11... | collective-permute-start | bytes 2383880 | tf_op jit(solution)/shard_map/ppermute | solution.py:56
  54.2 30.3 %collective-permute-start.6 = (bf16[816,128]{1,0:T(8,128)(2,1)S(1)}, bf16[816,128]{1,0:T(8,128)(2,1)S(1)}, u32[]{:S(2)}, u32[]{:S(2)}) collective-permute-start(bf16[816,128]{1,0:T(8,128)(2,1)S(1)} %slice.9), channel_id=1, source_target_pairs={{0,192},{1,193},{2,194},{3,195},{4,196},{5,197},{6,198},{7,199},{8... | collective-permute-start | bytes 626696 | tf_op jit(solution)/shard_map/ppermute | solution.py:56
  70.0 23.1 %collective-permute-start.4 = (bf16[816,128]{1,0:T(8,128)(2,1)S(1)}, bf16[816,128]{1,0:T(8,128)(2,1)S(1)}, u32[]{:S(2)}, u32[]{:S(2)}) collective-permute-start(bf16[816,128]{1,0:T(8,128)(2,1)S(1)} %slice.8), channel_id=1, source_target_pairs={{0,64},{1,65},{2,66},{3,67},{4,68},{5,69},{6,70},{7,71},{8,72},{9,... | collective-permute-start | bytes 626696 | tf_op jit(solution)/shard_map/ppermute | solution.py:56
  84.5 23.5 %collective-permute-start.10 = (bf16[2,3,544,128]{3,2,1,0:T(8,128)(2,1)S(1)}, bf16[2,3,544,128]{3,2,1,0:T(8,128)(2,1)S(1)}, u32[]{:S(2)}, u32[]{:S(2)}) collective-permute-start(bf16[2,3,544,128]{3,2,1,0:T(8,128)(2,1)S(1)} %get-tuple-element.31), channel_id=1, source_target_pairs={{0,248},{1,249},{2,250},{3,251},{4,252},{5,253},{6,254},{7,255},{8... | collective-permute-start | bytes 2506760 | tf_op jit(solution)/shard_map/ppermute | solution.py:56
  93.1 14.9 %collective-permute-start.9 = (bf16[2,3,544,128]{3,2,1,0:T(8,128)(2,1)S(1)}, bf16[2,3,544,128]{3,2,1,0:T(8,128)(2,1)S(1)}, u32[]{:S(2)}, u32[]{:S(2)}) collective-permute-start(bf16[2,3,544,128]{3,2,1,0:T(8,128)(2,1)S(1)} %get-tuple-element.30), channel_id=1, source_target_pairs={{0,8},{1,9},{2,10},{3,11},{4,12},{5,13},{6,14},{7,15},{8,0},{9,1},... | collective-permute-start | bytes 2506760 | tf_op jit(solution)/shard_map/ppermute | solution.py:56
  98.0 15.2 %collective-permute-start.7 = (bf16[2,1,544,128]{3,2,1,0:T(8,128)(2,1)S(1)}, bf16[2,1,544,128]{3,2,1,0:T(8,128)(2,1)S(1)}, u32[]{:S(2)}, u32[]{:S(2)}) collective-permute-start(bf16[2,1,544,128]{3,2,1,0:T(8,128)(2,1)S(1)} %get-tuple-element.28), channel_id=1, source_target_pairs={{0,8},{1,9},{2,10},{3,11},{4,12},{5,13},{6,14},{7,15},{8,0},{9,1},... | collective-permute-start | bytes 835592 | tf_op jit(solution)/shard_map/ppermute | solution.py:56
  100.0 13.2 %collective-permute-start.8 = (bf16[2,1,544,128]{3,2,1,0:T(8,128)(2,1)S(1)}, bf16[2,1,544,128]{3,2,1,0:T(8,128)(2,1)S(1)}, u32[]{:S(2)}, u32[]{:S(2)}) collective-permute-start(bf16[2,1,544,128]{3,2,1,0:T(8,128)(2,1)S(1)} %get-tuple-element.29), channel_id=1, source_target_pairs={{0,248},{1,249},{2,250},{3,251},{4,252},{5,253},{6,254},{7,255},{8... | collective-permute-start | bytes 835592 | tf_op jit(solution)/shard_map/ppermute | solution.py:56
  116.2 13.5 %collective-permute-start.15 = (f32[3,2,128,128]{3,2,1,0:T(8,128)S(1)}, f32[3,2,128,128]{3,2,1,0:T(8,128)S(1)}, u32[]{:S(2)}, u32[]{:S(2)}) collective-permute-start(f32[3,2,128,128]{3,2,1,0:T(8,128)S(1)} %get-tuple-element.38), channel_id=1, source_target_pairs={{0,256},{1,257},{2,258},{3,259},{4,260},{5,261},{6,262},{7,263},{8... | collective-permute-start | bytes 1179656 | tf_op jit(solution)/shard_map/ppermute | solution.py:56
  127.6 12.5 %collective-permute-start.14 = (f32[3,2,128,128]{3,2,1,0:T(8,128)S(1)}, f32[3,2,128,128]{3,2,1,0:T(8,128)S(1)}, u32[]{:S(2)}, u32[]{:S(2)}) collective-permute-start(f32[3,2,128,128]{3,2,1,0:T(8,128)S(1)} %get-tuple-element.36), channel_id=1, source_target_pairs={{0,256},{1,257},{2,258},{3,259},{4,260},{5,261},{6,262},{7,263},{8... | collective-permute-start | bytes 1179656 | tf_op jit(solution)/shard_map/ppermute | solution.py:56

commit v6 on v4

--- a/solution.py
+++ b/solution.py
@@ -11,7 +11,7 @@
 T = 128
 EDGE = (0, 0)
 MULT = (3 << 30, 3 << 30)
-LEFT = 5700000000
+LEFT = 5600000000
 SORT = 0
 BEGIN = 0
 LIMIT = 48 << 20

time: 133 us -> 133 us (level)
  the two profiles are of different devices: /device:TPU:107 before, /device:TPU:6 now
where the time goes in v6:
time: 133 us; the launch traced here: 132 us
  starting transfers between devices  55.7 us (42%)
  waiting for transfers between devices  49.7 us (37%)
  Pallas kernels  24.1 us (18%)
  local copies, waits for them, and re-layouts  2.45 us (2%)
    ppermute x14, starting transfers between devices, send(): return lax.ppermute(block, ('row', 'col'), pairs)  55.7 us
    ppermute x14, waiting for transfers between devices, send(): return lax.ppermute(block, ('row', 'col'), pairs)  49.7 us
    pallas_call x2, Pallas kernels, begin(): pl.pallas_call(functools.partial(begin_kernel, h), out_shape=jax.ShapeDty...  8.32 us
    pallas_call x2, Pallas kernels, multiply(): pl.pallas_call(functools.partial(multiply_kernel, h), out_shape=[shape, s...  8.04 us
    pallas_call x1, Pallas kernels, left_panels(): pl.pallas_call(left_kernel, out_shape=[jax.ShapeDtypeStruct((3, 4, 2 * T,...  4.58 us
  transfers between devices with their start and end apart: 14, of which 9 were waited for; matrix products, arithmetic and copies ran while one was open for 0% of the time, Pallas kernels for 14%

profile of v6, /device:TPU:6, one launch (start us, length us, event | category | flops | bytes accessed | tf_op | source)
XLA Modules:
  0.0 132.2 jit_solution(5943942134385680657)
XLA Ops:
  0.0 0.1 stack.27.place
  0.1 0.0 copy-start
  0.1 1.0 copy-done
  1.1 0.0 copy-start.1
  1.1 0.7 copy-done.1
  1.8 0.0 copy-start.2
  1.8 0.7 copy-done.2
  2.4 0.8 pack.1
  3.3 12.7 %collective-permute-start.1 = (bf16[1632,128]{1,0:T(8,128)(2,1)S(1)}, bf16[1632,128]{1,0:T(8,128)(2,1)S(1)}, u32[]{:S(2)}, u32[]{:S(2)}) collective-permute-start(bf16[1632,128]{1,0:T(8,128)(2,1)S(1)} %get-tuple-element.20.own), channel_id=1, source_target_pairs={{0,192},{1,193},{2,194},{3,195},{4,196},{5,197},{6,198},{7,199},{8... | collective-permute-start | bytes 1253384 | tf_op jit(solution)/shard_map/ppermute | solution.py:56
  16.0 1.9 %collective-permute-start = (bf16[1632,128]{1,0:T(8,128)(2,1)S(1)}, bf16[1632,128]{1,0:T(8,128)(2,1)S(1)}, u32[]{:S(2)}, u32[]{:S(2)}) collective-permute-start(bf16[1632,128]{1,0:T(8,128)(2,1)S(1)} %get-tuple-element.20.own), channel_id=1, source_target_pairs={{0,64},{1,65},{2,66},{3,67},{4,68},{5,69},{6,70},{7,71},{8,72},{9,... | collective-permute-start | bytes 1253384 | tf_op jit(solution)/shard_map/ppermute | solution.py:56
  17.9 2.9 %collective-permute-start.2 = (bf16[1552,128]{1,0:T(8,128)(2,1)S(1)}, bf16[1552,128]{1,0:T(8,128)(2,1)S(1)}, u32[]{:S(2)}, u32[]{:S(2)}) collective-permute-start(bf16[1552,128]{1,0:T(8,128)(2,1)S(1)} %get-tuple-element.21.own), channel_id=1, source_target_pairs={{0,2},{1,3},{2,4},{3,5},{4,6},{5,7},{6,0},{7,1},{8,10},{9,11},{10,... | collective-permute-start | bytes 1191944 | tf_op jit(solution)/shard_map/ppermute | solution.py:56
  20.8 3.9 %collective-permute-start.3 = (bf16[1552,128]{1,0:T(8,128)(2,1)S(1)}, bf16[1552,128]{1,0:T(8,128)(2,1)S(1)}, u32[]{:S(2)}, u32[]{:S(2)}) collective-permute-start(bf16[1552,128]{1,0:T(8,128)(2,1)S(1)} %get-tuple-element.21.own), channel_id=1, source_target_pairs={{0,4},{1,5},{2,6},{3,7},{4,0},{5,1},{6,2},{7,3},{8,12},{9,13},{10,... | collective-permute-start | bytes 1191944 | tf_op jit(solution)/shard_map/ppermute | solution.py:56
  24.7 1.9 %collective-permute-start.4 = (bf16[1552,128]{1,0:T(8,128)(2,1)S(1)}, bf16[1552,128]{1,0:T(8,128)(2,1)S(1)}, u32[]{:S(2)}, u32[]{:S(2)}) collective-permute-start(bf16[1552,128]{1,0:T(8,128)(2,1)S(1)} %get-tuple-element.21.own), channel_id=1, source_target_pairs={{0,6},{1,7},{2,0},{3,1},{4,2},{5,3},{6,4},{7,5},{8,14},{9,15},{10,... | collective-permute-start | bytes 1191944 | tf_op jit(solution)/shard_map/ppermute | solution.py:56
  26.6 5.4 %collective-permute-done.2.g1 = bf16[1552,128]{1,0:T(8,128)(2,1)S(1)} collective-permute-done((bf16[1552,128]{1,0:T(8,128)(2,1)S(1)}, bf16[1552,128]{1,0:T(8,128)(2,1)S(1)}, u32[]{:S(2)}, u32[]{:S(2)}) %collective-permute-start.2) | collective-permute-done | bytes 397344 | tf_op jit(solution)/shard_map/ppermute | solution.py:56
  31.9 4.4 %collective-permute-done.3.g2 = bf16[1552,128]{1,0:T(8,128)(2,1)S(1)} collective-permute-done((bf16[1552,128]{1,0:T(8,128)(2,1)S(1)}, bf16[1552,128]{1,0:T(8,128)(2,1)S(1)}, u32[]{:S(2)}, u32[]{:S(2)}) %collective-permute-start.3) | collective-permute-done | bytes 397344 | tf_op jit(solution)/shard_map/ppermute | solution.py:56
  36.4 6.2 %collective-permute-done.4.g3 = bf16[1552,128]{1,0:T(8,128)(2,1)S(1)} collective-permute-done((bf16[1552,128]{1,0:T(8,128)(2,1)S(1)}, bf16[1552,128]{1,0:T(8,128)(2,1)S(1)}, u32[]{:S(2)}, u32[]{:S(2)}) %collective-permute-start.4) | collective-permute-done | bytes 397344 | tf_op jit(solution)/shard_map/ppermute | solution.py:56
  42.6 0.7 sort_panels.1
  43.3 4.9 %collective-permute-start.10 = (bf16[3120,128]{1,0:T(8,128)(2,1)S(1)}, bf16[3120,128]{1,0:T(8,128)(2,1)S(1)}, u32[]{:S(2)}, u32[]{:S(2)}) collective-permute-start(bf16[3120,128]{1,0:T(8,128)(2,1)S(1)} %get-tuple-element.23), channel_id=1, source_target_pairs={{0,257},{1,256},{2,259},{3,258},{4,261},{5,260},{6,263},{7,262},{8... | collective-permute-start | bytes 2396168 | tf_op jit(solution)/shard_map/ppermute | solution.py:56
  48.3 1.9 %collective-permute-start.9 = (bf16[3120,128]{1,0:T(8,128)(2,1)S(1)}, bf16[3120,128]{1,0:T(8,128)(2,1)S(1)}, u32[]{:S(2)}, u32[]{:S(2)}) collective-permute-start(bf16[3120,128]{1,0:T(8,128)(2,1)S(1)} %get-tuple-element.23), channel_id=1, source_target_pairs={{0,256},{1,257},{2,258},{3,259},{4,260},{5,261},{6,262},{7,263},{8... | collective-permute-start | bytes 2396168 | tf_op jit(solution)/shard_map/ppermute | solution.py:56
  50.2 1.6 %collective-permute-done.1.down = bf16[1632,128]{1,0:T(8,128)(2,1)S(1)} collective-permute-done((bf16[1632,128]{1,0:T(8,128)(2,1)S(1)}, bf16[1632,128]{1,0:T(8,128)(2,1)S(1)}, u32[]{:S(2)}, u32[]{:S(2)}) %collective-permute-start.1) | collective-permute-done | bytes 417824 | tf_op jit(solution)/shard_map/ppermute | solution.py:56
  51.8 8.3 %collective-permute-start.6 = (bf16[816,128]{1,0:T(8,128)(2,1)S(1)}, bf16[816,128]{1,0:T(8,128)(2,1)S(1)}, u32[]{:S(2)}, u32[]{:S(2)}) collective-permute-start(bf16[816,128]{1,0:T(8,128)(2,1)S(1)} %slice.9), channel_id=1, source_target_pairs={{0,192},{1,193},{2,194},{3,195},{4,196},{5,197},{6,198},{7,199},{8... | collective-permute-start | bytes 626696 | tf_op jit(solution)/shard_map/ppermute | solution.py:56
  60.1 0.0 collective-permute-done.up
  60.1 1.9 %collective-permute-start.5 = (bf16[816,128]{1,0:T(8,128)(2,1)S(1)}, bf16[816,128]{1,0:T(8,128)(2,1)S(1)}, u32[]{:S(2)}, u32[]{:S(2)}) collective-permute-start(bf16[816,128]{1,0:T(8,128)(2,1)S(1)} %slice.8), channel_id=1, source_target_pairs={{0,64},{1,65},{2,66},{3,67},{4,68},{5,69},{6,70},{7,71},{8,72},{9,... | collective-permute-start | bytes 626696 | tf_op jit(solution)/shard_map/ppermute | solution.py:56
  62.1 5.1 %collective-permute-start.11 = (bf16[3104,128]{1,0:T(8,128)(2,1)S(1)}, bf16[3104,128]{1,0:T(8,128)(2,1)S(1)}, u32[]{:S(2)}, u32[]{:S(2)}) collective-permute-start(bf16[3104,128]{1,0:T(8,128)(2,1)S(1)} %get-tuple-element.28.same), channel_id=1, source_target_pairs={{0,1},{1,0},{2,3},{3,2},{4,5},{5,4},{6,7},{7,6},{8,9},{9,8},{10,11... | collective-permute-start | bytes 2383880 | tf_op jit(solution)/shard_map/ppermute | solution.py:56
  67.2 9.3 %collective-permute-done.6.far1 = bf16[816,128]{1,0:T(8,128)(2,1)S(1)} collective-permute-done((bf16[816,128]{1,0:T(8,128)(2,1)S(1)}, bf16[816,128]{1,0:T(8,128)(2,1)S(1)}, u32[]{:S(2)}, u32[]{:S(2)}) %collective-permute-start.6) | collective-permute-done | bytes 208928 | tf_op jit(solution)/shard_map/ppermute | solution.py:56
  76.5 9.1 %collective-permute-done.5.far0 = bf16[816,128]{1,0:T(8,128)(2,1)S(1)} collective-permute-done((bf16[816,128]{1,0:T(8,128)(2,1)S(1)}, bf16[816,128]{1,0:T(8,128)(2,1)S(1)}, u32[]{:S(2)}, u32[]{:S(2)}) %collective-permute-start.5) | collective-permute-done | bytes 208928 | tf_op jit(solution)/shard_map/ppermute | solution.py:56
  85.6 0.7 edges.1
  86.3 1.9 %collective-permute-start.7 = (bf16[2,4,544,128]{3,2,1,0:T(8,128)(2,1)S(1)}, bf16[2,4,544,128]{3,2,1,0:T(8,128)(2,1)S(1)}, u32[]{:S(2)}, u32[]{:S(2)}) collective-permute-start(bf16[2,4,544,128]{3,2,1,0:T(8,128)(2,1)S(1)} %get-tuple-element.26), channel_id=1, source_target_pairs={{0,8},{1,9},{2,10},{3,11},{4,12},{5,13},{6,14},{7,15},{8,0},{9,1},... | collective-permute-start | bytes 3342344 | tf_op jit(solution)/shard_map/ppermute | solution.py:56
  88.2 2.5 %collective-permute-start.8 = (bf16[2,4,544,128]{3,2,1,0:T(8,128)(2,1)S(1)}, bf16[2,4,544,128]{3,2,1,0:T(8,128)(2,1)S(1)}, u32[]{:S(2)}, u32[]{:S(2)}) collective-permute-start(bf16[2,4,544,128]{3,2,1,0:T(8,128)(2,1)S(1)} %get-tuple-element.27), channel_id=1, source_target_pairs={{0,248},{1,249},{2,250},{3,251},{4,252},{5,253},{6,254},{7,255},{8... | collective-permute-start | bytes 3342344 | tf_op jit(solution)/shard_map/ppermute | solution.py:56
  90.8 0.0 collective-permute-done.11.r2
  90.8 0.0 collective-permute-done.10.rm
  90.8 0.0 collective-permute-done.9.r1
  90.8 4.6 %left_panels.1 = (bf16[3,4,256,640]{3,2,1,0:T(8,128)(2,1)}, bf16[16,128]{1,0:T(8,128)(2,1)S(1)}) custom-call(s32[6]{0:T(128)S(1)} %stack.27.place, bf16[3104,128]{1,0:T(8,128)(2,1)S(1)} %get-tuple-element.28.same, bf16[3120,128]{1,0:T(8,128)(2,1)S(1)} %collective-permute-done.9.r1, bf16[3120,128]{1,0:T(8,128)(2,1)S(1)} %collective-permute-done.10.rm, ...), custom_call_target="tpu_custom_call" | custom-call | flops 5600000000 | bytes 8388608 | tf_op jit(solution)/shard_map/left_panels/pallas_call | solution.py:187
  95.4 4.2 %begin.3.begun = f32[3,256,384]{2,1,0:T(8,128)S(1)} custom-call(s32[6]{0:T(128)S(1)} %stack.27.place, bf16[1632,128]{1,0:T(8,128)(2,1)S(1)} %get-tuple-element.20.own, bf16[1632,128]{1,0:T(8,128)(2,1)S(1)} %collective-permute-done.up, bf16[1632,128]{1,0:T(8,128)(2,1)S(1)} %collective-permute-done.1.down, bf16[816,128]{1,0:T(8,128)(2,1)S(1)} %collective-permute-done.5.far0, ...), custom_call_target="tpu_custom_call" | custom-call | bytes 6291456 | tf_op jit(solution)/shard_map/begin/pallas_call | solution.py:267
  99.6 4.2 %begin.2.begun = f32[3,256,384]{2,1,0:T(8,128)S(1)} custom-call(s32[6]{0:T(128)S(1)} %stack.27.place, bf16[1632,128]{1,0:T(8,128)(2,1)S(1)} %get-tuple-element.20.own, bf16[1632,128]{1,0:T(8,128)(2,1)S(1)} %collective-permute-done.up, bf16[1632,128]{1,0:T(8,128)(2,1)S(1)} %collective-permute-done.1.down, bf16[816,128]{1,0:T(8,128)(2,1)S(1)} %collective-permute-done.5.far0, ...), custom_call_target="tpu_custom_call" | custom-call | bytes 6291456 | tf_op jit(solution)/shard_map/begin/pallas_call | solution.py:267
  103.7 0.0 collective-permute-done.7.from_core
  103.7 2.6 %collective-permute-done.8.from_halo = bf16[2,4,544,128]{3,2,1,0:T(8,128)(2,1)S(1)} collective-permute-done((bf16[2,4,544,128]{3,2,1,0:T(8,128)(2,1)S(1)}, bf16[2,4,544,128]{3,2,1,0:T(8,128)(2,1)S(1)}, u32[]{:S(2)}, u32[]{:S(2)}) %collective-permute-start.8) | collective-permute-done | bytes 1114144 | tf_op jit(solution)/shard_map/ppermute | solution.py:56
  106.3 4.0 %multiply.3 = (f32[3,2,128,128]{3,2,1,0:T(8,128)S(1)}, f32[3,2,128,128]{3,2,1,0:T(8,128)S(1)}) custom-call(s32[6]{0:T(128)S(1)} %stack.27.place, bf16[2,4,544,128]{3,2,1,0:T(8,128)(2,1)S(1)} %collective-permute-done.7.from_core, bf16[2,4,544,128]{3,2,1,0:T(8,128)(2,1)S(1)} %collective-permute-done.8.from_halo, f32[3,256,384]{2,1,0:T(8,128)S(1)} %begin.3.begun, ...), custom_call_target="tpu_custom_call" | custom-call | flops 3221225472 | bytes 10485760 | tf_op jit(solution)/shard_map/multiply/pallas_call | solution.py:325
  110.3 1.9 %collective-permute-start.13 = (f32[3,2,128,128]{3,2,1,0:T(8,128)S(1)}, f32[3,2,128,128]{3,2,1,0:T(8,128)S(1)}, u32[]{:S(2)}, u32[]{:S(2)}) collective-permute-start(f32[3,2,128,128]{3,2,1,0:T(8,128)S(1)} %get-tuple-element.34), channel_id=1, source_target_pairs={{0,256},{1,257},{2,258},{3,259},{4,260},{5,261},{6,262},{7,263},{8... | collective-permute-start | bytes 1179656 | tf_op jit(solution)/shard_map/ppermute | solution.py:56
  112.2 4.0 %multiply.2 = (f32[3,2,128,128]{3,2,1,0:T(8,128)S(1)}, f32[3,2,128,128]{3,2,1,0:T(8,128)S(1)}) custom-call(s32[6]{0:T(128)S(1)} %stack.27.place, bf16[2,4,544,128]{3,2,1,0:T(8,128)(2,1)S(1)} %collective-permute-done.7.from_core, bf16[2,4,544,128]{3,2,1,0:T(8,128)(2,1)S(1)} %collective-permute-done.8.from_halo, f32[3,256,384]{2,1,0:T(8,128)S(1)} %begin.2.begun, ...), custom_call_target="tpu_custom_call" | custom-call | flops 3221225472 | bytes 10485760 | tf_op jit(solution)/shard_map/multiply/pallas_call | solution.py:325
  116.3 3.9 %collective-permute-start.12 = (f32[3,2,128,128]{3,2,1,0:T(8,128)S(1)}, f32[3,2,128,128]{3,2,1,0:T(8,128)S(1)}, u32[]{:S(2)}, u32[]{:S(2)}) collective-permute-start(f32[3,2,128,128]{3,2,1,0:T(8,128)S(1)} %get-tuple-element.32), channel_id=1, source_target_pairs={{0,256},{1,257},{2,258},{3,259},{4,260},{5,261},{6,262},{7,263},{8... | collective-permute-start | bytes 1179656 | tf_op jit(solution)/shard_map/ppermute | solution.py:56
  120.2 4.0 %collective-permute-done.13.got1 = f32[3,2,128,128]{3,2,1,0:T(8,128)S(1)} collective-permute-done((f32[3,2,128,128]{3,2,1,0:T(8,128)S(1)}, f32[3,2,128,128]{3,2,1,0:T(8,128)S(1)}, u32[]{:S(2)}, u32[]{:S(2)}) %collective-permute-start.13) | collective-permute-done | bytes 393248 | tf_op jit(solution)/shard_map/ppermute | solution.py:56
  124.2 7.0 %collective-permute-done.12.got0 = f32[3,2,128,128]{3,2,1,0:T(8,128)S(1)} collective-permute-done((f32[3,2,128,128]{3,2,1,0:T(8,128)S(1)}, f32[3,2,128,128]{3,2,1,0:T(8,128)S(1)}, u32[]{:S(2)}, u32[]{:S(2)}) %collective-permute-start.12) | collective-permute-done | bytes 393248 | tf_op jit(solution)/shard_map/ppermute | solution.py:56
  131.2 1.0 finish.1
  (2 shorter events, 0.0 us)
Async XLA Ops:
  0.1 1.0 copy-start
  1.1 0.7 copy-start.1
  1.8 0.7 copy-start.2
  3.3 48.6 %collective-permute-start.1 = (bf16[1632,128]{1,0:T(8,128)(2,1)S(1)}, bf16[1632,128]{1,0:T(8,128)(2,1)S(1)}, u32[]{:S(2)}, u32[]{:S(2)}) collective-permute-start(bf16[1632,128]{1,0:T(8,128)(2,1)S(1)} %get-tuple-element.20.own), channel_id=1, source_target_pairs={{0,192},{1,193},{2,194},{3,195},{4,196},{5,197},{6,198},{7,199},{8... | collective-permute-start | bytes 1253384 | tf_op jit(solution)/shard_map/ppermute | solution.py:56
  16.0 44.1 %collective-permute-start = (bf16[1632,128]{1,0:T(8,128)(2,1)S(1)}, bf16[1632,128]{1,0:T(8,128)(2,1)S(1)}, u32[]{:S(2)}, u32[]{:S(2)}) collective-permute-start(bf16[1632,128]{1,0:T(8,128)(2,1)S(1)} %get-tuple-element.20.own), channel_id=1, source_target_pairs={{0,64},{1,65},{2,66},{3,67},{4,68},{5,69},{6,70},{7,71},{8,72},{9,... | collective-permute-start | bytes 1253384 | tf_op jit(solution)/shard_map/ppermute | solution.py:56
  17.9 14.0 %collective-permute-start.2 = (bf16[1552,128]{1,0:T(8,128)(2,1)S(1)}, bf16[1552,128]{1,0:T(8,128)(2,1)S(1)}, u32[]{:S(2)}, u32[]{:S(2)}) collective-permute-start(bf16[1552,128]{1,0:T(8,128)(2,1)S(1)} %get-tuple-element.21.own), channel_id=1, source_target_pairs={{0,2},{1,3},{2,4},{3,5},{4,6},{5,7},{6,0},{7,1},{8,10},{9,11},{10,... | collective-permute-start | bytes 1191944 | tf_op jit(solution)/shard_map/ppermute | solution.py:56
  20.8 15.6 %collective-permute-start.3 = (bf16[1552,128]{1,0:T(8,128)(2,1)S(1)}, bf16[1552,128]{1,0:T(8,128)(2,1)S(1)}, u32[]{:S(2)}, u32[]{:S(2)}) collective-permute-start(bf16[1552,128]{1,0:T(8,128)(2,1)S(1)} %get-tuple-element.21.own), channel_id=1, source_target_pairs={{0,4},{1,5},{2,6},{3,7},{4,0},{5,1},{6,2},{7,3},{8,12},{9,13},{10,... | collective-permute-start | bytes 1191944 | tf_op jit(solution)/shard_map/ppermute | solution.py:56
  24.7 18.0 %collective-permute-start.4 = (bf16[1552,128]{1,0:T(8,128)(2,1)S(1)}, bf16[1552,128]{1,0:T(8,128)(2,1)S(1)}, u32[]{:S(2)}, u32[]{:S(2)}) collective-permute-start(bf16[1552,128]{1,0:T(8,128)(2,1)S(1)} %get-tuple-element.21.own), channel_id=1, source_target_pairs={{0,6},{1,7},{2,0},{3,1},{4,2},{5,3},{6,4},{7,5},{8,14},{9,15},{10,... | collective-permute-start | bytes 1191944 | tf_op jit(solution)/shard_map/ppermute | solution.py:56
  43.3 47.4 %collective-permute-start.10 = (bf16[3120,128]{1,0:T(8,128)(2,1)S(1)}, bf16[3120,128]{1,0:T(8,128)(2,1)S(1)}, u32[]{:S(2)}, u32[]{:S(2)}) collective-permute-start(bf16[3120,128]{1,0:T(8,128)(2,1)S(1)} %get-tuple-element.23), channel_id=1, source_target_pairs={{0,257},{1,256},{2,259},{3,258},{4,261},{5,260},{6,263},{7,262},{8... | collective-permute-start | bytes 2396168 | tf_op jit(solution)/shard_map/ppermute | solution.py:56
  48.3 42.5 %collective-permute-start.9 = (bf16[3120,128]{1,0:T(8,128)(2,1)S(1)}, bf16[3120,128]{1,0:T(8,128)(2,1)S(1)}, u32[]{:S(2)}, u32[]{:S(2)}) collective-permute-start(bf16[3120,128]{1,0:T(8,128)(2,1)S(1)} %get-tuple-element.23), channel_id=1, source_target_pairs={{0,256},{1,257},{2,258},{3,259},{4,260},{5,261},{6,262},{7,263},{8... | collective-permute-start | bytes 2396168 | tf_op jit(solution)/shard_map/ppermute | solution.py:56
  51.8 24.7 %collective-permute-start.6 = (bf16[816,128]{1,0:T(8,128)(2,1)S(1)}, bf16[816,128]{1,0:T(8,128)(2,1)S(1)}, u32[]{:S(2)}, u32[]{:S(2)}) collective-permute-start(bf16[816,128]{1,0:T(8,128)(2,1)S(1)} %slice.9), channel_id=1, source_target_pairs={{0,192},{1,193},{2,194},{3,195},{4,196},{5,197},{6,198},{7,199},{8... | collective-permute-start | bytes 626696 | tf_op jit(solution)/shard_map/ppermute | solution.py:56
  60.1 25.5 %collective-permute-start.5 = (bf16[816,128]{1,0:T(8,128)(2,1)S(1)}, bf16[816,128]{1,0:T(8,128)(2,1)S(1)}, u32[]{:S(2)}, u32[]{:S(2)}) collective-permute-start(bf16[816,128]{1,0:T(8,128)(2,1)S(1)} %slice.8), channel_id=1, source_target_pairs={{0,64},{1,65},{2,66},{3,67},{4,68},{5,69},{6,70},{7,71},{8,72},{9,... | collective-permute-start | bytes 626696 | tf_op jit(solution)/shard_map/ppermute | solution.py:56
  62.1 28.7 %collective-permute-start.11 = (bf16[3104,128]{1,0:T(8,128)(2,1)S(1)}, bf16[3104,128]{1,0:T(8,128)(2,1)S(1)}, u32[]{:S(2)}, u32[]{:S(2)}) collective-permute-start(bf16[3104,128]{1,0:T(8,128)(2,1)S(1)} %get-tuple-element.28.same), channel_id=1, source_target_pairs={{0,1},{1,0},{2,3},{3,2},{4,5},{5,4},{6,7},{7,6},{8,9},{9,8},{10,11... | collective-permute-start | bytes 2383880 | tf_op jit(solution)/shard_map/ppermute | solution.py:56
  86.3 17.4 %collective-permute-start.7 = (bf16[2,4,544,128]{3,2,1,0:T(8,128)(2,1)S(1)}, bf16[2,4,544,128]{3,2,1,0:T(8,128)(2,1)S(1)}, u32[]{:S(2)}, u32[]{:S(2)}) collective-permute-start(bf16[2,4,544,128]{3,2,1,0:T(8,128)(2,1)S(1)} %get-tuple-element.26), channel_id=1, source_target_pairs={{0,8},{1,9},{2,10},{3,11},{4,12},{5,13},{6,14},{7,15},{8,0},{9,1},... | collective-permute-start | bytes 3342344 | tf_op jit(solution)/shard_map/ppermute | solution.py:56
  88.2 18.0 %collective-permute-start.8 = (bf16[2,4,544,128]{3,2,1,0:T(8,128)(2,1)S(1)}, bf16[2,4,544,128]{3,2,1,0:T(8,128)(2,1)S(1)}, u32[]{:S(2)}, u32[]{:S(2)}) collective-permute-start(bf16[2,4,544,128]{3,2,1,0:T(8,128)(2,1)S(1)} %get-tuple-element.27), channel_id=1, source_target_pairs={{0,248},{1,249},{2,250},{3,251},{4,252},{5,253},{6,254},{7,255},{8... | collective-permute-start | bytes 3342344 | tf_op jit(solution)/shard_map/ppermute | solution.py:56
  110.3 13.9 %collective-permute-start.13 = (f32[3,2,128,128]{3,2,1,0:T(8,128)S(1)}, f32[3,2,128,128]{3,2,1,0:T(8,128)S(1)}, u32[]{:S(2)}, u32[]{:S(2)}) collective-permute-start(f32[3,2,128,128]{3,2,1,0:T(8,128)S(1)} %get-tuple-element.34), channel_id=1, source_target_pairs={{0,256},{1,257},{2,258},{3,259},{4,260},{5,261},{6,262},{7,263},{8... | collective-permute-start | bytes 1179656 | tf_op jit(solution)/shard_map/ppermute | solution.py:56
  116.3 15.0 %collective-permute-start.12 = (f32[3,2,128,128]{3,2,1,0:T(8,128)S(1)}, f32[3,2,128,128]{3,2,1,0:T(8,128)S(1)}, u32[]{:S(2)}, u32[]{:S(2)}) collective-permute-start(f32[3,2,128,128]{3,2,1,0:T(8,128)S(1)} %get-tuple-element.32), channel_id=1, source_target_pairs={{0,256},{1,257},{2,258},{3,259},{4,260},{5,261},{6,262},{7,263},{8... | collective-permute-start | bytes 1179656 | tf_op jit(solution)/shard_map/ppermute | solution.py:56

commit v7 on v6

--- a/solution.py
+++ b/solution.py
@@ -80,7 +80,7 @@
     return pltpu.roll(v, T // 2, 1)
 
 
-def pack_kernel(place, cols, counts, x, a_out, b_out, k_out):
+def pack_kernel(place, x, a_out, b_out, k_out):
     row = lax.broadcasted_iota(I32, (16, T), 0)
     left = lax.broadcasted_iota(I32, (16, T), 1) < T // 2
     plain = jnp.full((16, T), 9, I32)
@@ -88,9 +88,9 @@
     for r in range(3):
         keys = []
         for t in range(4):
-            away = (cols[r, t] - (place[0] * 3 + r) + 240) % 24
+            away = (place[6 + 4 * r + t] - (place[0] * 3 + r) + 240) % 24
             away = jnp.where(away > 12, away - 24, away)
-            keys.append(jnp.where(t < counts[0, r], away, 9))
+            keys.append(jnp.where(t < place[18 + r], away, 9))
             plain = jnp.where(row == r * 4 + t, keys[t], plain)
         for m in range(2):
             first, second = keys[2 * m], keys[2 * m + 1]
@@ -117,17 +117,17 @@
             b_out[PIECE + at : PIECE + at + T, :] = jnp.where(here, turned(even), odd).astype(BF16)
 
 
-def pack(place, cols, counts, x):
+def pack(place, x):
     shapes = ((BLOCK, T), (2 * PIECE, T), (16, T))
     return pl.pallas_call(
         pack_kernel,
         out_shape=[jax.ShapeDtypeStruct(s, BF16) for s in shapes],
-        in_specs=[SMEM, SMEM, SMEM, VMEM],
+        in_specs=[SMEM, VMEM],
         out_specs=[VMEM] * 3,
         compiler_params=params(),
         cost_estimate=cost(1 << 20, 6 << 20),
         name="pack",
-    )(place, cols, counts.T, x)
+    )(place, x)
 
 
 def sort_kernel(place, own, g1, g2, g3, keys, same, other):
@@ -363,7 +363,8 @@
 def body(x_tiles, tile_cols, tile_counts):
     row, col = lax.axis_index("row"), lax.axis_index("col")
     place = jnp.stack([row, row // 32, row // 8 % 4, row % 2, col // 2, col % 2]).astype(I32)
-    block, whole, keys = pack(place, tile_cols, tile_counts, x_tiles)
+    place = jnp.concatenate([place, tile_cols.reshape(12), tile_counts.reshape(3)])
+    block, whole, keys = pack(place, x_tiles)
     up, down = send(whole, along_z(4)), send(whole, along_z(-4))
     g1, g3, g2 = send(block, along_x(1)), send(block, along_x(-1)), send(block, along_x(2))
     same, other = sort_panels(place, block, g1, g2, g3, keys)

time: 133 us -> 133 us (level)
    unnamed x6 -> x2, local copies, waits for them, and re-layouts: 2.33 us -> 1 us
where the time goes in v7:
time: 133 us; the launch traced here: 132 us
  starting transfers between devices  55.7 us (42%)
  waiting for transfers between devices  49.7 us (37%)
  Pallas kernels  24.1 us (18%)
  local copies, waits for them, and re-layouts  2.53 us (2%)
    ppermute x14, starting transfers between devices, send(): return lax.ppermute(block, ('row', 'col'), pairs)  55.7 us
    ppermute x14, waiting for transfers between devices, send(): return lax.ppermute(block, ('row', 'col'), pairs)  49.7 us
    pallas_call x2, Pallas kernels, begin(): pl.pallas_call(functools.partial(begin_kernel, h), out_shape=jax.ShapeDty...  8.33 us
    pallas_call x2, Pallas kernels, multiply(): pl.pallas_call(functools.partial(multiply_kernel, h), out_shape=[shape, s...  8.04 us
    pallas_call x1, Pallas kernels, left_panels(): pl.pallas_call(left_kernel, out_shape=[jax.ShapeDtypeStruct((3, 4, 2 * T,...  4.58 us
  transfers between devices with their start and end apart: 14, of which 9 were waited for; matrix products, arithmetic and copies ran while one was open for 0% of the time, Pallas kernels for 14%

profile of v7, /device:TPU:6, one launch (start us, length us, event | category | flops | bytes accessed | tf_op | source)
XLA Modules:
  0.0 132.2 jit_solution(1901135430723404987)
XLA Ops:
  0.0 0.8 reshape.6
  0.8 0.7 concatenate.3.place
  1.5 0.0 copy-start
  1.5 1.0 copy-done
  2.5 0.8 pack.1
  3.3 12.7 %collective-permute-start.1 = (bf16[1632,128]{1,0:T(8,128)(2,1)S(1)}, bf16[1632,128]{1,0:T(8,128)(2,1)S(1)}, u32[]{:S(2)}, u32[]{:S(2)}) collective-permute-start(bf16[1632,128]{1,0:T(8,128)(2,1)S(1)} %get-tuple-element.20.own), channel_id=1, source_target_pairs={{0,192},{1,193},{2,194},{3,195},{4,196},{5,197},{6,198},{7,199},{8... | collective-permute-start | bytes 1253384 | tf_op jit(solution)/shard_map/ppermute | solution.py:56
  16.0 1.9 %collective-permute-start = (bf16[1632,128]{1,0:T(8,128)(2,1)S(1)}, bf16[1632,128]{1,0:T(8,128)(2,1)S(1)}, u32[]{:S(2)}, u32[]{:S(2)}) collective-permute-start(bf16[1632,128]{1,0:T(8,128)(2,1)S(1)} %get-tuple-element.20.own), channel_id=1, source_target_pairs={{0,64},{1,65},{2,66},{3,67},{4,68},{5,69},{6,70},{7,71},{8,72},{9,... | collective-permute-start | bytes 1253384 | tf_op jit(solution)/shard_map/ppermute | solution.py:56
  18.0 2.9 %collective-permute-start.2 = (bf16[1552,128]{1,0:T(8,128)(2,1)S(1)}, bf16[1552,128]{1,0:T(8,128)(2,1)S(1)}, u32[]{:S(2)}, u32[]{:S(2)}) collective-permute-start(bf16[1552,128]{1,0:T(8,128)(2,1)S(1)} %get-tuple-element.21.own), channel_id=1, source_target_pairs={{0,2},{1,3},{2,4},{3,5},{4,6},{5,7},{6,0},{7,1},{8,10},{9,11},{10,... | collective-permute-start | bytes 1191944 | tf_op jit(solution)/shard_map/ppermute | solution.py:56
  20.8 3.9 %collective-permute-start.3 = (bf16[1552,128]{1,0:T(8,128)(2,1)S(1)}, bf16[1552,128]{1,0:T(8,128)(2,1)S(1)}, u32[]{:S(2)}, u32[]{:S(2)}) collective-permute-start(bf16[1552,128]{1,0:T(8,128)(2,1)S(1)} %get-tuple-element.21.own), channel_id=1, source_target_pairs={{0,4},{1,5},{2,6},{3,7},{4,0},{5,1},{6,2},{7,3},{8,12},{9,13},{10,... | collective-permute-start | bytes 1191944 | tf_op jit(solution)/shard_map/ppermute | solution.py:56
  24.7 1.9 %collective-permute-start.4 = (bf16[1552,128]{1,0:T(8,128)(2,1)S(1)}, bf16[1552,128]{1,0:T(8,128)(2,1)S(1)}, u32[]{:S(2)}, u32[]{:S(2)}) collective-permute-start(bf16[1552,128]{1,0:T(8,128)(2,1)S(1)} %get-tuple-element.21.own), channel_id=1, source_target_pairs={{0,6},{1,7},{2,0},{3,1},{4,2},{5,3},{6,4},{7,5},{8,14},{9,15},{10,... | collective-permute-start | bytes 1191944 | tf_op jit(solution)/shard_map/ppermute | solution.py:56
  26.6 5.4 %collective-permute-done.2.g1 = bf16[1552,128]{1,0:T(8,128)(2,1)S(1)} collective-permute-done((bf16[1552,128]{1,0:T(8,128)(2,1)S(1)}, bf16[1552,128]{1,0:T(8,128)(2,1)S(1)}, u32[]{:S(2)}, u32[]{:S(2)}) %collective-permute-start.2) | collective-permute-done | bytes 397344 | tf_op jit(solution)/shard_map/ppermute | solution.py:56
  32.0 4.4 %collective-permute-done.3.g2 = bf16[1552,128]{1,0:T(8,128)(2,1)S(1)} collective-permute-done((bf16[1552,128]{1,0:T(8,128)(2,1)S(1)}, bf16[1552,128]{1,0:T(8,128)(2,1)S(1)}, u32[]{:S(2)}, u32[]{:S(2)}) %collective-permute-start.3) | collective-permute-done | bytes 397344 | tf_op jit(solution)/shard_map/ppermute | solution.py:56
  36.4 6.2 %collective-permute-done.4.g3 = bf16[1552,128]{1,0:T(8,128)(2,1)S(1)} collective-permute-done((bf16[1552,128]{1,0:T(8,128)(2,1)S(1)}, bf16[1552,128]{1,0:T(8,128)(2,1)S(1)}, u32[]{:S(2)}, u32[]{:S(2)}) %collective-permute-start.4) | collective-permute-done | bytes 397344 | tf_op jit(solution)/shard_map/ppermute | solution.py:56
  42.7 0.7 sort_panels.1
  43.4 4.9 %collective-permute-start.10 = (bf16[3120,128]{1,0:T(8,128)(2,1)S(1)}, bf16[3120,128]{1,0:T(8,128)(2,1)S(1)}, u32[]{:S(2)}, u32[]{:S(2)}) collective-permute-start(bf16[3120,128]{1,0:T(8,128)(2,1)S(1)} %get-tuple-element.23), channel_id=1, source_target_pairs={{0,257},{1,256},{2,259},{3,258},{4,261},{5,260},{6,263},{7,262},{8... | collective-permute-start | bytes 2396168 | tf_op jit(solution)/shard_map/ppermute | solution.py:56
  48.3 1.9 %collective-permute-start.9 = (bf16[3120,128]{1,0:T(8,128)(2,1)S(1)}, bf16[3120,128]{1,0:T(8,128)(2,1)S(1)}, u32[]{:S(2)}, u32[]{:S(2)}) collective-permute-start(bf16[3120,128]{1,0:T(8,128)(2,1)S(1)} %get-tuple-element.23), channel_id=1, source_target_pairs={{0,256},{1,257},{2,258},{3,259},{4,260},{5,261},{6,262},{7,263},{8... | collective-permute-start | bytes 2396168 | tf_op jit(solution)/shard_map/ppermute | solution.py:56
  50.2 1.6 %collective-permute-done.1.down = bf16[1632,128]{1,0:T(8,128)(2,1)S(1)} collective-permute-done((bf16[1632,128]{1,0:T(8,128)(2,1)S(1)}, bf16[1632,128]{1,0:T(8,128)(2,1)S(1)}, u32[]{:S(2)}, u32[]{:S(2)}) %collective-permute-start.1) | collective-permute-done | bytes 417824 | tf_op jit(solution)/shard_map/ppermute | solution.py:56
  51.9 8.3 %collective-permute-start.6 = (bf16[816,128]{1,0:T(8,128)(2,1)S(1)}, bf16[816,128]{1,0:T(8,128)(2,1)S(1)}, u32[]{:S(2)}, u32[]{:S(2)}) collective-permute-start(bf16[816,128]{1,0:T(8,128)(2,1)S(1)} %slice.9), channel_id=1, source_target_pairs={{0,192},{1,193},{2,194},{3,195},{4,196},{5,197},{6,198},{7,199},{8... | collective-permute-start | bytes 626696 | tf_op jit(solution)/shard_map/ppermute | solution.py:56
  60.1 0.0 collective-permute-done.up
  60.2 1.9 %collective-permute-start.5 = (bf16[816,128]{1,0:T(8,128)(2,1)S(1)}, bf16[816,128]{1,0:T(8,128)(2,1)S(1)}, u32[]{:S(2)}, u32[]{:S(2)}) collective-permute-start(bf16[816,128]{1,0:T(8,128)(2,1)S(1)} %slice.8), channel_id=1, source_target_pairs={{0,64},{1,65},{2,66},{3,67},{4,68},{5,69},{6,70},{7,71},{8,72},{9,... | collective-permute-start | bytes 626696 | tf_op jit(solution)/shard_map/ppermute | solution.py:56
  62.1 5.1 %collective-permute-start.11 = (bf16[3104,128]{1,0:T(8,128)(2,1)S(1)}, bf16[3104,128]{1,0:T(8,128)(2,1)S(1)}, u32[]{:S(2)}, u32[]{:S(2)}) collective-permute-start(bf16[3104,128]{1,0:T(8,128)(2,1)S(1)} %get-tuple-element.28.same), channel_id=1, source_target_pairs={{0,1},{1,0},{2,3},{3,2},{4,5},{5,4},{6,7},{7,6},{8,9},{9,8},{10,11... | collective-permute-start | bytes 2383880 | tf_op jit(solution)/shard_map/ppermute | solution.py:56
  67.2 9.3 %collective-permute-done.6.far1 = bf16[816,128]{1,0:T(8,128)(2,1)S(1)} collective-permute-done((bf16[816,128]{1,0:T(8,128)(2,1)S(1)}, bf16[816,128]{1,0:T(8,128)(2,1)S(1)}, u32[]{:S(2)}, u32[]{:S(2)}) %collective-permute-start.6) | collective-permute-done | bytes 208928 | tf_op jit(solution)/shard_map/ppermute | solution.py:56
  76.5 9.1 %collective-permute-done.5.far0 = bf16[816,128]{1,0:T(8,128)(2,1)S(1)} collective-permute-done((bf16[816,128]{1,0:T(8,128)(2,1)S(1)}, bf16[816,128]{1,0:T(8,128)(2,1)S(1)}, u32[]{:S(2)}, u32[]{:S(2)}) %collective-permute-start.5) | collective-permute-done | bytes 208928 | tf_op jit(solution)/shard_map/ppermute | solution.py:56
  85.7 0.7 edges.1
  86.4 1.9 %collective-permute-start.7 = (bf16[2,4,544,128]{3,2,1,0:T(8,128)(2,1)S(1)}, bf16[2,4,544,128]{3,2,1,0:T(8,128)(2,1)S(1)}, u32[]{:S(2)}, u32[]{:S(2)}) collective-permute-start(bf16[2,4,544,128]{3,2,1,0:T(8,128)(2,1)S(1)} %get-tuple-element.26), channel_id=1, source_target_pairs={{0,8},{1,9},{2,10},{3,11},{4,12},{5,13},{6,14},{7,15},{8,0},{9,1},... | collective-permute-start | bytes 3342344 | tf_op jit(solution)/shard_map/ppermute | solution.py:56
  88.3 2.5 %collective-permute-start.8 = (bf16[2,4,544,128]{3,2,1,0:T(8,128)(2,1)S(1)}, bf16[2,4,544,128]{3,2,1,0:T(8,128)(2,1)S(1)}, u32[]{:S(2)}, u32[]{:S(2)}) collective-permute-start(bf16[2,4,544,128]{3,2,1,0:T(8,128)(2,1)S(1)} %get-tuple-element.27), channel_id=1, source_target_pairs={{0,248},{1,249},{2,250},{3,251},{4,252},{5,253},{6,254},{7,255},{8... | collective-permute-start | bytes 3342344 | tf_op jit(solution)/shard_map/ppermute | solution.py:56
  90.8 0.0 collective-permute-done.11.r2
  90.8 0.0 collective-permute-done.10.rm
  90.8 0.0 collective-permute-done.9.r1
  90.8 4.6 %left_panels.1 = (bf16[3,4,256,640]{3,2,1,0:T(8,128)(2,1)}, bf16[16,128]{1,0:T(8,128)(2,1)S(1)}) custom-call(s32[21]{0:T(128)S(1)} %concatenate.3.place, bf16[3104,128]{1,0:T(8,128)(2,1)S(1)} %get-tuple-element.28.same, bf16[3120,128]{1,0:T(8,128)(2,1)S(1)} %collective-permute-done.9.r1, bf16[3120,128]{1,0:T(8,128)(2,1)S(1)} %collective-permute-done.10.rm, ...), custom_call_target="tpu_custom_call" | custom-call | flops 5600000000 | bytes 8388608 | tf_op jit(solution)/shard_map/left_panels/pallas_call | solution.py:187
  95.4 4.2 %begin.3.begun = f32[3,256,384]{2,1,0:T(8,128)S(1)} custom-call(s32[21]{0:T(128)S(1)} %concatenate.3.place, bf16[1632,128]{1,0:T(8,128)(2,1)S(1)} %get-tuple-element.20.own, bf16[1632,128]{1,0:T(8,128)(2,1)S(1)} %collective-permute-done.up, bf16[1632,128]{1,0:T(8,128)(2,1)S(1)} %collective-permute-done.1.down, ...), custom_call_target="tpu_custom_call" | custom-call | bytes 6291456 | tf_op jit(solution)/shard_map/begin/pallas_call | solution.py:267
  99.6 4.2 %begin.2.begun = f32[3,256,384]{2,1,0:T(8,128)S(1)} custom-call(s32[21]{0:T(128)S(1)} %concatenate.3.place, bf16[1632,128]{1,0:T(8,128)(2,1)S(1)} %get-tuple-element.20.own, bf16[1632,128]{1,0:T(8,128)(2,1)S(1)} %collective-permute-done.up, bf16[1632,128]{1,0:T(8,128)(2,1)S(1)} %collective-permute-done.1.down, ...), custom_call_target="tpu_custom_call" | custom-call | bytes 6291456 | tf_op jit(solution)/shard_map/begin/pallas_call | solution.py:267
  103.8 0.0 collective-permute-done.7.from_core
  103.8 2.5 %collective-permute-done.8.from_halo = bf16[2,4,544,128]{3,2,1,0:T(8,128)(2,1)S(1)} collective-permute-done((bf16[2,4,544,128]{3,2,1,0:T(8,128)(2,1)S(1)}, bf16[2,4,544,128]{3,2,1,0:T(8,128)(2,1)S(1)}, u32[]{:S(2)}, u32[]{:S(2)}) %collective-permute-start.8) | collective-permute-done | bytes 1114144 | tf_op jit(solution)/shard_map/ppermute | solution.py:56
  106.3 4.0 %multiply.3 = (f32[3,2,128,128]{3,2,1,0:T(8,128)S(1)}, f32[3,2,128,128]{3,2,1,0:T(8,128)S(1)}) custom-call(s32[21]{0:T(128)S(1)} %concatenate.3.place, bf16[2,4,544,128]{3,2,1,0:T(8,128)(2,1)S(1)} %collective-permute-done.7.from_core, bf16[2,4,544,128]{3,2,1,0:T(8,128)(2,1)S(1)} %collective-permute-done.8.from_halo, f32[3,256,384]{2,1,0:T(8,128)S(1)} %begin.3.begun, ...), custom_call_target="tpu_custom_call" | custom-call | flops 3221225472 | bytes 10485760 | tf_op jit(solution)/shard_map/multiply/pallas_call | solution.py:325
  110.3 1.9 %collective-permute-start.13 = (f32[3,2,128,128]{3,2,1,0:T(8,128)S(1)}, f32[3,2,128,128]{3,2,1,0:T(8,128)S(1)}, u32[]{:S(2)}, u32[]{:S(2)}) collective-permute-start(f32[3,2,128,128]{3,2,1,0:T(8,128)S(1)} %get-tuple-element.34), channel_id=1, source_target_pairs={{0,256},{1,257},{2,258},{3,259},{4,260},{5,261},{6,262},{7,263},{8... | collective-permute-start | bytes 1179656 | tf_op jit(solution)/shard_map/ppermute | solution.py:56
  112.3 4.0 %multiply.2 = (f32[3,2,128,128]{3,2,1,0:T(8,128)S(1)}, f32[3,2,128,128]{3,2,1,0:T(8,128)S(1)}) custom-call(s32[21]{0:T(128)S(1)} %concatenate.3.place, bf16[2,4,544,128]{3,2,1,0:T(8,128)(2,1)S(1)} %collective-permute-done.7.from_core, bf16[2,4,544,128]{3,2,1,0:T(8,128)(2,1)S(1)} %collective-permute-done.8.from_halo, f32[3,256,384]{2,1,0:T(8,128)S(1)} %begin.2.begun, ...), custom_call_target="tpu_custom_call" | custom-call | flops 3221225472 | bytes 10485760 | tf_op jit(solution)/shard_map/multiply/pallas_call | solution.py:325
  116.3 3.9 %collective-permute-start.12 = (f32[3,2,128,128]{3,2,1,0:T(8,128)S(1)}, f32[3,2,128,128]{3,2,1,0:T(8,128)S(1)}, u32[]{:S(2)}, u32[]{:S(2)}) collective-permute-start(f32[3,2,128,128]{3,2,1,0:T(8,128)S(1)} %get-tuple-element.32), channel_id=1, source_target_pairs={{0,256},{1,257},{2,258},{3,259},{4,260},{5,261},{6,262},{7,263},{8... | collective-permute-start | bytes 1179656 | tf_op jit(solution)/shard_map/ppermute | solution.py:56
  120.2 4.0 %collective-permute-done.13.got1 = f32[3,2,128,128]{3,2,1,0:T(8,128)S(1)} collective-permute-done((f32[3,2,128,128]{3,2,1,0:T(8,128)S(1)}, f32[3,2,128,128]{3,2,1,0:T(8,128)S(1)}, u32[]{:S(2)}, u32[]{:S(2)}) %collective-permute-start.13) | collective-permute-done | bytes 393248 | tf_op jit(solution)/shard_map/ppermute | solution.py:56
  124.3 7.0 %collective-permute-done.12.got0 = f32[3,2,128,128]{3,2,1,0:T(8,128)S(1)} collective-permute-done((f32[3,2,128,128]{3,2,1,0:T(8,128)S(1)}, f32[3,2,128,128]{3,2,1,0:T(8,128)S(1)}, u32[]{:S(2)}, u32[]{:S(2)}) %collective-permute-start.12) | collective-permute-done | bytes 393248 | tf_op jit(solution)/shard_map/ppermute | solution.py:56
  131.3 1.0 finish.1
  (2 shorter events, 0.0 us)
Async XLA Ops:
  1.5 1.0 copy-start
  3.3 48.6 %collective-permute-start.1 = (bf16[1632,128]{1,0:T(8,128)(2,1)S(1)}, bf16[1632,128]{1,0:T(8,128)(2,1)S(1)}, u32[]{:S(2)}, u32[]{:S(2)}) collective-permute-start(bf16[1632,128]{1,0:T(8,128)(2,1)S(1)} %get-tuple-element.20.own), channel_id=1, source_target_pairs={{0,192},{1,193},{2,194},{3,195},{4,196},{5,197},{6,198},{7,199},{8... | collective-permute-start | bytes 1253384 | tf_op jit(solution)/shard_map/ppermute | solution.py:56
  16.0 44.1 %collective-permute-start = (bf16[1632,128]{1,0:T(8,128)(2,1)S(1)}, bf16[1632,128]{1,0:T(8,128)(2,1)S(1)}, u32[]{:S(2)}, u32[]{:S(2)}) collective-permute-start(bf16[1632,128]{1,0:T(8,128)(2,1)S(1)} %get-tuple-element.20.own), channel_id=1, source_target_pairs={{0,64},{1,65},{2,66},{3,67},{4,68},{5,69},{6,70},{7,71},{8,72},{9,... | collective-permute-start | bytes 1253384 | tf_op jit(solution)/shard_map/ppermute | solution.py:56
  18.0 14.0 %collective-permute-start.2 = (bf16[1552,128]{1,0:T(8,128)(2,1)S(1)}, bf16[1552,128]{1,0:T(8,128)(2,1)S(1)}, u32[]{:S(2)}, u32[]{:S(2)}) collective-permute-start(bf16[1552,128]{1,0:T(8,128)(2,1)S(1)} %get-tuple-element.21.own), channel_id=1, source_target_pairs={{0,2},{1,3},{2,4},{3,5},{4,6},{5,7},{6,0},{7,1},{8,10},{9,11},{10,... | collective-permute-start | bytes 1191944 | tf_op jit(solution)/shard_map/ppermute | solution.py:56
  20.8 15.6 %collective-permute-start.3 = (bf16[1552,128]{1,0:T(8,128)(2,1)S(1)}, bf16[1552,128]{1,0:T(8,128)(2,1)S(1)}, u32[]{:S(2)}, u32[]{:S(2)}) collective-permute-start(bf16[1552,128]{1,0:T(8,128)(2,1)S(1)} %get-tuple-element.21.own), channel_id=1, source_target_pairs={{0,4},{1,5},{2,6},{3,7},{4,0},{5,1},{6,2},{7,3},{8,12},{9,13},{10,... | collective-permute-start | bytes 1191944 | tf_op jit(solution)/shard_map/ppermute | solution.py:56
  24.7 18.0 %collective-permute-start.4 = (bf16[1552,128]{1,0:T(8,128)(2,1)S(1)}, bf16[1552,128]{1,0:T(8,128)(2,1)S(1)}, u32[]{:S(2)}, u32[]{:S(2)}) collective-permute-start(bf16[1552,128]{1,0:T(8,128)(2,1)S(1)} %get-tuple-element.21.own), channel_id=1, source_target_pairs={{0,6},{1,7},{2,0},{3,1},{4,2},{5,3},{6,4},{7,5},{8,14},{9,15},{10,... | collective-permute-start | bytes 1191944 | tf_op jit(solution)/shard_map/ppermute | solution.py:56
  43.4 47.4 %collective-permute-start.10 = (bf16[3120,128]{1,0:T(8,128)(2,1)S(1)}, bf16[3120,128]{1,0:T(8,128)(2,1)S(1)}, u32[]{:S(2)}, u32[]{:S(2)}) collective-permute-start(bf16[3120,128]{1,0:T(8,128)(2,1)S(1)} %get-tuple-element.23), channel_id=1, source_target_pairs={{0,257},{1,256},{2,259},{3,258},{4,261},{5,260},{6,263},{7,262},{8... | collective-permute-start | bytes 2396168 | tf_op jit(solution)/shard_map/ppermute | solution.py:56
  48.3 42.5 %collective-permute-start.9 = (bf16[3120,128]{1,0:T(8,128)(2,1)S(1)}, bf16[3120,128]{1,0:T(8,128)(2,1)S(1)}, u32[]{:S(2)}, u32[]{:S(2)}) collective-permute-start(bf16[3120,128]{1,0:T(8,128)(2,1)S(1)} %get-tuple-element.23), channel_id=1, source_target_pairs={{0,256},{1,257},{2,258},{3,259},{4,260},{5,261},{6,262},{7,263},{8... | collective-permute-start | bytes 2396168 | tf_op jit(solution)/shard_map/ppermute | solution.py:56
  51.9 24.7 %collective-permute-start.6 = (bf16[816,128]{1,0:T(8,128)(2,1)S(1)}, bf16[816,128]{1,0:T(8,128)(2,1)S(1)}, u32[]{:S(2)}, u32[]{:S(2)}) collective-permute-start(bf16[816,128]{1,0:T(8,128)(2,1)S(1)} %slice.9), channel_id=1, source_target_pairs={{0,192},{1,193},{2,194},{3,195},{4,196},{5,197},{6,198},{7,199},{8... | collective-permute-start | bytes 626696 | tf_op jit(solution)/shard_map/ppermute | solution.py:56
  60.2 25.5 %collective-permute-start.5 = (bf16[816,128]{1,0:T(8,128)(2,1)S(1)}, bf16[816,128]{1,0:T(8,128)(2,1)S(1)}, u32[]{:S(2)}, u32[]{:S(2)}) collective-permute-start(bf16[816,128]{1,0:T(8,128)(2,1)S(1)} %slice.8), channel_id=1, source_target_pairs={{0,64},{1,65},{2,66},{3,67},{4,68},{5,69},{6,70},{7,71},{8,72},{9,... | collective-permute-start | bytes 626696 | tf_op jit(solution)/shard_map/ppermute | solution.py:56
  62.1 28.7 %collective-permute-start.11 = (bf16[3104,128]{1,0:T(8,128)(2,1)S(1)}, bf16[3104,128]{1,0:T(8,128)(2,1)S(1)}, u32[]{:S(2)}, u32[]{:S(2)}) collective-permute-start(bf16[3104,128]{1,0:T(8,128)(2,1)S(1)} %get-tuple-element.28.same), channel_id=1, source_target_pairs={{0,1},{1,0},{2,3},{3,2},{4,5},{5,4},{6,7},{7,6},{8,9},{9,8},{10,11... | collective-permute-start | bytes 2383880 | tf_op jit(solution)/shard_map/ppermute | solution.py:56
  86.4 17.4 %collective-permute-start.7 = (bf16[2,4,544,128]{3,2,1,0:T(8,128)(2,1)S(1)}, bf16[2,4,544,128]{3,2,1,0:T(8,128)(2,1)S(1)}, u32[]{:S(2)}, u32[]{:S(2)}) collective-permute-start(bf16[2,4,544,128]{3,2,1,0:T(8,128)(2,1)S(1)} %get-tuple-element.26), channel_id=1, source_target_pairs={{0,8},{1,9},{2,10},{3,11},{4,12},{5,13},{6,14},{7,15},{8,0},{9,1},... | collective-permute-start | bytes 3342344 | tf_op jit(solution)/shard_map/ppermute | solution.py:56
  88.3 18.0 %collective-permute-start.8 = (bf16[2,4,544,128]{3,2,1,0:T(8,128)(2,1)S(1)}, bf16[2,4,544,128]{3,2,1,0:T(8,128)(2,1)S(1)}, u32[]{:S(2)}, u32[]{:S(2)}) collective-permute-start(bf16[2,4,544,128]{3,2,1,0:T(8,128)(2,1)S(1)} %get-tuple-element.27), channel_id=1, source_target_pairs={{0,248},{1,249},{2,250},{3,251},{4,252},{5,253},{6,254},{7,255},{8... | collective-permute-start | bytes 3342344 | tf_op jit(solution)/shard_map/ppermute | solution.py:56
  110.3 13.9 %collective-permute-start.13 = (f32[3,2,128,128]{3,2,1,0:T(8,128)S(1)}, f32[3,2,128,128]{3,2,1,0:T(8,128)S(1)}, u32[]{:S(2)}, u32[]{:S(2)}) collective-permute-start(f32[3,2,128,128]{3,2,1,0:T(8,128)S(1)} %get-tuple-element.34), channel_id=1, source_target_pairs={{0,256},{1,257},{2,258},{3,259},{4,260},{5,261},{6,262},{7,263},{8... | collective-permute-start | bytes 1179656 | tf_op jit(solution)/shard_map/ppermute | solution.py:56
  116.3 15.0 %collective-permute-start.12 = (f32[3,2,128,128]{3,2,1,0:T(8,128)S(1)}, f32[3,2,128,128]{3,2,1,0:T(8,128)S(1)}, u32[]{:S(2)}, u32[]{:S(2)}) collective-permute-start(f32[3,2,128,128]{3,2,1,0:T(8,128)S(1)} %get-tuple-element.32), channel_id=1, source_target_pairs={{0,256},{1,257},{2,258},{3,259},{4,260},{5,261},{6,262},{7,263},{8... | collective-permute-start | bytes 1179656 | tf_op jit(solution)/shard_map/ppermute | solution.py:56
